TPU v7x, 32 devices: a whole 2x2x4 slice. The times are simulated.
32 devices in a mesh: pipe: 2 (over x), tensor: 4 (over y, core), dp: 4 (over z).
Axes of the slice: x: 2, y: 2, z: 4, core: 2. Of those that a mesh axis runs over, the one named last changes fastest.
Arguments:
- tokens: bfloat16 [8, 1024, 768], P('dp', 'tensor'), may hold values from -6 to 6
- segment_ids: int32 [8, 1024], P('dp'), may hold values from 0 to 3, never falling along the last dimension, each value on 1 to 512 neighbouring positions
- pad_mask: int32 [8, 1024], P('dp'), may hold values from 0 to 1, as said below
- block_perm: int32 [2, 12, 2], P('pipe', 'tensor'), may hold values from 0 to 1, each once within a row
- qkv_weight: bfloat16 [2, 3, 768, 768], P('pipe', None, None, 'tensor'), may hold values from -0.21875 to 0.21875
- qkv_bias: bfloat16 [2, 2, 768], P('pipe', None, 'tensor'), may hold values from -2 to 2
- out_weight: bfloat16 [2, 768, 768], P('pipe', 'tensor'), may hold values from -1.75 to 1.75
- up_weight: bfloat16 [2, 768, 3072], P('pipe', None, 'tensor'), may hold values from -0.21875 to 0.21875
- up_bias: bfloat16 [2, 3072], P('pipe', 'tensor'), may hold values from -3 to 3
- down_weight: bfloat16 [2, 3072, 768], P('pipe', 'tensor'), may hold values from -0.109375 to 0.109375
- norm_gain: float32 [2, 2, 768], P('pipe'), may hold values from 0.5 to 1.5
- shift_bias: float32 [2, 4, 768], P('pipe'), may hold values from -3 to 3
- cotangent: bfloat16 [8, 1024, 768], P('dp', 'tensor'), may hold values from -6 to 6
Outputs:
- layer_out: bfloat16 [2, 8, 1024, 768], P('pipe', 'dp', 'tensor')
- input_grad: bfloat16 [2, 8, 1024, 768], P('pipe', 'dp', 'tensor')
- grad_qkv_weight: float32 [2, 3, 768, 768], P('pipe', None, None, 'tensor')
- grad_qkv_bias: float32 [2, 2, 768], P('pipe', None, 'tensor')
- grad_out_weight: float32 [2, 768, 768], P('pipe', 'tensor')
- grad_up_weight: float32 [2, 768, 3072], P('pipe', None, 'tensor')
- grad_up_bias: float32 [2, 3072], P('pipe', 'tensor')
- grad_down_weight: float32 [2, 3072, 768], P('pipe', 'tensor')
- grad_norm_gain: float32 [2, 2, 768], P('pipe')
- grad_shift_bias: float32 [2, 4, 768], P('pipe')
Inputs may be any that keep to these rules, and one draw needn't show every extreme that they name: In each sequence the ones of pad_mask form a prefix.
All inputs are finite; a program needn't handle non-finite values.
Results may differ from a plain program's by a relative error of at most 0.018.
Values may be sent and summed in bfloat16 or wider, within the bound.
No kernel may reach another device: no remote copies, remote signals or barrier semaphores. Data moves between devices by JAX's collectives and lax.ppermute only.
A program may use at most 192 MiB of HBM per device.

v0:
```python
import jax
import jax.numpy as jnp
from jax import lax
from jax.sharding import PartitionSpec as P

HEAD_DIM = 64


NORM_EPSILON_TERM = 1e-06
MASKED = -1e30


def shifted(value, axis, steps):
    count = lax.axis_size(axis)
    leading, last = (max(0, -steps), min(count, count - steps))
    return lax.ppermute(value, axis, [(source, source + steps) for source in range(leading, last)])


def norm_forward(resid, gain, shift):
    centred = resid - jnp.mean(resid, axis=-1, keepdims=True)
    inverse = lax.rsqrt(jnp.mean(centred * centred, axis=-1, keepdims=True) + NORM_EPSILON_TERM)
    normed = centred * inverse
    return (normed * gain + shift, normed, inverse)


def norm_backward(upstream, normed, inverse, gain):
    scaled = upstream * gain
    inner = (
        scaled
        - jnp.mean(scaled, axis=-1, keepdims=True)
        - normed * jnp.mean(scaled * normed, axis=-1, keepdims=True)
    )
    return (inverse * inner, jnp.sum(upstream * normed, axis=0), jnp.sum(upstream, axis=0))


def block_layout(block_order, seg_row, pad_row):
    blocks = block_order.shape[1]
    chosen_blocks_list = (
        block_order[:, :, None] == jnp.arange(blocks, dtype=jnp.int32)[None, None, :]
    )
    seg_blocks = seg_row.reshape(blocks, -1)
    pad_blocks = pad_row.reshape(blocks, -1)
    seg_keys = jnp.sum(jnp.where(chosen_blocks_list[..., None], seg_blocks[None, None], 0), axis=2)
    pad_keys = jnp.sum(jnp.where(chosen_blocks_list[..., None], pad_blocks[None, None], 0), axis=2)
    allowed = (seg_blocks[None, :, :, None] == seg_keys[:, :, None, :]) & (
        pad_keys[:, :, None, :] == 1
    )
    return (chosen_blocks_list, allowed)


def pick_blocks(chosen_blocks_list, tensor4):
    picked = jnp.einsum(
        "hij,jbhe->hibe",
        chosen_blocks_list.astype(jnp.bfloat16),
        tensor4,
        preferred_element_type=jnp.float32,
    )
    return picked.astype(jnp.bfloat16)


def returned_block_indices(chosen_blocks_list, grad_sel):
    spread = jnp.sum(
        jnp.where(chosen_blocks_list[:, :, :, None, None], grad_sel[:, :, None], 0.0), axis=1
    )
    return jnp.transpose(spread, (1, 2, 0, 3))


def masked_scores(query4, keys_sel, allowed, score_scale):
    raw = (
        jnp.einsum("iahe,hibe->hiab", query4, keys_sel, preferred_element_type=jnp.float32)
        * score_scale
    )
    return jnp.where(allowed, raw, MASKED)


def attend(query4, keys_sel, values_sel, allowed, score_scale):
    scores = masked_scores(query4, keys_sel, allowed, score_scale)
    ceiling = jnp.maximum(jnp.max(scores, axis=-1, keepdims=True), 0.0)
    weights = jnp.where(allowed, jnp.exp(scores - ceiling), 0.0)
    total = jnp.exp(-ceiling) + jnp.sum(weights, axis=-1, keepdims=True)
    probs = (weights / total).astype(jnp.bfloat16)
    mixed = jnp.einsum("hiab,hibe->iahe", probs, values_sel, preferred_element_type=jnp.float32)
    return (mixed, ceiling + jnp.log(total))


def attend_back(
    query4, keys_sel, values_sel, allowed, log_total, grad4, score_scale, chosen_blocks_list
):
    scores = masked_scores(query4, keys_sel, allowed, score_scale)
    probs = jnp.where(allowed, jnp.exp(scores - log_total), 0.0)
    grad_probs = jnp.einsum(
        "iahe,hibe->hiab", grad4, values_sel, preferred_element_type=jnp.float32
    )
    centre = jnp.sum(probs * grad_probs, axis=-1, keepdims=True)
    grad_scores = (probs * (grad_probs - centre)).astype(jnp.bfloat16)
    grad_selected_values = jnp.einsum(
        "hiab,iahe->hibe", probs.astype(jnp.bfloat16), grad4, preferred_element_type=jnp.float32
    )
    grad_query_rows = (
        jnp.einsum("hiab,hibe->iahe", grad_scores, keys_sel, preferred_element_type=jnp.float32)
        * score_scale
    )
    grad_selected_keys = (
        jnp.einsum("hiab,iahe->hibe", grad_scores, query4, preferred_element_type=jnp.float32)
        * score_scale
    )
    return (
        grad_query_rows,
        returned_block_indices(chosen_blocks_list, grad_selected_keys),
        returned_block_indices(chosen_blocks_list, grad_selected_values),
    )


def gelu_exact(values):
    return jax.nn.gelu(values, approximate=False)


def body(
    tokens,
    segment_ids,
    pad_mask,
    block_perm,
    qkv_weight,
    qkv_bias,
    out_weight,
    up_weight,
    up_bias,
    down_weight,
    norm_gain,
    shift_bias,
    cotangent,
):
    section_index = lax.axis_index("pipe")
    micro_count = tokens.shape[0]
    w_qkv = qkv_weight[0]
    b_qkv = qkv_bias[0].astype(jnp.float32)
    w_out = out_weight[0]
    norm_gains = norm_gain[0]
    norm_shifts = shift_bias[0]
    block_order = block_perm[0]
    local_width = w_qkv.shape[2]
    head_count = local_width // HEAD_DIM
    blocks = block_order.shape[1]
    score_scale = HEAD_DIM ** (-0.5)
    w_up_all, w_down_all, b_up_all = (up_weight, down_weight, up_bias)
    w_up = w_up_all[0]
    w_down = w_down_all[0]
    b_up = b_up_all[0].astype(jnp.float32)

    def split_heads(matrix):
        return matrix.reshape(blocks, matrix.shape[0] // blocks, head_count, HEAD_DIM)

    forward_outs = []
    stored_list = []
    received = jnp.zeros_like(tokens[0])
    for clock in range(micro_count + 1):
        own_rows = tokens[min(clock, micro_count - 1)]
        rows_in = jnp.where(section_index == 0, own_rows, received)
        batch_index = jnp.clip(clock - section_index, 0, micro_count - 1)
        seg_row = lax.dynamic_index_in_dim(segment_ids, batch_index, 0, keepdims=False)
        pad_row = lax.dynamic_index_in_dim(pad_mask, batch_index, 0, keepdims=False)
        forward_x_full = lax.all_gather(rows_in, "tensor", axis=0, tiled=True)
        forward_length = forward_x_full.shape[0]
        proj = jnp.einsum("rd,kde->kre", forward_x_full, w_qkv, preferred_element_type=jnp.float32)
        forward_query = (proj[0] + b_qkv[0]).astype(jnp.bfloat16)
        forward_keys = proj[1].astype(jnp.bfloat16)
        forward_values = (proj[2] + b_qkv[1]).astype(jnp.bfloat16)
        forward_chosen_blocks_list, forward_allowed = block_layout(block_order, seg_row, pad_row)
        forward_keys_sel = pick_blocks(forward_chosen_blocks_list, split_heads(forward_keys))
        forward_values_sel = pick_blocks(forward_chosen_blocks_list, split_heads(forward_values))
        mixed, forward_log_total = attend(
            split_heads(forward_query),
            forward_keys_sel,
            forward_values_sel,
            forward_allowed,
            score_scale,
        )
        forward_attn = mixed.reshape(forward_length, local_width).astype(jnp.bfloat16)
        projected = lax.psum_scatter(
            jnp.dot(forward_attn, w_out, preferred_element_type=jnp.float32),
            "tensor",
            scatter_dimension=0,
            tiled=True,
        )
        resid1 = rows_in.astype(jnp.float32) + projected + norm_shifts[0]
        hidden, forward_normed1, forward_inverse1 = norm_forward(
            resid1, norm_gains[0], norm_shifts[1]
        )
        hidden_low = hidden.astype(jnp.bfloat16)
        forward_ffn_in = lax.all_gather(hidden_low, "tensor", axis=0, tiled=True)
        forward_pre = jnp.dot(forward_ffn_in, w_up, preferred_element_type=jnp.float32) + b_up
        forward_act = gelu_exact(forward_pre).astype(jnp.bfloat16)
        branch = lax.psum_scatter(
            jnp.dot(forward_act, w_down, preferred_element_type=jnp.float32),
            "tensor",
            scatter_dimension=0,
            tiled=True,
        )
        resid2 = hidden + branch + norm_shifts[2]
        output, forward_normed2, forward_inverse2 = norm_forward(
            resid2, norm_gains[1], norm_shifts[3]
        )
        forward_stored = (
            forward_x_full,
            forward_query,
            forward_keys,
            forward_values,
            forward_log_total,
            forward_attn,
            forward_normed1,
            forward_inverse1,
            forward_ffn_in,
            forward_pre,
            forward_normed2,
            forward_inverse2,
        )
        output, stored = (output, forward_stored)
        low_output = output.astype(jnp.bfloat16)
        forward_outs.append(low_output)
        stored_list.append(stored)
        if clock < micro_count:
            received = shifted(low_output, "pipe", 1)
    grad_outs = []
    weight_acc = None
    small_acc = None
    grad_received = jnp.zeros(tokens.shape[1:], jnp.float32)
    for clock in range(micro_count + 1):
        batch_index = jnp.clip(clock - 1 + section_index, 0, micro_count - 1)
        seg_row = lax.dynamic_index_in_dim(segment_ids, batch_index, 0, keepdims=False)
        pad_row = lax.dynamic_index_in_dim(pad_mask, batch_index, 0, keepdims=False)
        active = jnp.where(section_index == 0, clock >= 1, clock < micro_count).astype(jnp.float32)
        cotangent_rows = cotangent[min(clock, micro_count - 1)].astype(jnp.float32)
        grad_out = jnp.where(section_index == 1, cotangent_rows, grad_received) * active
        earlier = stored_list[max(clock - 1, 0)]
        later = stored_list[min(clock + 1, micro_count)]
        stored = jax.tree.map(
            lambda first, second: jnp.where(section_index == 0, first, second), earlier, later
        )
        (
            x_full,
            query,
            keys,
            values,
            log_total,
            attn,
            normed1,
            inverse1,
            ffn_in,
            pre,
            normed2,
            inverse2,
        ) = stored
        length = x_full.shape[0]
        grad_resid2, grad_gain2, grad_shift2 = norm_backward(
            grad_out, normed2, inverse2, norm_gains[1]
        )
        grad_bias2 = jnp.sum(grad_resid2, axis=0)
        grad_branch = grad_resid2.astype(jnp.bfloat16)
        activation_value, gelu_back = jax.vjp(gelu_exact, pre)
        act = activation_value.astype(jnp.bfloat16)
        branch_rows = lax.all_gather(grad_branch, "tensor", axis=0, tiled=True)
        backward_grad_down = jnp.einsum(
            "rf,rd->fd", act, branch_rows, preferred_element_type=jnp.float32
        )
        grad_act = jnp.einsum("rd,fd->rf", branch_rows, w_down, preferred_element_type=jnp.float32)
        grad_pre = gelu_back(grad_act)[0].astype(jnp.bfloat16)
        backward_grad_up = jnp.einsum(
            "rd,rf->df", ffn_in, grad_pre, preferred_element_type=jnp.float32
        )
        backward_grad_upbias = jnp.sum(grad_pre.astype(jnp.float32), axis=0)
        grad_hidden = lax.psum_scatter(
            jnp.einsum("rf,df->rd", grad_pre, w_up, preferred_element_type=jnp.float32).astype(
                jnp.bfloat16
            ),
            "tensor",
            scatter_dimension=0,
            tiled=True,
        ).astype(jnp.float32)
        grad_resid1, grad_gain1, grad_shift1 = norm_backward(
            grad_hidden + grad_resid2, normed1, inverse1, norm_gains[0]
        )
        grad_biasout = jnp.sum(grad_resid1, axis=0)
        grad_mixed = lax.all_gather(grad_resid1.astype(jnp.bfloat16), "tensor", axis=0, tiled=True)
        backward_grad_outw = jnp.einsum(
            "re,rd->ed", attn, grad_mixed, preferred_element_type=jnp.float32
        )
        grad_attn = jnp.einsum(
            "rd,ed->re", grad_mixed, w_out, preferred_element_type=jnp.float32
        ).astype(jnp.bfloat16)
        chosen_blocks_list, allowed = block_layout(block_order, seg_row, pad_row)
        keys_sel = pick_blocks(chosen_blocks_list, split_heads(keys))
        values_sel = pick_blocks(chosen_blocks_list, split_heads(values))
        grad_query_rows, grad_keys, grad_values = attend_back(
            split_heads(query),
            keys_sel,
            values_sel,
            allowed,
            log_total,
            split_heads(grad_attn),
            score_scale,
            chosen_blocks_list,
        )
        stacked = jnp.stack(
            [
                grad_query_rows.reshape(length, local_width),
                grad_keys.reshape(length, local_width),
                grad_values.reshape(length, local_width),
            ]
        ).astype(jnp.bfloat16)
        backward_grad_qkvw = jnp.einsum(
            "rd,kre->kde", x_full, stacked, preferred_element_type=jnp.float32
        )
        stacked_sums = jnp.sum(stacked.astype(jnp.float32), axis=1)
        backward_grad_qkvb = jnp.stack([stacked_sums[0], stacked_sums[2]])
        grad_rows = lax.psum_scatter(
            jnp.einsum("kre,kde->rd", stacked, w_qkv, preferred_element_type=jnp.float32).astype(
                jnp.bfloat16
            ),
            "tensor",
            scatter_dimension=0,
            tiled=True,
        ).astype(jnp.float32)
        grad_in = (grad_rows + grad_resid1).astype(jnp.bfloat16)
        weight_terms = (
            backward_grad_qkvw,
            backward_grad_qkvb,
            backward_grad_outw,
            backward_grad_up,
            backward_grad_upbias,
            backward_grad_down,
        )
        small_terms = (
            jnp.stack([grad_gain1, grad_gain2]),
            jnp.stack([grad_biasout, grad_shift1, grad_bias2, grad_shift2]),
        )
        grad_in, weight_terms, small_terms = (grad_in, weight_terms, small_terms)
        grad_outs.append(grad_in)
        if weight_acc is None:
            weight_acc = weight_terms
            small_acc = small_terms
        else:
            weight_acc = jax.tree.map(
                lambda first, second: first + second, weight_acc, weight_terms
            )
            small_acc = jax.tree.map(lambda first, second: first + second, small_acc, small_terms)
        if clock < micro_count:
            grad_received = shifted(grad_in, "pipe", -1).astype(jnp.float32)
    grad_qkvw, grad_qkvb, grad_outw, grad_up, grad_upbias, grad_down = weight_acc
    summed = (
        lax.psum(grad_qkvw.astype(jnp.bfloat16), "dp").astype(jnp.float32),
        lax.psum(grad_qkvb.astype(jnp.bfloat16), "dp").astype(jnp.float32),
        lax.psum(grad_outw.astype(jnp.bfloat16), "dp").astype(jnp.float32),
        lax.psum(grad_up.astype(jnp.bfloat16), "dp").astype(jnp.float32),
        lax.psum(grad_upbias.astype(jnp.bfloat16), "dp").astype(jnp.float32),
        lax.psum(grad_down.astype(jnp.bfloat16), "dp").astype(jnp.float32),
    )
    gain_sum, shift_sum = lax.psum(small_acc, ("tensor", "dp"))
    layer_rows = [
        jnp.where(section_index == 0, forward_outs[index], forward_outs[index + 1])
        for index in range(micro_count)
    ]
    input_rows = [
        jnp.where(section_index == 0, grad_outs[index + 1], grad_outs[index])
        for index in range(micro_count)
    ]
    layer_out = jnp.stack(layer_rows)[None]
    input_grad = jnp.stack(input_rows)[None]
    return (
        layer_out,
        input_grad,
        summed[0][None],
        summed[1][None],
        summed[2][None],
        summed[3][None],
        summed[4][None],
        summed[5][None],
        gain_sum[None],
        shift_sum[None],
    )


def solution(mesh):
    return jax.shard_map(
        body,
        mesh=mesh,
        in_specs=(
            P("dp", "tensor", None),
            P("dp", None),
            P("dp", None),
            P("pipe", "tensor", None),
            P("pipe", None, None, "tensor"),
            P("pipe", None, "tensor"),
            P("pipe", "tensor", None),
            P("pipe", None, "tensor"),
            P("pipe", "tensor"),
            P("pipe", "tensor", None),
            P("pipe", None, None),
            P("pipe", None, None),
            P("dp", "tensor", None),
        ),
        out_specs=(
            P("pipe", "dp", "tensor", None),
            P("pipe", "dp", "tensor", None),
            P("pipe", None, None, "tensor"),
            P("pipe", None, "tensor"),
            P("pipe", "tensor", None),
            P("pipe", None, "tensor"),
            P("pipe", "tensor"),
            P("pipe", "tensor", None),
            P("pipe", None, None),
            P("pipe", None, None),
        ),
        check_vma=False,
    )
```

profile of v0, /device:TPU:0, one launch (start us, length us, event | category | flops | bytes accessed | tf_op | source)
XLA Modules:
  0.0 1172.0 jit_solution(18072374809878943531)
XLA Ops:
  15.1 17.4 %all-gather.36.cloned.1.call-done = bf16[1,1024,768]{2,1,0:T(8,128)(2,1)} async-done(((bf16[1,256,768]{2,1,0:T(8,128)(2,1)}), bf16[1,1024,768]{2,1,0:T(8,128)(2,1)}) %all-gather.36.cloned.1.call-update) | async-done | bytes 1572880 | tf_op jit(solution)/shard_map/all_gather | solution.py:162
  43.2 4.6 fusion
  51.2 3.9 fusion.134
  59.0 37.4 %reduce-scatter.13.cloned.1.call-done = f32[256,768]{1,0:T(8,128)} async-done(((f32[1024,768]{1,0:T(8,128)}), f32[256,768]{1,0:T(8,128)}) %reduce-scatter.13.cloned.1.call-update) | async-done | bytes 786448 | tf_op jit(solution)/shard_map/reduce_scatter | solution.py:179
  99.9 18.8 %all-gather.14.cloned.1.call-done = bf16[1024,768]{1,0:T(8,128)(2,1)} async-done(((bf16[256,768]{1,0:T(8,128)(2,1)}), bf16[1024,768]{1,0:T(8,128)(2,1)}) %all-gather.14.cloned.1.call-update) | async-done | bytes 1572880 | tf_op jit(solution)/shard_map/all_gather | solution.py:190
  123.4 9.4 fusion.97
  132.8 38.0 %reduce-scatter.15.cloned.1.call-done = f32[256,768]{1,0:T(8,128)} async-done(((f32[1024,768]{1,0:T(8,128)}), f32[256,768]{1,0:T(8,128)}) %reduce-scatter.15.cloned.1.call-update) | async-done | bytes 786448 | tf_op jit(solution)/shard_map/reduce_scatter | solution.py:193
  176.8 8.3 collective-permute-done
  188.3 19.5 %all-gather.16.cloned.1.call-done = bf16[1024,768]{1,0:T(8,128)(2,1)} async-done(((bf16[256,768]{1,0:T(8,128)(2,1)}), bf16[1024,768]{1,0:T(8,128)(2,1)}) %all-gather.16.cloned.1.call-update) | async-done | bytes 1572880 | tf_op jit(solution)/shard_map/all_gather | solution.py:162
  225.1 4.8 fusion.1
  232.7 3.9 fusion.137
  240.2 37.6 %reduce-scatter.17.cloned.1.call-done = f32[256,768]{1,0:T(8,128)} async-done(((f32[1024,768]{1,0:T(8,128)}), f32[256,768]{1,0:T(8,128)}) %reduce-scatter.17.cloned.1.call-update) | async-done | bytes 786448 | tf_op jit(solution)/shard_map/reduce_scatter | solution.py:179
  280.4 19.8 %all-gather.18.cloned.1.call-done = bf16[1024,768]{1,0:T(8,128)(2,1)} async-done(((bf16[256,768]{1,0:T(8,128)(2,1)}), bf16[1024,768]{1,0:T(8,128)(2,1)}) %all-gather.18.cloned.1.call-update) | async-done | bytes 1572880 | tf_op jit(solution)/shard_map/all_gather | solution.py:190
  304.8 9.4 fusion.95
  314.2 38.0 %reduce-scatter.19.cloned.1.call-done = f32[256,768]{1,0:T(8,128)} async-done(((f32[1024,768]{1,0:T(8,128)}), f32[256,768]{1,0:T(8,128)}) %reduce-scatter.19.cloned.1.call-update) | async-done | bytes 786448 | tf_op jit(solution)/shard_map/reduce_scatter | solution.py:193
  357.8 3.4 collective-permute-start.1
  361.2 8.3 collective-permute-done.1
  372.7 19.5 %all-gather.20.cloned.1.call-done = bf16[1024,768]{1,0:T(8,128)(2,1)} async-done(((bf16[256,768]{1,0:T(8,128)(2,1)}), bf16[1024,768]{1,0:T(8,128)(2,1)}) %all-gather.20.cloned.1.call-update) | async-done | bytes 1572880 | tf_op jit(solution)/shard_map/all_gather | solution.py:162
  413.7 4.8 fusion.2
  422.0 3.9 fusion.140
  429.5 38.0 %reduce-scatter.21.cloned.1.call-done = f32[256,768]{1,0:T(8,128)} async-done(((f32[1024,768]{1,0:T(8,128)}), f32[256,768]{1,0:T(8,128)}) %reduce-scatter.21.cloned.1.call-update) | async-done | bytes 786448 | tf_op jit(solution)/shard_map/reduce_scatter | solution.py:179
  476.7 15.0 %all-gather.22.cloned.1.call-done = bf16[1024,768]{1,0:T(8,128)(2,1)} async-done(((bf16[256,768]{1,0:T(8,128)(2,1)}), bf16[1024,768]{1,0:T(8,128)(2,1)}) %all-gather.22.cloned.1.call-update) | async-done | bytes 1572880 | tf_op jit(solution)/shard_map/all_gather | solution.py:190
  491.8 24.9 %fusion.14 = (f32[1024,768]{1,0:T(8,128)}, f32[1024,768]{1,0:T(8,128)}, f32[1024,768]{1,0:T(8,128)}, f32[1024,768]{1,0:T(8,128)}, f32[1024,768]{1,0:T(8,128)}, /*index=5*/f32[1024,768]{1,0:T(8,128)}, f32[1024,768]{1,0:T(8,128)}) fusion(f32[1024,768]{1,0:T(8,128)} %copy-done.197, f32[768]{0:T(1024)} %copy-done.182, pred[]{:T(512)S(6)} %eq.110, ...), kind=kOutput, calls=%fused_computation.41 | convolution fusion | flops 1358954496 | bytes 31067136 | tf_op jit(solution)/shard_map/dot_general | solution.py:191
  516.6 6.3 convert_reduce_fusion.2
  526.8 11.0 fusion.93
  538.0 17.1 %reduce-scatter.25.cloned.1.call-done = bf16[256,768]{1,0:T(8,128)(2,1)} async-done(((bf16[1024,768]{1,0:T(8,128)(2,1)}), bf16[256,768]{1,0:T(8,128)(2,1)}) %reduce-scatter.25.cloned.1.call-update) | async-done | bytes 393232 | tf_op jit(solution)/shard_map/reduce_scatter | solution.py:271
  559.4 36.1 %reduce-scatter.23.cloned.1.call-done = f32[256,768]{1,0:T(8,128)} async-done(((f32[1024,768]{1,0:T(8,128)}), f32[256,768]{1,0:T(8,128)}) %reduce-scatter.23.cloned.1.call-update) | async-done | bytes 786448 | tf_op jit(solution)/shard_map/reduce_scatter | solution.py:193
  595.5 3.9 fusion.377
  606.6 14.3 %all-gather.26.cloned.1.call-done = bf16[1024,768]{1,0:T(8,128)(2,1)} async-done(((bf16[256,768]{1,0:T(8,128)(2,1)}), bf16[1024,768]{1,0:T(8,128)(2,1)}) %all-gather.26.cloned.1.call-update) | async-done | bytes 1572880 | tf_op jit(solution)/shard_map/all_gather | solution.py:283
  655.3 3.7 bitcast_convert_fusion.2
  659.2 28.3 %reduce-scatter.27.cloned.1.call-done = bf16[256,768]{1,0:T(8,128)(2,1)} async-done(((bf16[1024,768]{1,0:T(8,128)(2,1)}), bf16[256,768]{1,0:T(8,128)(2,1)}) %reduce-scatter.27.cloned.1.call-update) | async-done | bytes 393232 | tf_op jit(solution)/shard_map/reduce_scatter | solution.py:315
  693.9 7.7 collective-permute-done.2
  705.4 18.9 %all-gather.28.cloned.1.call-done = bf16[1024,768]{1,0:T(8,128)(2,1)} async-done(((bf16[256,768]{1,0:T(8,128)(2,1)}), bf16[1024,768]{1,0:T(8,128)(2,1)}) %all-gather.28.cloned.1.call-update) | async-done | bytes 1572880 | tf_op jit(solution)/shard_map/all_gather | solution.py:261
  724.2 6.3 convert_reduce_fusion.1
  734.4 28.3 %reduce-scatter.29.cloned.1.call-done = bf16[256,768]{1,0:T(8,128)(2,1)} async-done(((bf16[1024,768]{1,0:T(8,128)(2,1)}), bf16[256,768]{1,0:T(8,128)(2,1)}) %reduce-scatter.29.cloned.1.call-update) | async-done | bytes 393232 | tf_op jit(solution)/shard_map/reduce_scatter | solution.py:271
  773.3 15.0 %all-gather.30.cloned.1.call-done = bf16[1024,768]{1,0:T(8,128)(2,1)} async-done(((bf16[256,768]{1,0:T(8,128)(2,1)}), bf16[1024,768]{1,0:T(8,128)(2,1)}) %all-gather.30.cloned.1.call-update) | async-done | bytes 1572880 | tf_op jit(solution)/shard_map/all_gather | solution.py:283
  815.6 3.8 bitcast_convert_fusion.1
  819.5 28.3 %reduce-scatter.31.cloned.1.call-done = bf16[256,768]{1,0:T(8,128)(2,1)} async-done(((bf16[1024,768]{1,0:T(8,128)(2,1)}), bf16[256,768]{1,0:T(8,128)(2,1)}) %reduce-scatter.31.cloned.1.call-update) | async-done | bytes 393232 | tf_op jit(solution)/shard_map/reduce_scatter | solution.py:315
  851.3 11.7 %collective-permute-done.3 = bf16[256,768]{1,0:T(8,128)(2,1)} collective-permute-done((bf16[256,768]{1,0:T(8,128)(2,1)}, bf16[256,768]{1,0:T(8,128)(2,1)}, u32[]{:S(2)}, u32[]{:S(2)}) %collective-permute-start.3) | collective-permute-done | bytes 393248 | tf_op jit(solution)/shard_map/ppermute | solution.py:16
  868.0 18.7 %all-gather.32.cloned.1.call-done = bf16[1024,768]{1,0:T(8,128)(2,1)} async-done(((bf16[256,768]{1,0:T(8,128)(2,1)}), bf16[1024,768]{1,0:T(8,128)(2,1)}) %all-gather.32.cloned.1.call-update) | async-done | bytes 1572880 | tf_op jit(solution)/shard_map/all_gather | solution.py:261
  886.6 6.3 convert_reduce_fusion
  904.5 20.5 %reduce-scatter.33.cloned.1.call-done = bf16[256,768]{1,0:T(8,128)(2,1)} async-done(((bf16[1024,768]{1,0:T(8,128)(2,1)}), bf16[256,768]{1,0:T(8,128)(2,1)}) %reduce-scatter.33.cloned.1.call-update) | async-done | bytes 393232 | tf_op jit(solution)/shard_map/reduce_scatter | solution.py:271
  933.0 4.1 fusion.72
  957.7 3.6 multiply_reduce_fusion
  985.3 3.8 bitcast_convert_fusion
  1017.8 65.0 %all-reduce = (f32[1,2,768]{2,1,0:T(2,128)}, f32[1,4,768]{2,1,0:T(4,128)}) all-reduce(f32[1,2,768]{2,1,0:T(2,128)} %fusion.251, f32[1,4,768]{2,1,0:T(4,128)S(1)} %fusion.249), channel_id=1, replica_groups=mesh['pipe'=2,'tensor'=4,'dp'=4] {'tensor','dp'}, use_global_device_ids=true, to_apply=%region_81.82 | all-reduce | flops 4608 | bytes 36864 | tf_op jit(solution)/shard_map/psum | solution.py:357
  1083.7 8.4 all-reduce.1
  1095.4 62.2 %all-reduce.5.cloned.1.call-done = (bf16[1,3,768,192]{2,3,1,0:T(8,128)(2,1)}, bf16[1,192,768]{2,1,0:T(8,128)(2,1)}, bf16[1,768,768]{2,1,0:T(8,128)(2,1)}, bf16[1,768,768]{2,1,0:T(8,128)(2,1)}) async-done(((bf16[1,3,768,192]{2,3,1,0:T(8,128)(2,1)}, bf16[1,192,768]{2,1,0:T(8,128)(2,1)}, bf16[1,768,768]{2,1,0:T(8,128)(2,1)}, bf16[1,768,768]{2,1,0:T(8,128)(2,1)}), (bf16[1,3,768,192]{2,3,1,0:T(8,128)(2,1)}, ...) | async-done | bytes 3538960 | tf_op jit(solution)/shard_map/psum | solution.py:350
  (719 shorter events, 333.1 us)
Async XLA Ops:
  7.2 111.6 %copy-start = (bf16[1,768,768]{2,1,0:T(8,128)(2,1)S(1)}, bf16[1,768,768]{2,1,0:T(8,128)(2,1)}, u32[]{:S(2)}) copy-start(bf16[1,768,768]{2,1,0:T(8,128)(2,1)} %param.20) | copy-start | bytes 3538948
  7.2 25.4 %all-gather.36.cloned.1.call-start = ((), (), s32[]{:S(2)}) async-start(), calls=%async_computation.35 | async-start | bytes 1966080 | tf_op jit(solution)/shard_map/all_gather | solution.py:162
  9.1 87.2 %reduce-scatter.13.cloned.1.call-start = ((), (), s32[]{:S(2)}) async-start(), calls=%async_computation.12 | async-start | bytes 3932160 | tf_op jit(solution)/shard_map/reduce_scatter | solution.py:179
  11.4 31.4 %copy-start.105 = (f32[3,64]{1,0:T(4,128)}, f32[3,64]{1,0:T(4,128)S(1)}, u32[]{:S(2)}) copy-start(f32[3,64]{1,0:T(4,128)S(1)} %add.479) | copy-start | bytes 2308
  42.9 179.7 %copy-start.9 = (f32[2,512,3,64]{1,0,3,2:T(2,128)}, f32[2,512,3,64]{1,0,3,2:T(2,128)S(1)}, u32[]{:S(2)}) copy-start(f32[2,512,3,64]{1,0,3,2:T(2,128)S(1)} %squeeze.60) | copy-start | bytes 2359300
  55.9 40.4 %copy-start.35 = (bf16[2,256,768]{2,1,0:T(8,128)(2,1)S(1)}, bf16[2,256,768]{2,1,0:T(8,128)(2,1)}, u32[]{:S(2)}) copy-start(bf16[2,256,768]{2,1,0:T(8,128)(2,1)} %param.13) | copy-start | bytes 2359300
  58.2 60.5 %all-gather.14.cloned.1.call-start = ((), (), s32[]{:S(2)}) async-start(), calls=%async_computation.13 | async-start | bytes 1966080 | tf_op jit(solution)/shard_map/all_gather | solution.py:190
  59.0 296.3 %copy-start.100 = (f32[768]{0:T(1024)}, f32[768]{0:T(1024)S(1)}, u32[]{:S(2)}) copy-start(f32[768]{0:T(1024)S(1)} %get-tuple-element.36) | copy-start | bytes 9220
  97.7 73.2 %copy-start.1 = (f32[256,768]{1,0:T(8,128)}, f32[256,768]{1,0:T(8,128)S(1)}, u32[]{:S(2)}) copy-start(f32[256,768]{1,0:T(8,128)S(1)} %get-tuple-element.125) | copy-start | bytes 2359300
  98.9 71.9 %reduce-scatter.15.cloned.1.call-start = ((), (), s32[]{:S(2)}) async-start(), calls=%async_computation.14 | async-start | bytes 3932160 | tf_op jit(solution)/shard_map/reduce_scatter | solution.py:193
  132.8 75.0 %all-gather.16.cloned.1.call-start = ((), (), s32[]{:S(2)}) async-start(), calls=%async_computation.15 | async-start | bytes 1966080 | tf_op jit(solution)/shard_map/all_gather | solution.py:162
  173.4 11.7 %collective-permute-start = (bf16[256,768]{1,0:T(8,128)(2,1)S(1)}, bf16[256,768]{1,0:T(8,128)(2,1)S(1)}, u32[]{:S(2)}, u32[]{:S(2)}) collective-permute-start(bf16[256,768]{1,0:T(8,128)(2,1)S(1)} %add_convert_fusion.15), channel_id=1, source_target_pairs={{0,16},{1,17},{2,18},{3,19},{4,20},{5,21},{6,22},{7,23},{8,24},{9,... | collective-permute-start | bytes 1179656 | tf_op jit(solution)/shard_map/ppermute | solution.py:16
  186.9 90.9 %reduce-scatter.17.cloned.1.call-start = ((), (), s32[]{:S(2)}) async-start(), calls=%async_computation.16 | async-start | bytes 3932160 | tf_op jit(solution)/shard_map/reduce_scatter | solution.py:179
  237.4 40.4 %copy-start.27 = (bf16[256,768]{1,0:T(8,128)(2,1)S(1)}, bf16[256,768]{1,0:T(8,128)(2,1)}, u32[]{:S(2)}) copy-start(bf16[256,768]{1,0:T(8,128)(2,1)} %bitcast_select_fusion.5) | copy-start | bytes 1179652
  237.4 40.4 %copy-start.102 = (f32[768]{0:T(1024)S(1)}, f32[768]{0:T(1024)}, u32[]{:S(2)}) copy-start(f32[768]{0:T(1024)} %get-tuple-element.38) | copy-start | bytes 9220
  239.7 60.5 %all-gather.18.cloned.1.call-start = ((), (), s32[]{:S(2)}) async-start(), calls=%async_computation.17 | async-start | bytes 1966080 | tf_op jit(solution)/shard_map/all_gather | solution.py:190
  280.4 71.9 %reduce-scatter.19.cloned.1.call-start = ((), (), s32[]{:S(2)}) async-start(), calls=%async_computation.18 | async-start | bytes 3932160 | tf_op jit(solution)/shard_map/reduce_scatter | solution.py:193
  314.2 78.0 %all-gather.20.cloned.1.call-start = ((), (), s32[]{:S(2)}) async-start(), calls=%async_computation.19 | async-start | bytes 1966080 | tf_op jit(solution)/shard_map/all_gather | solution.py:162
  353.7 118.3 %copy-start.5 = (f32[256,768]{1,0:T(8,128)}, f32[256,768]{1,0:T(8,128)S(1)}, u32[]{:S(2)}) copy-start(f32[256,768]{1,0:T(8,128)S(1)} %get-tuple-element.119) | copy-start | bytes 2359300
  357.8 11.7 %collective-permute-start.1 = (bf16[256,768]{1,0:T(8,128)(2,1)S(1)}, bf16[256,768]{1,0:T(8,128)(2,1)S(1)}, u32[]{:S(2)}, u32[]{:S(2)}) collective-permute-start(bf16[256,768]{1,0:T(8,128)(2,1)S(1)} %get-tuple-element.113), channel_id=1, source_target_pairs={{0,16},{1,17},{2,18},{3,19},{4,20},{5,21},{6,22},{7,23},{8,24},{9,... | collective-permute-start | bytes 1179656 | tf_op jit(solution)/shard_map/ppermute | solution.py:16
  371.3 96.1 %reduce-scatter.21.cloned.1.call-start = ((), (), s32[]{:S(2)}) async-start(), calls=%async_computation.20 | async-start | bytes 3932160 | tf_op jit(solution)/shard_map/reduce_scatter | solution.py:179
  427.1 40.3 %copy-start.103 = (f32[768]{0:T(1024)S(1)}, f32[768]{0:T(1024)}, u32[]{:S(2)}) copy-start(f32[768]{0:T(1024)} %get-tuple-element.38) | copy-start | bytes 9220
  429.4 62.3 %all-gather.22.cloned.1.call-start = ((), (), s32[]{:S(2)}) async-start(), calls=%async_computation.21 | async-start | bytes 1966080 | tf_op jit(solution)/shard_map/all_gather | solution.py:190
  472.0 44.7 %all-gather.24.cloned.1.call-start = ((), (), s32[]{:S(2)}) async-start(), calls=%async_computation.23 | async-start | bytes 1966080 | tf_op jit(solution)/shard_map/all_gather | solution.py:261
  476.5 78.6 %reduce-scatter.25.cloned.1.call-start = ((), (), s32[]{:S(2)}) async-start(), calls=%async_computation.24 | async-start | bytes 1966080 | tf_op jit(solution)/shard_map/reduce_scatter | solution.py:271
  526.8 68.7 %reduce-scatter.23.cloned.1.call-start = ((), (), s32[]{:S(2)}) async-start(), calls=%async_computation.22 | async-start | bytes 3932160 | tf_op jit(solution)/shard_map/reduce_scatter | solution.py:193
  537.9 57.6 %copy-start.104 = (f32[768]{0:T(1024)S(1)}, f32[768]{0:T(1024)}, u32[]{:S(2)}) copy-start(f32[768]{0:T(1024)} %get-tuple-element.39) | copy-start | bytes 9220
  537.9 83.0 %all-gather.26.cloned.1.call-start = ((), (), s32[]{:S(2)}) async-start(), calls=%async_computation.25 | async-start | bytes 1966080 | tf_op jit(solution)/shard_map/all_gather | solution.py:283
  601.1 86.3 %reduce-scatter.27.cloned.1.call-start = ((), (), s32[]{:S(2)}) async-start(), calls=%async_computation.26 | async-start | bytes 1966080 | tf_op jit(solution)/shard_map/reduce_scatter | solution.py:315
  659.1 42.5 %copy-start.113 = (f32[256]{0:T(256)S(1)}, f32[256]{0:T(256)}, u32[]{:S(2)}) copy-start(f32[256]{0:T(256)} %copy-done.112) | copy-start | bytes 3076
  659.1 65.1 %all-gather.28.cloned.1.call-start = ((), (), s32[]{:S(2)}) async-start(), calls=%async_computation.27 | async-start | bytes 1966080 | tf_op jit(solution)/shard_map/all_gather | solution.py:261
  688.8 12.7 %collective-permute-start.2 = (bf16[256,768]{1,0:T(8,128)(2,1)S(1)}, bf16[256,768]{1,0:T(8,128)(2,1)S(1)}, u32[]{:S(2)}, u32[]{:S(2)}) collective-permute-start(bf16[256,768]{1,0:T(8,128)(2,1)S(1)} %add_convert_fusion.8), channel_id=1, source_target_pairs={{16,0},{17,1},{18,2},{19,3},{20,4},{21,5},{22,6},{23,7},{24,8},{25... | collective-permute-start | bytes 1179656 | tf_op jit(solution)/shard_map/ppermute | solution.py:16
  705.3 57.3 %reduce-scatter.29.cloned.1.call-start = ((), (), s32[]{:S(2)}) async-start(), calls=%async_computation.28 | async-start | bytes 1966080 | tf_op jit(solution)/shard_map/reduce_scatter | solution.py:271
  731.7 30.9 %copy-start.4 = (f32[256,768]{1,0:T(8,128)S(1)}, f32[256,768]{1,0:T(8,128)}, u32[]{:S(2)}) copy-start(f32[256,768]{1,0:T(8,128)} %copy-done.3) | copy-start | bytes 2359300
  731.7 30.9 %copy-start.123 = (f32[256]{0:T(256)S(1)}, f32[256]{0:T(256)}, u32[]{:S(2)}) copy-start(f32[256]{0:T(256)} %copy-done.122) | copy-start | bytes 3076
  734.3 54.0 %all-gather.30.cloned.1.call-start = ((), (), s32[]{:S(2)}) async-start(), calls=%async_computation.29 | async-start | bytes 1966080 | tf_op jit(solution)/shard_map/all_gather | solution.py:283
  768.5 79.2 %reduce-scatter.31.cloned.1.call-start = ((), (), s32[]{:S(2)}) async-start(), calls=%async_computation.30 | async-start | bytes 1966080 | tf_op jit(solution)/shard_map/reduce_scatter | solution.py:315
  819.4 43.7 %copy-start.6 = (f32[256,768]{1,0:T(8,128)S(1)}, f32[256,768]{1,0:T(8,128)}, u32[]{:S(2)}) copy-start(f32[256,768]{1,0:T(8,128)} %copy-done.5) | copy-start | bytes 2359300
  819.4 43.7 %copy-start.127 = (f32[256]{0:T(256)S(1)}, f32[256]{0:T(256)}, u32[]{:S(2)}) copy-start(f32[256]{0:T(256)} %copy-done.126) | copy-start | bytes 3076
  819.4 67.2 %all-gather.32.cloned.1.call-start = ((), (), s32[]{:S(2)}) async-start(), calls=%async_computation.31 | async-start | bytes 1966080 | tf_op jit(solution)/shard_map/all_gather | solution.py:261
  850.0 13.1 %collective-permute-start.3 = (bf16[256,768]{1,0:T(8,128)(2,1)}, bf16[256,768]{1,0:T(8,128)(2,1)}, u32[]{:S(2)}, u32[]{:S(2)}) collective-permute-start(bf16[256,768]{1,0:T(8,128)(2,1)} %get-tuple-element.89), channel_id=1, source_target_pairs={{16,0},{17,1},{18,2},{19,3},{20,4},{21,5},{22,6},{23,7},{24,8},{25... | collective-permute-start | bytes 1179656 | tf_op jit(solution)/shard_map/ppermute | solution.py:16
  867.7 57.3 %reduce-scatter.33.cloned.1.call-start = ((), (), s32[]{:S(2)}) async-start(), calls=%async_computation.32 | async-start | bytes 1966080 | tf_op jit(solution)/shard_map/reduce_scatter | solution.py:271
  896.7 53.8 %all-gather.34.cloned.1.call-start = ((), (), s32[]{:S(2)}) async-start(), calls=%async_computation.33 | async-start | bytes 1966080 | tf_op jit(solution)/shard_map/all_gather | solution.py:283
  930.6 162.6 %reduce-scatter.35.cloned.1.call-start = ((), (), s32[]{:S(2)}) async-start(), calls=%async_computation.34 | async-start | bytes 1966080 | tf_op jit(solution)/shard_map/reduce_scatter | solution.py:315
  989.2 168.3 %all-reduce.5.cloned.1.call-start = ((), (), s32[]{:S(2)}) async-start(), calls=%async_computation.36 | async-start | bytes 7077888 | tf_op jit(solution)/shard_map/psum | solution.py:350
  1009.4 73.4 %copy-start.16 = (bf16[3,1024,192]{1,2,0:T(8,128)(2,1)S(1)}, bf16[3,1024,192]{1,2,0:T(8,128)(2,1)}, u32[]{:S(2)}) copy-start(bf16[3,1024,192]{1,2,0:T(8,128)(2,1)} %copy-done.14) | copy-start | bytes 3538948
  1014.2 79.1 %copy-start.19 = (f32[256,768]{1,0:T(8,128)S(1)}, f32[256,768]{1,0:T(8,128)}, u32[]{:S(2)}) copy-start(f32[256,768]{1,0:T(8,128)} %copy-done.18) | copy-start | bytes 2359300
  1015.2 79.2 %copy-start.54 = (bf16[1,256,768]{2,1,0:T(8,128)(2,1)S(1)}, bf16[1,256,768]{2,1,0:T(8,128)(2,1)}, u32[]{:S(2)}) copy-start(bf16[1,256,768]{2,1,0:T(8,128)(2,1)} %get-tuple-element.88) | copy-start | bytes 1179652
  (183 other events, 1054.3 us)
Sparse Core Ops, SparseCore 0:
  10.2 22.3 all-gather.35
  58.3 37.9 reduce-scatter.12
  99.1 19.6 all-gather.13
  132.9 37.9 reduce-scatter.14
  187.0 20.6 all-gather.15
  239.8 37.9 reduce-scatter.16
  280.5 19.6 all-gather.17
  314.3 37.9 reduce-scatter.18
  371.5 20.6 all-gather.19
  429.6 37.8 reduce-scatter.20
  472.1 19.6 all-gather.21
  493.8 19.6 all-gather.23
  526.9 28.1 reduce-scatter.24
  557.5 37.9 reduce-scatter.22
  601.2 19.6 all-gather.25
  659.2 28.1 reduce-scatter.26
  705.4 18.7 all-gather.27
  734.4 28.1 reduce-scatter.28
  768.6 19.6 all-gather.29
  819.5 28.1 reduce-scatter.30
  867.8 18.7 all-gather.31
  896.8 28.1 reduce-scatter.32
  930.8 19.6 all-gather.33
  989.3 28.1 reduce-scatter.34
  1020.7 136.7 all-reduce.4
where the time goes:
time: 1180 us; the launch traced here: 1170 us
  waiting for transfers between devices  625 us (53%)
  matrix products  230 us (19%)
  other arithmetic  112 us (9%)
  local copies, waits for them, and re-layouts  102 us (9%)
  blocking collectives  73.4 us (6%)
  between operations  16.7 us (1%)
  starting transfers between devices  12.5 us (1%)
    reduce_scatter x3, waiting for transfers between devices, body(): lax.psum_scatter(jnp.dot(forward_attn, w_out, preferred_element_type=jnp....  113 us
    reduce_scatter x3, waiting for transfers between devices, body(): lax.psum_scatter(jnp.dot(forward_act, w_down, preferred_element_type=jnp....  112 us
    reduce_scatter x3, waiting for transfers between devices, body(): lax.psum_scatter(jnp.einsum('rf,df->rd', grad_pre, w_up, preferred_elemen...  65.9 us
    psum x1, blocking collectives, body(): gain_sum, shift_sum = lax.psum(small_acc, ('tensor', 'dp'))  65 us
    psum x1, waiting for transfers between devices, body(): lax.psum(grad_qkvw.astype(jnp.bfloat16), 'dp').astype(jnp.float32)  62.2 us
    reduce_scatter x3, waiting for transfers between devices, body(): lax.psum_scatter(jnp.einsum('kre,kde->rd', stacked, w_qkv, preferred_elem...  56.6 us
    all_gather x3, waiting for transfers between devices, body(): forward_x_full = lax.all_gather(rows_in, 'tensor', axis=0, tiled=True)  56.4 us
    all_gather x3, waiting for transfers between devices, body(): forward_ffn_in = lax.all_gather(hidden_low, 'tensor', axis=0, tiled=True)  53.6 us
  transfers between devices with their start and end apart: 29, of which 27 were waited for; matrix products, arithmetic and copies ran while one was open for 10% of the time, Pallas kernels for 0%

commit v1 on v0

v1 whole, which is shorter than its diff:
```python
import jax
import jax.numpy as jnp
from jax import lax
from jax.sharding import PartitionSpec as P

HEAD_DIM = 64
NORM_EPSILON_TERM = 1e-06
MASKED = -1e30
BF16 = jnp.bfloat16
F32 = jnp.float32


def swap(value, axis, bit):
    count = lax.axis_size(axis)
    return lax.ppermute(value, axis, [(source, source ^ bit) for source in range(count)])


def core_swap(value):
    return swap(value, "tensor", 1)


def chip_swap(value):
    return swap(value, "tensor", 2)


def gather_rows(rows):
    rows = lax.optimization_barrier(rows)
    far = chip_swap(rows)
    near = core_swap(rows)
    far_near = core_swap(far)
    return jnp.concatenate([rows, near, far, far_near], axis=0)


def scatter_rows(partial):
    quarter = partial.shape[0] // 4
    blocks = [partial[r * quarter : (r + 1) * quarter] for r in range(4)]
    near_far = core_swap(blocks[3].astype(BF16))
    near = core_swap(blocks[1].astype(BF16))
    far_sum = blocks[2] + near_far.astype(F32)
    far = chip_swap(far_sum.astype(BF16))
    return blocks[0] + near.astype(F32) + far.astype(F32)


def norm_forward(resid, gain, shift):
    centred = resid - jnp.mean(resid, axis=-1, keepdims=True)
    inverse = lax.rsqrt(jnp.mean(centred * centred, axis=-1, keepdims=True) + NORM_EPSILON_TERM)
    normed = centred * inverse
    return (normed * gain + shift, normed, inverse)


def norm_backward(upstream, normed, inverse, gain):
    scaled = upstream * gain
    inner = (
        scaled
        - jnp.mean(scaled, axis=-1, keepdims=True)
        - normed * jnp.mean(scaled * normed, axis=-1, keepdims=True)
    )
    return (inverse * inner, jnp.sum(upstream * normed, axis=0), jnp.sum(upstream, axis=0))


def gelu_exact(values):
    return jax.nn.gelu(values, approximate=False)


def pick(blocks_swapped, tensor):
    return jnp.where(blocks_swapped[:, None, None, None], tensor[:, ::-1], tensor)


def split_heads(matrix):
    rows, width = matrix.shape
    heads = width // HEAD_DIM
    return matrix.reshape(2, rows // 2, heads, HEAD_DIM).transpose(2, 0, 1, 3)


def join_heads(tensor):
    heads, blocks, rows, _ = tensor.shape
    return tensor.transpose(1, 2, 0, 3).reshape(blocks * rows, heads * HEAD_DIM)


def dot(left, right):
    return jnp.dot(left, right, preferred_element_type=F32)


def dot_tn(left, right):
    return lax.dot_general(left, right, (((0,), (0,)), ((), ())), preferred_element_type=F32)


def dot_nt(left, right):
    return lax.dot_general(left, right, (((1,), (1,)), ((), ())), preferred_element_type=F32)


def scores_of(query, keys, allowed):
    raw = jnp.einsum("hiae,hibe->hiab", query, keys, preferred_element_type=F32)
    return jnp.where(allowed, raw * HEAD_DIM ** (-0.5), MASKED)


def attention_forward(query, keys, values, turned, allowed):
    q4, k4, v4 = split_heads(query), pick(turned, split_heads(keys)), pick(turned, split_heads(values))
    scores = scores_of(q4, k4, allowed)
    ceiling = jnp.maximum(jnp.max(scores, axis=-1, keepdims=True), 0.0)
    weights = jnp.where(allowed, jnp.exp(scores - ceiling), 0.0)
    total = jnp.exp(-ceiling) + jnp.sum(weights, axis=-1, keepdims=True)
    probs = (weights / total).astype(BF16)
    mixed = jnp.einsum("hiab,hibe->hiae", probs, v4, preferred_element_type=F32)
    return join_heads(mixed).astype(BF16), ceiling + jnp.log(total)


def attention_backward(query, keys, values, turned, allowed, log_total, grad):
    q4, k4, v4 = split_heads(query), pick(turned, split_heads(keys)), pick(turned, split_heads(values))
    g4 = split_heads(grad)
    scores = scores_of(q4, k4, allowed)
    probs = jnp.where(allowed, jnp.exp(scores - log_total), 0.0)
    grad_probs = jnp.einsum("hiae,hibe->hiab", g4, v4, preferred_element_type=F32)
    centre = jnp.sum(probs * grad_probs, axis=-1, keepdims=True)
    grad_scores = (probs * (grad_probs - centre)).astype(BF16)
    grad_values = jnp.einsum("hiab,hiae->hibe", probs.astype(BF16), g4, preferred_element_type=F32)
    scale = HEAD_DIM ** (-0.5)
    grad_query = scale * jnp.einsum(
        "hiab,hibe->hiae", grad_scores, k4, preferred_element_type=F32
    )
    grad_keys = scale * jnp.einsum("hiab,hiae->hibe", grad_scores, q4, preferred_element_type=F32)
    return (
        join_heads(grad_query.astype(BF16)),
        join_heads(pick(turned, grad_keys.astype(BF16))),
        join_heads(pick(turned, grad_values.astype(BF16))),
    )


def layer_forward(rows_in, weights, turned, allowed):
    w_qkv, b_qkv, w_out, w_up, b_up, w_down, gains, shifts = weights
    x_full = gather_rows(rows_in)
    query = (dot(x_full, w_qkv[0]) + b_qkv[0]).astype(BF16)
    keys = dot(x_full, w_qkv[1]).astype(BF16)
    values = (dot(x_full, w_qkv[2]) + b_qkv[1]).astype(BF16)
    attn, log_total = attention_forward(query, keys, values, turned, allowed)
    projected = scatter_rows(dot(attn, w_out))
    resid1 = rows_in.astype(F32) + projected + shifts[0]
    hidden, normed1, inverse1 = norm_forward(resid1, gains[0], shifts[1])
    ffn_in = gather_rows(hidden.astype(BF16))
    pre = dot(ffn_in, w_up) + b_up
    act = gelu_exact(pre).astype(BF16)
    branch = scatter_rows(dot(act, w_down))
    resid2 = hidden + branch + shifts[2]
    output, normed2, inverse2 = norm_forward(resid2, gains[1], shifts[3])
    kept = (x_full, query, keys, values, log_total, attn, normed1, inverse1, ffn_in, pre, act)
    return output.astype(BF16), kept + (normed2, inverse2)


def layer_backward(grad_out, kept, weights, turned, allowed):
    w_qkv, b_qkv, w_out, w_up, b_up, w_down, gains, shifts = weights
    x_full, query, keys, values, log_total, attn, normed1, inverse1, ffn_in, pre, act = kept[:11]
    normed2, inverse2 = kept[11:]
    grad_resid2, grad_gain2, grad_shift2 = norm_backward(grad_out, normed2, inverse2, gains[1])
    branch_rows = gather_rows(grad_resid2.astype(BF16))
    grad_act = dot_nt(branch_rows, w_down)
    grad_pre = jax.vjp(gelu_exact, pre)[1](grad_act)[0].astype(BF16)
    grad_hidden = scatter_rows(dot_nt(grad_pre, w_up))
    grad_down = dot_tn(act, branch_rows)
    grad_up = dot_tn(ffn_in, grad_pre)
    grad_upbias = jnp.sum(grad_pre.astype(F32), axis=0)
    grad_resid1, grad_gain1, grad_shift1 = norm_backward(
        grad_hidden + grad_resid2, normed1, inverse1, gains[0]
    )
    grad_mixed = gather_rows(grad_resid1.astype(BF16))
    grad_outw = dot_tn(attn, grad_mixed)
    grad_attn = dot_nt(grad_mixed, w_out).astype(BF16)
    grads = attention_backward(query, keys, values, turned, allowed, log_total, grad_attn)
    grad_rows = scatter_rows(
        dot_nt(grads[0], w_qkv[0]) + dot_nt(grads[1], w_qkv[1]) + dot_nt(grads[2], w_qkv[2])
    )
    grad_in = (grad_rows + grad_resid1).astype(BF16)
    grad_qkvw = jnp.stack([dot_tn(x_full, grad) for grad in grads])
    grad_qkvb = jnp.stack([jnp.sum(grads[k].astype(F32), axis=0) for k in (0, 2)])
    small = jnp.stack(
        [
            grad_gain1,
            grad_gain2,
            jnp.sum(grad_resid1, axis=0),
            grad_shift1,
            jnp.sum(grad_resid2, axis=0),
            grad_shift2,
        ]
    )
    return grad_in, (grad_qkvw, grad_outw, grad_up, grad_down), (grad_qkvb, grad_upbias), small


def sum_small(value, axes):
    for axis in axes:
        count = lax.axis_size(axis)
        if count & (count - 1):
            value = lax.psum(value, axis)
            continue
        bit = 1
        while bit < count:
            value = value + swap(value, axis, bit)
            bit *= 2
    return value


def body(
    tokens,
    segment_ids,
    pad_mask,
    block_perm,
    qkv_weight,
    qkv_bias,
    out_weight,
    up_weight,
    up_bias,
    down_weight,
    norm_gain,
    shift_bias,
    cotangent,
):
    section = lax.axis_index("pipe")
    place = lax.axis_index("tensor")
    first_section = section == 0
    own_weights = (
        qkv_weight[0],
        qkv_bias[0].astype(F32),
        out_weight[0],
        up_weight[0],
        up_bias[0].astype(F32),
        down_weight[0],
        norm_gain[0],
        shift_bias[0],
    )
    other_weights = tuple(swap(item, "pipe", 1) for item in own_weights)
    own_turned = block_perm[0][:, 0] == 1
    other_turned = swap(block_perm[0][:, 0].astype(F32), "pipe", 1) == 1

    def select(own, other):
        return (jnp.where(first_section, own, other), jnp.where(first_section, other, own))

    chosen = [select(own, other) for own, other in zip(own_weights, other_weights)]
    layers = [tuple(item[layer] for item in chosen) for layer in range(2)]
    turned = select(own_turned, other_turned)

    def relative(row):
        quarters = row.reshape(4, -1)
        return jnp.concatenate(
            [lax.dynamic_index_in_dim(quarters, place ^ r, 0, keepdims=False) for r in range(4)]
        ).reshape(2, -1)

    segments = relative(lax.dynamic_index_in_dim(segment_ids, section, 0, keepdims=False))
    real = relative(lax.dynamic_index_in_dim(pad_mask, section, 0, keepdims=False)) == 1

    def allowed_for(flags):
        key_segments = jnp.where(flags[:, None, None], segments[None, ::-1], segments[None])
        key_real = jnp.where(flags[:, None, None], real[None, ::-1], real[None])
        return (segments[None, :, :, None] == key_segments[:, :, None, :]) & key_real[:, :, None, :]

    allowed = [allowed_for(flags) for flags in turned]
    rows = lax.dynamic_index_in_dim(tokens, section, 0, keepdims=False)
    out_first, kept_first = layer_forward(rows, layers[0], turned[0], allowed[0])
    out_second, kept_second = layer_forward(out_first, layers[1], turned[1], allowed[1])

    def place_outputs(first, second):
        own = jnp.where(first_section, first, second)
        received = swap(jnp.where(first_section, second, first), "pipe", 1)
        return jnp.stack(
            [jnp.where(first_section, own, received), jnp.where(first_section, received, own)]
        )[None]

    layer_out = place_outputs(out_first, out_second)
    grad_out = lax.dynamic_index_in_dim(cotangent, section, 0, keepdims=False).astype(F32)
    grad_second, big_second, bias_second, small_second = layer_backward(
        grad_out, kept_second, layers[1], turned[1], allowed[1]
    )
    grad_first, big_first, bias_first, small_first = layer_backward(
        grad_second.astype(F32), kept_first, layers[0], turned[0], allowed[0]
    )
    input_grad = place_outputs(grad_first, grad_second)

    def over_parts(grad, source):
        low = grad.astype(BF16)
        received = lax.ppermute(low, "pipe", [(source, 1 - source)])
        return lax.psum((grad + received.astype(F32)).astype(BF16), "dp")

    second_sums = [over_parts(grad, 0) for grad in big_second]
    first_sums = [over_parts(grad, 1) for grad in big_first]
    qkvw, outw, upw, downw = [
        jnp.where(first_section, first, second).astype(F32)[None]
        for first, second in zip(first_sums, second_sums)
    ]

    def small_sums(biases, small):
        small = sum_small(small, ("tensor",))
        flat = jnp.concatenate([small.reshape(-1), biases[0].reshape(-1), biases[1].reshape(-1)])
        return sum_small(flat.reshape(-1, 128), ("pipe", "dp")).reshape(-1)

    flat = jnp.where(
        first_section, small_sums(bias_first, small_first), small_sums(bias_second, small_second)
    )
    width = tokens.shape[2]
    gains = flat[: 2 * width].reshape(1, 2, width)
    shifts = flat[2 * width : 6 * width].reshape(1, 4, width)
    local = qkv_bias.shape[2]
    qkvb = flat[6 * width : 6 * width + 2 * local].reshape(1, 2, local)
    upb = flat[6 * width + 2 * local :].reshape(1, -1)
    return (layer_out, input_grad, qkvw, qkvb, outw, upw, upb, downw, gains, shifts)


def solution(mesh):
    return jax.shard_map(
        body,
        mesh=mesh,
        in_specs=(
            P("dp", "tensor", None),
            P("dp", None),
            P("dp", None),
            P("pipe", "tensor", None),
            P("pipe", None, None, "tensor"),
            P("pipe", None, "tensor"),
            P("pipe", "tensor", None),
            P("pipe", None, "tensor"),
            P("pipe", "tensor"),
            P("pipe", "tensor", None),
            P("pipe", None, None),
            P("pipe", None, None),
            P("dp", "tensor", None),
        ),
        out_specs=(
            P("pipe", "dp", "tensor", None),
            P("pipe", "dp", "tensor", None),
            P("pipe", None, None, "tensor"),
            P("pipe", None, "tensor"),
            P("pipe", "tensor", None),
            P("pipe", None, "tensor"),
            P("pipe", "tensor"),
            P("pipe", "tensor", None),
            P("pipe", None, None),
            P("pipe", None, None),
        ),
        check_vma=False,
    )
```

time: 1180 us -> 707 us (0.60)
  waiting for transfers between devices: 625 us -> 441 us
  matrix products: 230 us -> 103 us
  blocking collectives: 73.4 us -> 0 us
  local copies, waits for them, and re-layouts: 102 us -> 32.8 us
  other arithmetic: 112 us -> 49.6 us
  starting transfers between devices: 12.5 us -> 56.8 us
    reduce_scatter x12 -> x0, waiting for transfers between devices: 348 us -> none  [the longest x3 113 us: body(): lax.psum_scatter(jnp.dot(forward_attn, w_out, preferred_element_type=jnp....]
    ppermute x4 -> x77, waiting for transfers between devices: 36.1 us -> 239 us  [the longest x69 194 us: swap(): lax.ppermute(value, axis, [(source, source ^ bit) for source in range(cou...]
    all_gather x12 -> x0, waiting for transfers between devices: 179 us -> none  [the longest x3 56.4 us: body(): forward_x_full = lax.all_gather(rows_in, 'tensor', axis=0, tiled=True)]
    psum x1, waiting for transfers between devices: 62.2 us -> 202 us  [over_parts(): return lax.psum((grad + received.astype(F32)).astype(BF16), 'dp')]
    dot_general x66 -> x48, matrix products: 222 us -> 103 us  [the longest x12 35.6 us: dot(): return jnp.dot(left, right, preferred_element_type=F32)]
    psum x2 -> x0, blocking collectives: 73.4 us -> none  [the longest x1 65 us: body(): gain_sum, shift_sum = lax.psum(small_acc, ('tensor', 'dp'))]
    ppermute x4 -> x77, starting transfers between devices: 9.78 us -> 56.8 us  [the longest x69 40.3 us: swap(): lax.ppermute(value, axis, [(source, source ^ bit) for source in range(cou...]
    reduce_sum x19 -> x10, other arithmetic: 34.6 us -> 8.4 us  [the longest x2 4.24 us: attention_forward(): total = jnp.exp(-ceiling) + jnp.sum(weights, axis=-1, keepdims=True)]
  transfers between devices with their start and end apart: 29 -> 78, of which waited for: 27 -> 41; matrix products, arithmetic and copies ran while one was open for 10% -> 17% of each run, Pallas kernels for 0% -> 0%
where the time goes in v1:
time: 707 us; the launch traced here: 700 us
  waiting for transfers between devices  441 us (62%)
  matrix products  103 us (15%)
  starting transfers between devices  56.8 us (8%)
  other arithmetic  49.6 us (7%)
  local copies, waits for them, and re-layouts  32.8 us (5%)
  between operations  16.9 us (2%)
    psum x1, waiting for transfers between devices, over_parts(): return lax.psum((grad + received.astype(F32)).astype(BF16), 'dp')  202 us
    ppermute x69, waiting for transfers between devices, swap(): lax.ppermute(value, axis, [(source, source ^ bit) for source in range(cou...  194 us
    ppermute x8, waiting for transfers between devices, over_parts(): received = lax.ppermute(low, 'pipe', [(source, 1 - source)])  45.8 us
    ppermute x69, starting transfers between devices, swap(): lax.ppermute(value, axis, [(source, source ^ bit) for source in range(cou...  40.3 us
    dot_general x12, matrix products, dot(): return jnp.dot(left, right, preferred_element_type=F32)  35.6 us
    dot_general x12, matrix products, dot_tn(): lax.dot_general(left, right, (((0,), (0,)), ((), ())), preferred_element_...  18.1 us
    dot_general x12, matrix products, dot_nt(): lax.dot_general(left, right, (((1,), (1,)), ((), ())), preferred_element_...  17.9 us
    ppermute x8, starting transfers between devices, over_parts(): received = lax.ppermute(low, 'pipe', [(source, 1 - source)])  16.5 us
  transfers between devices with their start and end apart: 78, of which 41 were waited for; matrix products, arithmetic and copies ran while one was open for 17% of the time, Pallas kernels for 0%

profile of v1, /device:TPU:0, one launch (start us, length us, event | category | flops | bytes accessed | tf_op | source)
XLA Modules:
  0.0 699.5 jit_solution(14699305576452700976)
XLA Ops:
  8.5 3.0 collective-permute-start.2
  20.8 22.2 %collective-permute-done.4 = bf16[3,768,192]{1,2,0:T(8,128)(2,1)S(1)} collective-permute-done((bf16[3,768,192]{1,2,0:T(8,128)(2,1)}, bf16[3,768,192]{1,2,0:T(8,128)(2,1)S(1)}, u32[]{:S(2)}, u32[]{:S(2)}) %collective-permute-start.4) | collective-permute-done | bytes 884768 | tf_op jit(solution)/shard_map/ppermute | solution.py:15
  57.7 3.1 fusion.40
  67.6 10.0 %collective-permute-done.9 = bf16[256,768]{0,1:T(8,128)(2,1)S(1)} collective-permute-done((bf16[256,768]{0,1:T(8,128)(2,1)S(1)}, bf16[256,768]{0,1:T(8,128)(2,1)S(1)}, u32[]{:S(2)}, u32[]{:S(2)}) %collective-permute-start.9) | collective-permute-done | bytes 393248 | tf_op jit(solution)/shard_map/ppermute | solution.py:15
  78.8 10.3 %collective-permute-done.13 = bf16[256,768]{0,1:T(8,128)(2,1)S(1)} collective-permute-done((bf16[256,768]{0,1:T(8,128)(2,1)S(1)}, bf16[256,768]{0,1:T(8,128)(2,1)S(1)}, u32[]{:S(2)}, u32[]{:S(2)}) %collective-permute-start.13) | collective-permute-done | bytes 393248 | tf_op jit(solution)/shard_map/ppermute | solution.py:15
  92.8 10.2 %multiply_convert_fusion.3 = (bf16[1024,768]{1,0:T(8,128)(2,1)S(1)}, f32[1024,768]{1,0:T(8,128)}, f32[1024,768]{1,0:T(8,128)}) fusion(f32[768]{0:T(1024)S(1)} %get-tuple-element.135, bf16[768,768]{1,0:T(8,128)(2,1)S(1)} %collective-permute-done.15, pred[]{:T(512)S(6)} %eq.51, bf16[1,768,768]{2,1,0:T(8,128)(2,1)S(1)} %copy-done.17, ...), kind=kOutput, calls=%fused_computation.43 | convolution fusion | flops 1266745344 | bytes 11799553 | tf_op jit(solution)/shard_map/dot_general | solution.py:81
  103.1 15.7 %collective-permute-done.17 = bf16[768,768]{1,0:T(8,128)(2,1)S(1)} collective-permute-done((bf16[768,768]{1,0:T(8,128)(2,1)S(1)}, bf16[768,768]{1,0:T(8,128)(2,1)S(1)}, u32[]{:S(2)}, u32[]{:S(2)}) %collective-permute-start.17) | collective-permute-done | bytes 1179680 | tf_op jit(solution)/shard_map/ppermute | solution.py:15
  122.8 10.6 %collective-permute-done.20 = bf16[256,768]{0,1:T(8,128)(2,1)S(1)} collective-permute-done((bf16[256,768]{0,1:T(8,128)(2,1)S(1)}, bf16[256,768]{0,1:T(8,128)(2,1)S(1)}, u32[]{:S(2)}, u32[]{:S(2)}) %collective-permute-start.20) | collective-permute-done | bytes 393248 | tf_op jit(solution)/shard_map/ppermute | solution.py:15
  134.9 9.8 %collective-permute-done.22 = bf16[256,768]{0,1:T(8,128)(2,1)S(1)} collective-permute-done((bf16[256,768]{0,1:T(8,128)(2,1)S(1)}, bf16[256,768]{0,1:T(8,128)(2,1)S(1)}, u32[]{:S(2)}, u32[]{:S(2)}) %collective-permute-start.22) | collective-permute-done | bytes 393248 | tf_op jit(solution)/shard_map/ppermute | solution.py:15
  151.9 2.7 convolution_convert_fusion.2
  156.3 4.7 fusion.197
  163.8 3.5 fusion.41
  171.6 10.0 %collective-permute-done.26 = bf16[256,768]{0,1:T(8,128)(2,1)S(1)} collective-permute-done((bf16[256,768]{0,1:T(8,128)(2,1)S(1)}, bf16[256,768]{0,1:T(8,128)(2,1)S(1)}, u32[]{:S(2)}, u32[]{:S(2)}) %collective-permute-start.26) | collective-permute-done | bytes 393248 | tf_op jit(solution)/shard_map/ppermute | solution.py:15
  183.1 9.8 %collective-permute-done.28 = bf16[256,768]{0,1:T(8,128)(2,1)S(1)} collective-permute-done((bf16[256,768]{0,1:T(8,128)(2,1)S(1)}, bf16[256,768]{0,1:T(8,128)(2,1)S(1)}, u32[]{:S(2)}, u32[]{:S(2)}) %collective-permute-start.28) | collective-permute-done | bytes 393248 | tf_op jit(solution)/shard_map/ppermute | solution.py:15
  194.6 10.1 %multiply_convert_fusion.2 = (bf16[1024,768]{1,0:T(8,128)(2,1)S(1)}, f32[1024,768]{1,0:T(8,128)}, f32[1024,768]{1,0:T(8,128)}) fusion(f32[768]{0:T(1024)S(1)} %get-tuple-element.134, bf16[768,768]{1,0:T(8,128)(2,1)S(1)} %copy-done.22, pred[]{:T(512)S(6)} %eq.51, bf16[1,768,768]{2,1,0:T(8,128)(2,1)S(1)} %copy-done.18, ...), kind=kOutput, calls=%fused_computation.30 | convolution fusion | flops 1266745344 | bytes 11799553 | tf_op jit(solution)/shard_map/dot_general | solution.py:81
  212.1 9.0 %collective-permute-done.32 = bf16[256,768]{0,1:T(8,128)(2,1)} collective-permute-done((bf16[256,768]{0,1:T(8,128)(2,1)}, bf16[256,768]{0,1:T(8,128)(2,1)}, u32[]{:S(2)}, u32[]{:S(2)}) %collective-permute-start.32) | collective-permute-done | bytes 393248 | tf_op jit(solution)/shard_map/ppermute | solution.py:15
  224.3 9.8 %collective-permute-done.35 = bf16[256,768]{0,1:T(8,128)(2,1)S(1)} collective-permute-done((bf16[256,768]{0,1:T(8,128)(2,1)S(1)}, bf16[256,768]{0,1:T(8,128)(2,1)S(1)}, u32[]{:S(2)}, u32[]{:S(2)}) %collective-permute-start.35) | collective-permute-done | bytes 393248 | tf_op jit(solution)/shard_map/ppermute | solution.py:15
  235.8 5.2 convert_reduce_fusion
  245.1 10.6 %collective-permute-done.39 = bf16[256,768]{0,1:T(8,128)(2,1)S(1)} collective-permute-done((bf16[256,768]{0,1:T(8,128)(2,1)S(1)}, bf16[256,768]{0,1:T(8,128)(2,1)S(1)}, u32[]{:S(2)}, u32[]{:S(2)}) %collective-permute-start.39) | collective-permute-done | bytes 393248 | tf_op jit(solution)/shard_map/ppermute | solution.py:15
  257.9 9.8 %collective-permute-done.41 = bf16[256,768]{0,1:T(8,128)(2,1)S(1)} collective-permute-done((bf16[256,768]{0,1:T(8,128)(2,1)S(1)}, bf16[256,768]{0,1:T(8,128)(2,1)S(1)}, u32[]{:S(2)}, u32[]{:S(2)}) %collective-permute-start.41) | collective-permute-done | bytes 393248 | tf_op jit(solution)/shard_map/ppermute | solution.py:15
  267.7 3.2 fusion.209
  270.9 3.5 collective-permute-start.76
  279.4 4.2 fusion.20
  283.7 2.6 multiply_reduce_fusion.1
  286.3 2.4 multiply_convert_fusion.1
  299.9 2.7 add_convert_fusion.2
  302.7 5.1 collective-permute-done.45
  309.0 16.4 %collective-permute-done.74 = bf16[768,768]{1,0:T(8,128)(2,1)S(1)} collective-permute-done((bf16[768,768]{1,0:T(8,128)(2,1)S(1)}, bf16[768,768]{1,0:T(8,128)(2,1)S(1)}, u32[]{:S(2)}, u32[]{:S(2)}) %collective-permute-start.74) | collective-permute-done | bytes 1179680 | tf_op jit(solution)/shard_map/ppermute | solution.py:277
  327.5 4.4 collective-permute-start.72
  336.2 3.5 convert_reduce_fusion.1
  348.8 6.8 collective-permute-done.51
  360.6 2.9 collective-permute-done.60
  364.6 3.9 collective-permute-done.53
  368.6 3.2 fusion.206
  373.2 3.9 collective-permute-done.75
  383.3 4.6 fusion.23
  388.0 2.6 multiply_reduce_fusion
  390.6 2.4 multiply_convert_fusion
  406.4 2.6 add_convert_fusion.5
  409.0 22.5 %collective-permute-done.71 = bf16[192,768]{1,0:T(8,128)(2,1)S(1)} collective-permute-done((bf16[192,768]{1,0:T(8,128)(2,1)S(1)}, bf16[192,768]{1,0:T(8,128)(2,1)S(1)}, u32[]{:S(2)}, u32[]{:S(2)}) %collective-permute-start.71) | collective-permute-done | bytes 294944 | tf_op jit(solution)/shard_map/ppermute | solution.py:277
  436.2 8.9 %collective-permute-done.33 = bf16[256,768]{0,1:T(8,128)(2,1)} collective-permute-done((bf16[256,768]{0,1:T(8,128)(2,1)}, bf16[256,768]{0,1:T(8,128)(2,1)}, u32[]{:S(2)}, u32[]{:S(2)}) %collective-permute-start.33) | collective-permute-done | bytes 393248 | tf_op jit(solution)/shard_map/ppermute | solution.py:15
  452.8 3.1 collective-permute-done.62
  463.2 2.6 collective-permute-start.70
  465.8 3.7 collective-permute-start.65
  469.5 2.7 collective-permute-done.57
  476.9 6.0 collective-permute-done.58
  484.3 201.5 %all-reduce.3.cloned.1.call-done = (bf16[3,768,192]{1,2,0:T(8,128)(2,1)}, bf16[3,768,192]{1,2,0:T(8,128)(2,1)}, bf16[192,768]{1,0:T(8,128)(2,1)}, bf16[192,768]{...) async-done(((bf16[3,768,192]{1,2,0:T(8,128)(2,1)}, ...) | async-done | bytes 7077904 | tf_op jit(solution)/shard_map/psum | solution.py:278
  685.8 2.6 bitcast_convert_fusion.2
  (627 shorter events, 167.4 us)
Async XLA Ops:
  7.2 678.6 %all-reduce.3.cloned.1.call-start = ((), (), s32[]{:S(2)}) async-start(), calls=%async_computation | async-start | bytes 14155776 | tf_op jit(solution)/shard_map/psum | solution.py:278
  8.5 12.3 %collective-permute-start.2 = (bf16[256,768]{0,1:T(8,128)(2,1)S(1)}, bf16[256,768]{0,1:T(8,128)(2,1)}, u32[]{:S(2)}, u32[]{:S(2)}) collective-permute-start(bf16[256,768]{0,1:T(8,128)(2,1)S(1)} %bitcast.379), channel_id=1, source_target_pairs={{0,8},{4,12},{8,0},{12,4},{1,9},{5,13},{9,1},{13,5},{2,10},{6,14},... | collective-permute-start | bytes 1179656 | tf_op jit(solution)/shard_map/ppermute | solution.py:15
  11.6 33.7 %collective-permute-start.1 = (bf16[256,768]{0,1:T(8,128)(2,1)S(1)}, bf16[256,768]{0,1:T(8,128)(2,1)}, u32[]{:S(2)}, u32[]{:S(2)}) collective-permute-start(bf16[256,768]{0,1:T(8,128)(2,1)S(1)} %bitcast.380), channel_id=1, source_target_pairs={{0,4},{4,0},{8,12},{12,8},{1,5},{5,1},{9,13},{13,9},{2,6},{6,2},{1... | collective-permute-start | bytes 1179656 | tf_op jit(solution)/shard_map/ppermute | solution.py:15
  12.2 5.4 collective-permute-start
  15.0 46.3 %collective-permute-start.6 = (bf16[192,768]{1,0:T(8,128)(2,1)}, bf16[192,768]{1,0:T(8,128)(2,1)S(1)}, u32[]{:S(2)}, u32[]{:S(2)}) collective-permute-start(bf16[192,768]{1,0:T(8,128)(2,1)} %bitcast.411), channel_id=1, source_target_pairs={{0,16},{16,0},{1,17},{17,1},{2,18},{18,2},{3,19},{19,3},{4,20},{20... | collective-permute-start | bytes 884744 | tf_op jit(solution)/shard_map/ppermute | solution.py:15
  17.6 25.4 %collective-permute-start.4 = (bf16[3,768,192]{1,2,0:T(8,128)(2,1)}, bf16[3,768,192]{1,2,0:T(8,128)(2,1)S(1)}, u32[]{:S(2)}, u32[]{:S(2)}) collective-permute-start(bf16[3,768,192]{1,2,0:T(8,128)(2,1)} %bitcast.412), channel_id=1, source_target_pairs={{0,16},{16,0},{1,17},{17,1},{2,18},{18,2},{3,19},{19,3},{4,20},{20... | collective-permute-start | bytes 2654216 | tf_op jit(solution)/shard_map/ppermute | solution.py:15
  20.8 24.4 %collective-permute-start.3 = (bf16[256,768]{0,1:T(8,128)(2,1)}, bf16[256,768]{0,1:T(8,128)(2,1)S(1)}, u32[]{:S(2)}, u32[]{:S(2)}) collective-permute-start(bf16[256,768]{0,1:T(8,128)(2,1)} %collective-permute-done.2), channel_id=1, source_target_pairs={{0,4},{4,0},{8,12},{12,8},{1,5},{5,1},{9,13},{13,9},{2,6},{6,2},{1... | collective-permute-start | bytes 1179656 | tf_op jit(solution)/shard_map/ppermute | solution.py:15
  64.2 28.6 %collective-permute-start.15 = (bf16[768,768]{1,0:T(8,128)(2,1)S(1)}, bf16[768,768]{1,0:T(8,128)(2,1)S(1)}, u32[]{:S(2)}, u32[]{:S(2)}) collective-permute-start(bf16[768,768]{1,0:T(8,128)(2,1)S(1)} %bitcast.374), channel_id=1, source_target_pairs={{0,16},{16,0},{1,17},{17,1},{2,18},{18,2},{3,19},{19,3},{4,20},{20... | collective-permute-start | bytes 3538952 | tf_op jit(solution)/shard_map/ppermute | solution.py:15
  66.0 11.6 %collective-permute-start.9 = (bf16[256,768]{0,1:T(8,128)(2,1)S(1)}, bf16[256,768]{0,1:T(8,128)(2,1)S(1)}, u32[]{:S(2)}, u32[]{:S(2)}) collective-permute-start(bf16[256,768]{0,1:T(8,128)(2,1)S(1)} %fusion.84), channel_id=1, source_target_pairs={{0,8},{4,12},{8,0},{12,4},{1,9},{5,13},{9,1},{13,5},{2,10},{6,14},... | collective-permute-start | bytes 1179656 | tf_op jit(solution)/shard_map/ppermute | solution.py:15
  78.3 10.8 %collective-permute-start.13 = (bf16[256,768]{0,1:T(8,128)(2,1)S(1)}, bf16[256,768]{0,1:T(8,128)(2,1)S(1)}, u32[]{:S(2)}, u32[]{:S(2)}) collective-permute-start(bf16[256,768]{0,1:T(8,128)(2,1)S(1)} %fusion.88), channel_id=1, source_target_pairs={{0,8},{4,12},{8,0},{12,4},{1,9},{5,13},{9,1},{13,5},{2,10},{6,14},... | collective-permute-start | bytes 1179656 | tf_op jit(solution)/shard_map/ppermute | solution.py:15
  78.8 14.0 %collective-permute-start.12 = (bf16[256,768]{0,1:T(8,128)(2,1)S(1)}, bf16[256,768]{0,1:T(8,128)(2,1)S(1)}, u32[]{:S(2)}, u32[]{:S(2)}) collective-permute-start(bf16[256,768]{0,1:T(8,128)(2,1)S(1)} %fusion.88), channel_id=1, source_target_pairs={{0,4},{4,0},{8,12},{12,8},{1,5},{5,1},{9,13},{13,9},{2,6},{6,2},{1... | collective-permute-start | bytes 1179656 | tf_op jit(solution)/shard_map/ppermute | solution.py:15
  90.6 28.1 %collective-permute-start.17 = (bf16[768,768]{1,0:T(8,128)(2,1)S(1)}, bf16[768,768]{1,0:T(8,128)(2,1)S(1)}, u32[]{:S(2)}, u32[]{:S(2)}) collective-permute-start(bf16[768,768]{1,0:T(8,128)(2,1)S(1)} %bitcast.373), channel_id=1, source_target_pairs={{0,16},{16,0},{1,17},{17,1},{2,18},{18,2},{3,19},{19,3},{4,20},{20... | collective-permute-start | bytes 3538952 | tf_op jit(solution)/shard_map/ppermute | solution.py:15
  122.2 11.2 %collective-permute-start.20 = (bf16[256,768]{0,1:T(8,128)(2,1)S(1)}, bf16[256,768]{0,1:T(8,128)(2,1)S(1)}, u32[]{:S(2)}, u32[]{:S(2)}) collective-permute-start(bf16[256,768]{0,1:T(8,128)(2,1)S(1)} %fusion.80), channel_id=1, source_target_pairs={{0,8},{4,12},{8,0},{12,4},{1,9},{5,13},{9,1},{13,5},{2,10},{6,14},... | collective-permute-start | bytes 1179656 | tf_op jit(solution)/shard_map/ppermute | solution.py:15
  134.3 10.4 %collective-permute-start.22 = (bf16[256,768]{0,1:T(8,128)(2,1)S(1)}, bf16[256,768]{0,1:T(8,128)(2,1)S(1)}, u32[]{:S(2)}, u32[]{:S(2)}) collective-permute-start(bf16[256,768]{0,1:T(8,128)(2,1)S(1)} %add_convert_fusion.9), channel_id=1, source_target_pairs={{0,8},{4,12},{8,0},{12,4},{1,9},{5,13},{9,1},{13,5},{2,10},{6,14},... | collective-permute-start | bytes 1179656 | tf_op jit(solution)/shard_map/ppermute | solution.py:15
  134.9 9.8 %collective-permute-start.21 = (bf16[256,768]{0,1:T(8,128)(2,1)S(1)}, bf16[256,768]{0,1:T(8,128)(2,1)S(1)}, u32[]{:S(2)}, u32[]{:S(2)}) collective-permute-start(bf16[256,768]{0,1:T(8,128)(2,1)S(1)} %add_convert_fusion.9), channel_id=1, source_target_pairs={{0,4},{4,0},{8,12},{12,8},{1,5},{5,1},{9,13},{13,9},{2,6},{6,2},{1... | collective-permute-start | bytes 1179656 | tf_op jit(solution)/shard_map/ppermute | solution.py:15
  170.4 11.2 %collective-permute-start.26 = (bf16[256,768]{0,1:T(8,128)(2,1)S(1)}, bf16[256,768]{0,1:T(8,128)(2,1)S(1)}, u32[]{:S(2)}, u32[]{:S(2)}) collective-permute-start(bf16[256,768]{0,1:T(8,128)(2,1)S(1)} %fusion.76), channel_id=1, source_target_pairs={{0,8},{4,12},{8,0},{12,4},{1,9},{5,13},{9,1},{13,5},{2,10},{6,14},... | collective-permute-start | bytes 1179656 | tf_op jit(solution)/shard_map/ppermute | solution.py:15
  182.5 10.4 %collective-permute-start.28 = (bf16[256,768]{0,1:T(8,128)(2,1)S(1)}, bf16[256,768]{0,1:T(8,128)(2,1)S(1)}, u32[]{:S(2)}, u32[]{:S(2)}) collective-permute-start(bf16[256,768]{0,1:T(8,128)(2,1)S(1)} %fusion.89), channel_id=1, source_target_pairs={{0,8},{4,12},{8,0},{12,4},{1,9},{5,13},{9,1},{13,5},{2,10},{6,14},... | collective-permute-start | bytes 1179656 | tf_op jit(solution)/shard_map/ppermute | solution.py:15
  183.1 9.8 %collective-permute-start.27 = (bf16[256,768]{0,1:T(8,128)(2,1)S(1)}, bf16[256,768]{0,1:T(8,128)(2,1)S(1)}, u32[]{:S(2)}, u32[]{:S(2)}) collective-permute-start(bf16[256,768]{0,1:T(8,128)(2,1)S(1)} %fusion.89), channel_id=1, source_target_pairs={{0,4},{4,0},{8,12},{12,8},{1,5},{5,1},{9,13},{13,9},{2,6},{6,2},{1... | collective-permute-start | bytes 1179656 | tf_op jit(solution)/shard_map/ppermute | solution.py:15
  209.6 11.5 %collective-permute-start.32 = (bf16[256,768]{0,1:T(8,128)(2,1)}, bf16[256,768]{0,1:T(8,128)(2,1)}, u32[]{:S(2)}, u32[]{:S(2)}) collective-permute-start(bf16[256,768]{0,1:T(8,128)(2,1)} %fusion.72), channel_id=1, source_target_pairs={{0,8},{4,12},{8,0},{12,4},{1,9},{5,13},{9,1},{13,5},{2,10},{6,14},... | collective-permute-start | bytes 1179656 | tf_op jit(solution)/shard_map/ppermute | solution.py:15
  223.7 10.4 %collective-permute-start.35 = (bf16[256,768]{0,1:T(8,128)(2,1)S(1)}, bf16[256,768]{0,1:T(8,128)(2,1)S(1)}, u32[]{:S(2)}, u32[]{:S(2)}) collective-permute-start(bf16[256,768]{0,1:T(8,128)(2,1)S(1)} %fusion.165), channel_id=1, source_target_pairs={{0,8},{4,12},{8,0},{12,4},{1,9},{5,13},{9,1},{13,5},{2,10},{6,14},... | collective-permute-start | bytes 1179656 | tf_op jit(solution)/shard_map/ppermute | solution.py:15
  224.3 9.8 %collective-permute-start.34 = (bf16[256,768]{0,1:T(8,128)(2,1)S(1)}, bf16[256,768]{0,1:T(8,128)(2,1)S(1)}, u32[]{:S(2)}, u32[]{:S(2)}) collective-permute-start(bf16[256,768]{0,1:T(8,128)(2,1)S(1)} %fusion.165), channel_id=1, source_target_pairs={{0,4},{4,0},{8,12},{12,8},{1,5},{5,1},{9,13},{13,9},{2,6},{6,2},{1... | collective-permute-start | bytes 1179656 | tf_op jit(solution)/shard_map/ppermute | solution.py:15
  244.5 11.2 %collective-permute-start.39 = (bf16[256,768]{0,1:T(8,128)(2,1)S(1)}, bf16[256,768]{0,1:T(8,128)(2,1)S(1)}, u32[]{:S(2)}, u32[]{:S(2)}) collective-permute-start(bf16[256,768]{0,1:T(8,128)(2,1)S(1)} %fusion.69), channel_id=1, source_target_pairs={{0,8},{4,12},{8,0},{12,4},{1,9},{5,13},{9,1},{13,5},{2,10},{6,14},... | collective-permute-start | bytes 1179656 | tf_op jit(solution)/shard_map/ppermute | solution.py:15
  257.3 10.4 %collective-permute-start.41 = (bf16[256,768]{0,1:T(8,128)(2,1)S(1)}, bf16[256,768]{0,1:T(8,128)(2,1)S(1)}, u32[]{:S(2)}, u32[]{:S(2)}) collective-permute-start(bf16[256,768]{0,1:T(8,128)(2,1)S(1)} %convert_element_type.423), channel_id=1, source_target_pairs={{0,8},{4,12},{8,0},{12,4},{1,9},{5,13},{9,1},{13,5},{2,10},{6,14},... | collective-permute-start | bytes 1179656 | tf_op jit(solution)/shard_map/ppermute | solution.py:15
  257.9 16.6 %collective-permute-start.40 = (bf16[256,768]{0,1:T(8,128)(2,1)S(1)}, bf16[256,768]{0,1:T(8,128)(2,1)S(1)}, u32[]{:S(2)}, u32[]{:S(2)}) collective-permute-start(bf16[256,768]{0,1:T(8,128)(2,1)S(1)} %convert_element_type.423), channel_id=1, source_target_pairs={{0,4},{4,0},{8,12},{12,8},{1,5},{5,1},{9,13},{13,9},{2,6},{6,2},{1... | collective-permute-start | bytes 1179656 | tf_op jit(solution)/shard_map/ppermute | solution.py:15
  267.7 6.8 collective-permute-start.42
  270.9 29.0 %collective-permute-start.76 = (bf16[768,768]{1,0:T(8,128)(2,1)}, bf16[768,768]{1,0:T(8,128)(2,1)}, u32[]{:S(2)}, u32[]{:S(2)}) collective-permute-start(bf16[768,768]{1,0:T(8,128)(2,1)} %get-tuple-element.196), channel_id=1, source_target_pairs={{0,16},{1,17},{2,18},{3,19},{4,20},{5,21},{6,22},{7,23},{8,24},{9,... | collective-permute-start | bytes 3538952 | tf_op jit(solution)/shard_map/ppermute | solution.py:277
  294.8 7.8 %collective-permute-start.43 = (bf16[256,768]{0,1:T(8,128)(2,1)S(1)}, bf16[256,768]{0,1:T(8,128)(2,1)S(1)}, u32[]{:S(2)}, u32[]{:S(2)}) collective-permute-start(bf16[256,768]{0,1:T(8,128)(2,1)S(1)} %get-tuple-element.100), channel_id=1, source_target_pairs={{0,4},{4,0},{8,12},{12,8},{1,5},{5,1},{9,13},{13,9},{2,6},{6,2},{1... | collective-permute-start | bytes 1179656 | tf_op jit(solution)/shard_map/ppermute | solution.py:15
  296.5 11.3 %collective-permute-start.45 = (bf16[256,768]{0,1:T(8,128)(2,1)S(1)}, bf16[256,768]{0,1:T(8,128)(2,1)S(1)}, u32[]{:S(2)}, u32[]{:S(2)}) collective-permute-start(bf16[256,768]{0,1:T(8,128)(2,1)S(1)} %fusion.65), channel_id=1, source_target_pairs={{0,8},{4,12},{8,0},{12,4},{1,9},{5,13},{9,1},{13,5},{2,10},{6,14},... | collective-permute-start | bytes 1179656 | tf_op jit(solution)/shard_map/ppermute | solution.py:15
  298.4 27.0 %collective-permute-start.74 = (bf16[768,768]{1,0:T(8,128)(2,1)S(1)}, bf16[768,768]{1,0:T(8,128)(2,1)S(1)}, u32[]{:S(2)}, u32[]{:S(2)}) collective-permute-start(bf16[768,768]{1,0:T(8,128)(2,1)S(1)} %get-tuple-element.192), channel_id=1, source_target_pairs={{0,16},{1,17},{2,18},{3,19},{4,20},{5,21},{6,22},{7,23},{8,24},{9,... | collective-permute-start | bytes 3538952 | tf_op jit(solution)/shard_map/ppermute | solution.py:277
  308.5 23.5 %collective-permute-start.47 = (bf16[256,768]{0,1:T(8,128)(2,1)S(1)}, bf16[256,768]{0,1:T(8,128)(2,1)S(1)}, u32[]{:S(2)}, u32[]{:S(2)}) collective-permute-start(bf16[256,768]{0,1:T(8,128)(2,1)S(1)} %fusion.163), channel_id=1, source_target_pairs={{0,8},{4,12},{8,0},{12,4},{1,9},{5,13},{9,1},{13,5},{2,10},{6,14},... | collective-permute-start | bytes 1179656 | tf_op jit(solution)/shard_map/ppermute | solution.py:15
  327.5 32.3 %collective-permute-start.72 = (bf16[192,768]{1,0:T(8,128)(2,1)S(1)}, bf16[192,768]{1,0:T(8,128)(2,1)S(1)}, u32[]{:S(2)}, u32[]{:S(2)}) collective-permute-start(bf16[192,768]{1,0:T(8,128)(2,1)S(1)} %get-tuple-element.188), channel_id=1, source_target_pairs={{0,16},{1,17},{2,18},{3,19},{4,20},{5,21},{6,22},{7,23},{8,24},{9,... | collective-permute-start | bytes 884744 | tf_op jit(solution)/shard_map/ppermute | solution.py:277
  342.3 21.2 %collective-permute-start.60 = (bf16[3,768,192]{1,2,0:T(8,128)(2,1)S(1)}, bf16[3,768,192]{1,2,0:T(8,128)(2,1)S(1)}, u32[]{:S(2)}, u32[]{:S(2)}) collective-permute-start(bf16[3,768,192]{1,2,0:T(8,128)(2,1)S(1)} %fusion.36), channel_id=1, source_target_pairs={{0,16},{1,17},{2,18},{3,19},{4,20},{5,21},{6,22},{7,23},{8,24},{9,... | collective-permute-start | bytes 2654216 | tf_op jit(solution)/shard_map/ppermute | solution.py:277
  344.4 11.2 %collective-permute-start.51 = (bf16[256,768]{0,1:T(8,128)(2,1)S(1)}, bf16[256,768]{0,1:T(8,128)(2,1)S(1)}, u32[]{:S(2)}, u32[]{:S(2)}) collective-permute-start(bf16[256,768]{0,1:T(8,128)(2,1)S(1)} %fusion.62), channel_id=1, source_target_pairs={{0,8},{4,12},{8,0},{12,4},{1,9},{5,13},{9,1},{13,5},{2,10},{6,14},... | collective-permute-start | bytes 1179656 | tf_op jit(solution)/shard_map/ppermute | solution.py:15
  347.5 29.6 %collective-permute-start.75 = (bf16[768,768]{1,0:T(8,128)(2,1)S(1)}, bf16[768,768]{1,0:T(8,128)(2,1)S(1)}, u32[]{:S(2)}, u32[]{:S(2)}) collective-permute-start(bf16[768,768]{1,0:T(8,128)(2,1)S(1)} %get-tuple-element.194), channel_id=1, source_target_pairs={{16,0},{17,1},{18,2},{19,3},{20,4},{21,5},{22,6},{23,7},{24,8},{25... | collective-permute-start | bytes 3538952 | tf_op jit(solution)/shard_map/ppermute | solution.py:277
  358.2 10.3 %collective-permute-start.53 = (bf16[256,768]{0,1:T(8,128)(2,1)S(1)}, bf16[256,768]{0,1:T(8,128)(2,1)S(1)}, u32[]{:S(2)}, u32[]{:S(2)}) collective-permute-start(bf16[256,768]{0,1:T(8,128)(2,1)S(1)} %convert_element_type.443), channel_id=1, source_target_pairs={{0,8},{4,12},{8,0},{12,4},{1,9},{5,13},{9,1},{13,5},{2,10},{6,14},... | collective-permute-start | bytes 1179656 | tf_op jit(solution)/shard_map/ppermute | solution.py:15
  364.6 13.8 %collective-permute-start.52 = (bf16[256,768]{0,1:T(8,128)(2,1)S(1)}, bf16[256,768]{0,1:T(8,128)(2,1)S(1)}, u32[]{:S(2)}, u32[]{:S(2)}) collective-permute-start(bf16[256,768]{0,1:T(8,128)(2,1)S(1)} %convert_element_type.443), channel_id=1, source_target_pairs={{0,4},{4,0},{8,12},{12,8},{1,5},{5,1},{9,13},{13,9},{2,6},{6,2},{1... | collective-permute-start | bytes 1179656 | tf_op jit(solution)/shard_map/ppermute | solution.py:15
  368.5 10.0 %collective-permute-start.54 = (bf16[256,768]{0,1:T(8,128)(2,1)S(1)}, bf16[256,768]{0,1:T(8,128)(2,1)S(1)}, u32[]{:S(2)}, u32[]{:S(2)}) collective-permute-start(bf16[256,768]{0,1:T(8,128)(2,1)S(1)} %collective-permute-done.53), channel_id=1, source_target_pairs={{0,4},{4,0},{8,12},{12,8},{1,5},{5,1},{9,13},{13,9},{2,6},{6,2},{1... | collective-permute-start | bytes 1179656 | tf_op jit(solution)/shard_map/ppermute | solution.py:15
  371.7 34.6 %collective-permute-start.73 = (bf16[768,768]{1,0:T(8,128)(2,1)}, bf16[768,768]{1,0:T(8,128)(2,1)}, u32[]{:S(2)}, u32[]{:S(2)}) collective-permute-start(bf16[768,768]{1,0:T(8,128)(2,1)} %get-tuple-element.190), channel_id=1, source_target_pairs={{16,0},{17,1},{18,2},{19,3},{20,4},{21,5},{22,6},{23,7},{24,8},{25... | collective-permute-start | bytes 3538952 | tf_op jit(solution)/shard_map/ppermute | solution.py:277
  402.7 29.6 %collective-permute-start.59 = (bf16[3,768,192]{1,2,0:T(8,128)(2,1)S(1)}, bf16[3,768,192]{1,2,0:T(8,128)(2,1)S(1)}, u32[]{:S(2)}, u32[]{:S(2)}) collective-permute-start(bf16[3,768,192]{1,2,0:T(8,128)(2,1)S(1)} %fusion.37), channel_id=1, source_target_pairs={{16,0},{17,1},{18,2},{19,3},{20,4},{21,5},{22,6},{23,7},{24,8},{25... | collective-permute-start | bytes 2654216 | tf_op jit(solution)/shard_map/ppermute | solution.py:277
  404.9 26.7 %collective-permute-start.71 = (bf16[192,768]{1,0:T(8,128)(2,1)S(1)}, bf16[192,768]{1,0:T(8,128)(2,1)S(1)}, u32[]{:S(2)}, u32[]{:S(2)}) collective-permute-start(bf16[192,768]{1,0:T(8,128)(2,1)S(1)} %get-tuple-element.186), channel_id=1, source_target_pairs={{16,0},{17,1},{18,2},{19,3},{20,4},{21,5},{22,6},{23,7},{24,8},{25... | collective-permute-start | bytes 884744 | tf_op jit(solution)/shard_map/ppermute | solution.py:277
  435.8 9.3 %collective-permute-start.33 = (bf16[256,768]{0,1:T(8,128)(2,1)}, bf16[256,768]{0,1:T(8,128)(2,1)}, u32[]{:S(2)}, u32[]{:S(2)}) collective-permute-start(bf16[256,768]{0,1:T(8,128)(2,1)} %get-tuple-element.80), channel_id=1, source_target_pairs={{0,16},{16,0},{1,17},{17,1},{2,18},{18,2},{3,19},{19,3},{4,20},{20... | collective-permute-start | bytes 1179656 | tf_op jit(solution)/shard_map/ppermute | solution.py:15
  436.1 10.5 %collective-permute-start.66 = (f32[6,768]{1,0:T(8,128)S(1)}, f32[6,768]{1,0:T(8,128)S(1)}, u32[]{:S(2)}, u32[]{:S(2)}) collective-permute-start(f32[6,768]{1,0:T(8,128)S(1)} %stack.132), channel_id=1, source_target_pairs={{0,4},{4,0},{8,12},{12,8},{1,5},{5,1},{9,13},{13,9},{2,6},{6,2},{1... | collective-permute-start | bytes 55304 | tf_op jit(solution)/shard_map/ppermute | solution.py:15
  452.5 6.1 collective-permute-start.68
  460.3 9.3 %collective-permute-start.55 = (bf16[256,768]{0,1:T(8,128)(2,1)S(1)}, bf16[256,768]{0,1:T(8,128)(2,1)S(1)}, u32[]{:S(2)}, u32[]{:S(2)}) collective-permute-start(bf16[256,768]{0,1:T(8,128)(2,1)S(1)} %get-tuple-element.96), channel_id=1, source_target_pairs={{0,4},{4,0},{8,12},{12,8},{1,5},{5,1},{9,13},{13,9},{2,6},{6,2},{1... | collective-permute-start | bytes 1179656 | tf_op jit(solution)/shard_map/ppermute | solution.py:15
  461.8 10.4 %collective-permute-start.57 = (bf16[256,768]{0,1:T(8,128)(2,1)S(1)}, bf16[256,768]{0,1:T(8,128)(2,1)S(1)}, u32[]{:S(2)}, u32[]{:S(2)}) collective-permute-start(bf16[256,768]{0,1:T(8,128)(2,1)S(1)} %fusion.58), channel_id=1, source_target_pairs={{0,8},{4,12},{8,0},{12,4},{1,9},{5,13},{9,1},{13,5},{2,10},{6,14},... | collective-permute-start | bytes 1179656 | tf_op jit(solution)/shard_map/ppermute | solution.py:15
  463.2 11.2 %collective-permute-start.70 = (f32[45,128]{1,0:T(8,128)S(1)}, f32[45,128]{1,0:T(8,128)S(1)}, u32[]{:S(2)}, u32[]{:S(2)}) collective-permute-start(f32[45,128]{1,0:T(8,128)S(1)} %fusion.249), channel_id=1, source_target_pairs={{0,2},{1,3},{2,0},{3,1},{4,6},{5,7},{6,4},{7,5},{8,10},{9,11},{10,... | collective-permute-start | bytes 69128 | tf_op jit(solution)/shard_map/ppermute | solution.py:15
  465.8 8.6 %collective-permute-start.65 = (f32[45,128]{1,0:T(8,128)S(1)}, f32[45,128]{1,0:T(8,128)S(1)}, u32[]{:S(2)}, u32[]{:S(2)}) collective-permute-start(f32[45,128]{1,0:T(8,128)S(1)} %fusion.248), channel_id=1, source_target_pairs={{0,2},{1,3},{2,0},{3,1},{4,6},{5,7},{6,4},{7,5},{8,10},{9,11},{10,... | collective-permute-start | bytes 69128 | tf_op jit(solution)/shard_map/ppermute | solution.py:15
  472.6 10.4 %collective-permute-start.58 = (bf16[256,768]{0,1:T(8,128)(2,1)S(1)}, bf16[256,768]{0,1:T(8,128)(2,1)S(1)}, u32[]{:S(2)}, u32[]{:S(2)}) collective-permute-start(bf16[256,768]{0,1:T(8,128)(2,1)S(1)} %get-tuple-element.75), channel_id=1, source_target_pairs={{0,16},{16,0},{1,17},{17,1},{2,18},{18,2},{3,19},{19,3},{4,20},{20... | collective-permute-start | bytes 1179656 | tf_op jit(solution)/shard_map/ppermute | solution.py:15
  (168 other events, 1558.1 us)
Sparse Core Ops, SparseCore 0:
  433.6 252.1 all-reduce.2

commit v2 on v1

v2 whole, which is shorter than its diff:
```python
from functools import partial

import jax
import jax.numpy as jnp
from jax import lax
from jax.experimental import pallas as pl
from jax.experimental.pallas import tpu as pltpu
from jax.sharding import PartitionSpec as P

BF16 = jnp.bfloat16
F32 = jnp.float32
HEAD_DIM = 64
PAIR = 2 * HEAD_DIM
LOG2E = 1.4426950408889634
MASKED = -1e30
VMEM_LIMIT = 16 * 1024 * 1024
NORM_EPSILON_TERM = 1e-06

FLAGS = 5

SPACES = {"v": pltpu.VMEM, "s": pltpu.SMEM, "h": pl.ANY}
PLACES = {"v": pltpu.VMEM, "s": pl.ANY, "h": pltpu.HBM}


def shape(dims, dtype=BF16):
    return jax.ShapeDtypeStruct(dims, dtype)


def call(kernel, outs, args, flops=0, scratch=(), copies=0):
    scratch = list(scratch)
    if copies:
        scratch.append(pltpu.SemaphoreType.DMA((copies,)))
    return pl.pallas_call(
        kernel,
        out_shape=[PLACES[space](item.shape, item.dtype) for space, item in outs],
        in_specs=[pl.BlockSpec(memory_space=SPACES[space]) for space, _ in args],
        out_specs=[pl.BlockSpec(memory_space=SPACES[space]) for space, _ in outs],
        scratch_shapes=scratch,
        compiler_params=pltpu.CompilerParams(vmem_limit_bytes=VMEM_LIMIT),
        cost_estimate=pl.CostEstimate(flops=flops, bytes_accessed=0, transcendentals=0),
    )(*[pltpu.with_memory_space_constraint(item, PLACES[space]) for space, item in args])


class Copies:
    def __init__(self, sems):
        self.sems, self.pending = sems, []

    def start(self, source, target):
        copy = pltpu.make_async_copy(source, target, self.sems.at[len(self.pending)])
        copy.start()
        self.pending.append(copy)

    def start_one(self, cases, target):
        sem = self.sems.at[len(self.pending)]
        made = []
        for condition, source in cases:
            made.append(pltpu.make_async_copy(source, target, sem))
            pl.when(condition)(made[-1].start)
        self.pending.append(made[0])

    def done(self):
        for copy in self.pending:
            copy.wait()


def dot(left, right):
    return jnp.dot(left, right, preferred_element_type=F32)


def dot_tn(left, right):
    return lax.dot_general(left, right, (((0,), (0,)), ((), ())), preferred_element_type=F32)


def dot_nt(left, right):
    return lax.dot_general(left, right, (((1,), (1,)), ((), ())), preferred_element_type=F32)


def pack_kernel(gains_in, shifts_in, up_in, qkv_in, perm_ref, out_ref, gains, shifts, up, qkv_b, sems):
    copies = Copies(sems)
    for source, target in ((gains_in, gains), (shifts_in, shifts), (up_in, up), (qkv_in, qkv_b)):
        copies.start(source, target)
    out_ref[...] = jnp.zeros_like(out_ref)
    lane = lax.broadcasted_iota(jnp.int32, (1, out_ref.shape[1]), 1)
    flags = jnp.zeros((1, out_ref.shape[1]), F32)
    for head in range(perm_ref.shape[1]):
        flags = jnp.where(lane == head, perm_ref[0, head, 0].astype(F32), flags)
    out_ref[9:10] = flags
    copies.done()
    out_ref[0:2] = gains[0]
    out_ref[2:6] = shifts[0]
    out_ref[6:7] = up[...].astype(F32)
    out_ref[7:9, 0 : qkv_b.shape[2]] = qkv_b[0].astype(F32)


GAIN1, GAIN2, BIAS_OUT, SHIFT1, BIAS2, SHIFT2, BIAS_UP, BIAS_Q, TURNED = 0, 1, 2, 3, 4, 5, 6, 8, 10


def params_kernel(where_ref, own_ref, other_ref, pair_ref, other_pair_ref, first_out, second_out, flags_copy, flags, sems):
    section, core = where_ref[0], where_ref[1]
    width = own_ref.shape[1]
    local = width // 4
    heads = local // HEAD_DIM
    lane = lax.broadcasted_iota(jnp.int32, (1, width), 1)
    flags[...] = jnp.zeros_like(flags)
    for layer, out_ref in enumerate((first_out, second_out)):
        here = section == layer
        mine = jnp.where(here, own_ref[...], other_ref[...])
        pair = jnp.where(here, pair_ref[...], other_pair_ref[...])
        first = jnp.where(core == 0, mine, pair)
        second = jnp.where(core == 0, pair, mine)
        out_ref[...] = mine
        out_ref[BIAS_UP + 1 : BIAS_UP + 2] = pair[BIAS_UP : BIAS_UP + 1]
        biases = jnp.where(lane < local, first, pltpu.roll(second, local, 1))
        out_ref[BIAS_Q : BIAS_Q + 2] = biases[7:9]
        turned = jnp.where(lane < heads, first, pltpu.roll(second, heads, 1))[9:10]
        lanes = jnp.zeros((1, width), F32)
        for head in range(2 * heads):
            chosen = (lane // HEAD_DIM) % (2 * heads) == head
            lanes = jnp.where(chosen, turned[:, head : head + 1], lanes)
        out_ref[TURNED : TURNED + 1] = lanes
        flags[layer : layer + 1] = turned[:, 0:PAIR]
    copies = Copies(sems)
    copies.start(flags, flags_copy)
    copies.done()


def marks_kernel(where_ref, segments_ref, real_ref, out_ref):
    quarter = out_ref.shape[1] // 2
    out_ref[...] = jnp.zeros_like(out_ref)
    for r in range(4):
        cols = pl.ds(pl.multiple_of((where_ref[4] ^ r) * quarter, PAIR), quarter)
        at = slice((r % 2) * quarter, (r % 2 + 1) * quarter)
        segment = jnp.where(where_ref[0] == 0, segments_ref[0:1, cols], segments_ref[1:2, cols])
        real = jnp.where(where_ref[0] == 0, real_ref[0:1, cols], real_ref[1:2, cols])
        out_ref[1 + r // 2 : 2 + r // 2, at] = jnp.where(real == 1, segment, -1)
        if r % 2 == 0:
            out_ref[0:1, (r // 2) * quarter : (r // 2 + 1) * quarter] = segment


def halve_kernel(where_ref, *refs):
    count = len(refs) // 2
    copies = Copies(refs[-1])
    for source, half in zip(refs[:count], refs[count:-1]):
        columns = half.shape[2]
        copies.start_one(
            [
                (where_ref[2] == side, source.at[:, :, pl.ds(side * columns, columns)])
                for side in range(2)
            ],
            half,
        )
    copies.done()


def halves_of(where, *wholes):
    return call(
        halve_kernel,
        [("v", shape(whole.shape[:2] + (whole.shape[2] // 2,))) for whole in wholes],
        [("s", where)] + [("h", whole) for whole in wholes],
        copies=len(wholes),
    )


def weight_copies(copies, where_ref, layer, k, own, other, target):
    here = where_ref[0] == layer
    if len(other) == 1:
        copies.start_one(
            [(here, own.at[k]), (jnp.logical_not(here), other[0].at[k])], target(slice(None))
        )
        return
    columns = other[0].shape[-1]
    for side in range(2):
        cols = pl.ds(side * columns, columns)
        direct = where_ref[2] == side
        copies.start_one(
            [
                (here, own.at[k, :, cols]),
                (jnp.logical_not(here) & direct, other[0].at[k]),
                (jnp.logical_not(here) & jnp.logical_not(direct), other[1].at[k]),
            ],
            target(cols),
        )


def load_kernel(layer, items, plain, where_ref, *refs):
    sems = refs[-1]
    copies = Copies(sems)
    count = sum(2 * (1 + parts) for _, parts in items)
    sources, plain_in, outs = refs[:count], refs[count : count + plain], refs[count + plain : -1]
    for (by_core, parts), out_ref in zip(items, outs):
        for pair in range(2):
            own, *other = sources[: 1 + parts]
            sources = sources[1 + parts :]
            if by_core:
                rows = out_ref.shape[1] // 2
                slot = (where_ref[1] + pair) % 2
                at = pl.ds(pl.multiple_of(slot * rows, rows), rows)
                for k in range(out_ref.shape[0]):
                    weight_copies(
                        copies, where_ref, layer, k, own, other, lambda cols, k=k: out_ref.at[k, at, cols]
                    )
            else:
                weight_copies(
                    copies, where_ref, layer, 0, own, other, lambda cols: out_ref.at[pair, :, cols]
                )
    for source, target in zip(plain_in, outs[len(items) :]):
        copies.start(source, target)
    copies.done()


def load(layer, where, items, arrays=()):
    outs, sources, kinds, count = [], [], [], len(arrays)
    for by_core, own, other, pair_own, pair_other in items:
        k, rows, columns = own.shape
        outs.append(shape((k, 2 * rows, columns)) if by_core else shape((2, rows, columns)))
        sources += [own, *other, pair_own, *pair_other]
        kinds.append((by_core, len(other)))
        count += 2 * k * len(other)
    outs += [shape(item.shape, item.dtype) for item in arrays]
    return call(
        partial(load_kernel, layer, kinds, len(arrays)),
        [("v", item) for item in outs],
        [("s", where)] + [("h", item) for item in (*sources, *arrays)],
        copies=count,
    )


def qkv_kernel(x_ref, w_ref, b_ref, q_ref, kv_ref, x_copy, q_copy, sems):
    copies = Copies(sems)
    copies.start(x_ref, x_copy)
    x = x_ref[...]
    width = q_ref.shape[1]
    q_ref[...] = (dot_nt(x, w_ref[0]) + b_ref[BIAS_Q : BIAS_Q + 1, :width]).astype(BF16)
    copies.start(q_ref, q_copy)
    kv_ref[:, :width] = dot_nt(x, w_ref[1]).astype(BF16)
    kv_ref[:, width:] = (dot_nt(x, w_ref[2]) + b_ref[BIAS_Q + 1 : BIAS_Q + 2, :width]).astype(BF16)
    copies.done()


def qkv(x, w, b):
    rows, width = x.shape[0], w.shape[1]
    return call(
        qkv_kernel,
        [
            ("v", shape((rows, width))),
            ("v", shape((rows, 2 * width))),
            ("h", shape(x.shape)),
            ("h", shape((rows, width))),
        ],
        [("v", x), ("v", w), ("v", b)],
        6 * rows * x.shape[1] * width,
        copies=2,
    )


def lanes_of(rows):
    return lax.broadcasted_iota(jnp.int32, (rows, PAIR), 1)


def fill_bias(bias, side, marks_ref):
    rows = bias.shape[1]
    wanted = jnp.transpose(marks_ref[:, side * rows : (side + 1) * rows])[:, 0:1]
    for j in range(2):
        bias[j] = jnp.where(wanted == marks_ref[1 + j : 2 + j, :], 0.0, MASKED).astype(F32)


def block_of(where_ref, layer, head, turned):
    return where_ref[FLAGS + 6 * layer + head] ^ turned


def attn_rows(layer, where_ref, turned, q_ref, kv_ref, marks_ref, o_ref, lse_ref, bias):
    rows, width = q_ref.shape
    fill_bias(bias, turned, marks_ref)
    lanes = lanes_of(rows)
    low = lanes < HEAD_DIM
    scale = HEAD_DIM**-0.5 * LOG2E
    logs = jnp.zeros((rows, PAIR), F32)
    for tile in range(width // PAIR):
        cols = slice(tile * PAIR, (tile + 1) * PAIR)
        vcols = slice(width + cols.start, width + cols.stop)
        q = q_ref[:, cols]
        mixed = []
        for side in range(2):
            head = 2 * tile + side
            block = block_of(where_ref, layer, head, turned)
            q_head = jnp.where(low if side == 0 else ~low, q, jnp.zeros_like(q))
            s = dot_nt(q_head, kv_ref[block, :, cols]) * scale + bias[block]
            top = jnp.maximum(jnp.max(s, axis=1, keepdims=True), 0.0)
            e = jnp.exp2(s - top)
            total = jnp.exp2(-top) + jnp.sum(e, axis=1, keepdims=True)
            p = (e * (1.0 / total)).astype(BF16)
            mixed.append(dot(p, kv_ref[block, :, vcols]))
            logs = jnp.where(lanes == head, top + jnp.log2(total), logs)
        o_ref[:, cols] = jnp.where(low, mixed[0], mixed[1]).astype(BF16)
    lse_ref[...] = logs


def attn_far_kernel(
    layer, where_ref, q_ref, kv0_ref, kv1_ref, kv2_ref, kv3_ref, marks_ref, w_ref,
    out_ref, kv_ref, kv_copy, o_copy, lse_copy, bias, o_ref, lse_ref, sems,
):
    copies = Copies(sems)
    half = kv0_ref.shape[0]
    for block, pair in enumerate(((kv0_ref, kv1_ref), (kv2_ref, kv3_ref))):
        kv_ref[block, :half] = pair[0][...]
        kv_ref[block, half:] = pair[1][...]
    copies.start(kv_ref, kv_copy)
    attn_rows(layer, where_ref, 1, q_ref, kv_ref, marks_ref, o_ref, lse_ref, bias)
    copies.start(o_ref, o_copy)
    copies.start(lse_ref, lse_copy)
    out_ref[...] = dot(o_ref[...], w_ref[0]).astype(out_ref.dtype)
    copies.done()


def attn_own_kernel(
    layer, where_ref, q_ref, kv_ref, marks_ref, w_ref, out_ref, o_copy, lse_copy, bias, o_ref, lse_ref, sems
):
    copies = Copies(sems)
    attn_rows(layer, where_ref, 0, q_ref, kv_ref, marks_ref, o_ref, lse_ref, bias)
    copies.start(o_ref, o_copy)
    copies.start(lse_ref, lse_copy)
    out_ref[...] = dot(o_ref[...], w_ref[0]).astype(out_ref.dtype)
    copies.done()


def attn(layer, where, q, kv, marks, w):
    rows, width = q.shape
    far = len(kv) > 1
    outs = [("v", shape((rows, w.shape[2]), BF16 if far else F32))]
    if far:
        joined = shape((2, 2 * rows, kv[0].shape[1]))
        outs += [("v", joined), ("h", joined)]
    outs += [("h", shape((rows, width))), ("h", shape((rows, PAIR), F32))]
    args = [("s", where)] + [("v", item) for item in (q, *kv, marks, w)]
    return call(
        partial(attn_far_kernel if far else attn_own_kernel, layer),
        outs,
        args,
        8 * rows * rows * width + 2 * rows * width * w.shape[2],
        scratch=[
            pltpu.VMEM((2, rows, 2 * rows), F32),
            pltpu.VMEM((rows, width), BF16),
            pltpu.VMEM((rows, PAIR), F32),
        ],
        copies=3 if far else 2,
    )


def normed_rows(resid):
    centred = resid - jnp.mean(resid, axis=1, keepdims=True)
    inverse = lax.rsqrt(jnp.mean(centred * centred, axis=1, keepdims=True) + NORM_EPSILON_TERM)
    return centred * inverse, inverse


def norm1_kernel(x_ref, own_ref, far_ref, norms_ref, low_ref, full_ref, resid_copy, low_copy, resid, sems):
    copies = Copies(sems)
    projected = own_ref[...] + far_ref[...].astype(F32)
    total = x_ref[...].astype(F32) + projected + norms_ref[BIAS_OUT : BIAS_OUT + 1, :]
    resid[...] = total
    copies.start(resid, resid_copy)
    hidden = normed_rows(total)[0] * norms_ref[GAIN1 : GAIN1 + 1, :] + norms_ref[SHIFT1 : SHIFT1 + 1, :]
    full_ref[...] = hidden
    low_ref[...] = hidden.astype(BF16)
    copies.start(low_ref, low_copy)
    copies.done()


def norm1(x, own, far, norms):
    return call(
        norm1_kernel,
        [("v", shape(x.shape)), ("v", shape(x.shape, F32)), ("h", shape(x.shape, F32)), ("h", shape(x.shape))],
        [("v", x), ("v", own), ("v", far), ("v", norms)],
        scratch=[pltpu.VMEM(x.shape, F32)],
        copies=2,
    )


def norm2_kernel(h_ref, own_ref, far_ref, norms_ref, low_ref, resid_copy, low_copy, resid, sems):
    copies = Copies(sems)
    branch = own_ref[...] + far_ref[...].astype(F32)
    total = h_ref[...] + branch + norms_ref[BIAS2 : BIAS2 + 1, :]
    resid[...] = total
    copies.start(resid, resid_copy)
    out = normed_rows(total)[0] * norms_ref[GAIN2 : GAIN2 + 1, :] + norms_ref[SHIFT2 : SHIFT2 + 1, :]
    low_ref[...] = out.astype(BF16)
    copies.start(low_ref, low_copy)
    copies.done()


def norm2(h, own, far, norms):
    return call(
        norm2_kernel,
        [("v", shape(h.shape)), ("h", shape(h.shape, F32)), ("h", shape(h.shape))],
        [("v", h), ("v", own), ("v", far), ("v", norms)],
        scratch=[pltpu.VMEM(h.shape, F32)],
        copies=2,
    )


TAIL = tuple(
    0.5 * c
    for c in (
        0.05029408002973294, -0.1830316054165625, 0.16930258232763196, -0.005798692821681883,
        0.14152663657068731, 0.16851528425000623, 0.20784663429852349, 0.22566934002005623,
        0.22567586682378352,
    )
)


def gelu_and_slope(u):
    bell = jnp.exp2(u * u * (-0.5 * LOG2E))
    t = 1.0 / (1.0 + jnp.abs(u) * (0.4 * 0.5**0.5))
    poly = TAIL[0]
    for c in TAIL[1:]:
        poly = poly * t + c
    tail = poly * t * bell
    below = jnp.where(u < 0.0, tail, 1.0 - tail)
    return u * below, below + u * bell * 0.3989422804014327


def ffn_kernel(far, h_ref, up_ref, down_ref, b_ref, out_ref, act_copy, slope_copy, *rest):
    act_ref, slope_ref, sems = rest[-3:]
    copies = Copies(sems)
    if far:
        copies.start(h_ref, rest[0])
    h = h_ref[...]
    units = up_ref.shape[2]
    total = None
    for half in range(2):
        cols = slice(half * units, (half + 1) * units)
        act, slope = gelu_and_slope(dot(h, up_ref[half]) + b_ref[BIAS_UP + half : BIAS_UP + half + 1, :])
        act = act.astype(BF16)
        act_ref[:, cols] = act
        slope_ref[:, cols] = slope.astype(BF16)
        copies.start(act_ref.at[:, cols], act_copy.at[:, cols])
        copies.start(slope_ref.at[:, cols], slope_copy.at[:, cols])
        part = dot(act, down_ref[half])
        total = part if total is None else total + part
    out_ref[...] = total.astype(out_ref.dtype)
    copies.done()


def ffn(h, up, down, b, far):
    rows, width = h.shape
    units = 2 * up.shape[2]
    outs = [
        ("v", shape((rows, width), BF16 if far else F32)),
        ("h", shape((rows, units))),
        ("h", shape((rows, units))),
    ]
    if far:
        outs.append(("h", shape(h.shape)))
    return call(
        partial(ffn_kernel, far),
        outs,
        [("v", h), ("v", up), ("v", down), ("v", b)],
        4 * rows * width * units,
        scratch=[pltpu.VMEM((rows, units), BF16)] * 2,
        copies=5,
    )


def norm_back(upstream, resid, gain, low_ref, full_ref, sums_ref):
    normed, inverse = normed_rows(resid)
    scaled = upstream * gain
    inner = (
        scaled
        - jnp.mean(scaled, axis=1, keepdims=True)
        - normed * jnp.mean(scaled * normed, axis=1, keepdims=True)
    )
    grad = inverse * inner
    full_ref[...] = grad
    low_ref[...] = grad.astype(BF16)
    sums_ref[...] = jnp.zeros_like(sums_ref)
    sums_ref[0:1] = jnp.sum(upstream * normed, axis=0, keepdims=True)
    sums_ref[1:2] = jnp.sum(upstream, axis=0, keepdims=True)
    sums_ref[2:3] = jnp.sum(grad, axis=0, keepdims=True)


def norm2_back_kernel(inner, *refs):
    if inner:
        own_ref, far_ref, resid1_ref, resid_in, norms_ref, low_ref, full_ref, sums_ref, grad_ref, resid, sems = refs
    else:
        up_ref, resid_in, norms_ref, low_ref, full_ref, sums_ref, resid, sems = refs
    copies = Copies(sems)
    copies.start(resid_in, resid)
    if inner:
        grad_in = (own_ref[...] + far_ref[...].astype(F32) + resid1_ref[...]).astype(BF16)
        grad_ref[...] = grad_in
    else:
        grad_in = up_ref[...]
    copies.done()
    gain = norms_ref[GAIN2 : GAIN2 + 1, :]
    norm_back(grad_in.astype(F32), resid[...], gain, low_ref, full_ref, sums_ref)


def norm2_back(upstream, resid, norms):
    dims = upstream[0].shape
    inner = len(upstream) > 1
    outs = [("v", shape(dims)), ("v", shape(dims, F32)), ("v", shape((8, dims[1]), F32))]
    if inner:
        outs.append(("v", shape(dims)))
    return call(
        partial(norm2_back_kernel, inner),
        outs,
        [("v", item) for item in upstream] + [("h", resid), ("v", norms)],
        scratch=[pltpu.VMEM(dims, F32)],
        copies=1,
    )


def norm1_back_kernel(own_ref, far_ref, skip_ref, resid_in, norms_ref, low_ref, full_ref, sums_ref, resid, sems):
    copies = Copies(sems)
    copies.start(resid_in, resid)
    upstream = own_ref[...] + far_ref[...].astype(F32) + skip_ref[...]
    copies.done()
    gain = norms_ref[GAIN1 : GAIN1 + 1, :]
    norm_back(upstream, resid[...], gain, low_ref, full_ref, sums_ref)


def norm1_back(own, far, skip, resid, norms):
    dims = own.shape
    return call(
        norm1_back_kernel,
        [("v", shape(dims)), ("v", shape(dims, F32)), ("v", shape((8, dims[1]), F32))],
        [("v", own), ("v", far), ("v", skip), ("h", resid), ("v", norms)],
        scratch=[pltpu.VMEM(dims, F32)],
        copies=1,
    )


def ffn_back_kernel(df_ref, slope_ref, up_ref, down_ref, dh_ref, du_ref, db_ref):
    df = df_ref[...]
    units = up_ref.shape[2]
    total = None
    for half in range(2):
        cols = slice(half * units, (half + 1) * units)
        du = (dot_nt(df, down_ref[half]) * slope_ref[:, cols].astype(F32)).astype(BF16)
        du_ref[:, cols] = du
        db_ref[half : half + 1, :] = jnp.sum(du.astype(F32), axis=0, keepdims=True)
        part = dot_nt(du, up_ref[half])
        total = part if total is None else total + part
    dh_ref[...] = total.astype(dh_ref.dtype)


def ffn_back(df, slope, up, down, far):
    rows, width = df.shape
    units = 2 * up.shape[2]
    return call(
        ffn_back_kernel,
        [
            ("v", shape((rows, width), BF16 if far else F32)),
            ("v", shape((rows, units))),
            ("v", shape((2, units // 2), F32)),
        ],
        [("v", df), ("v", slope), ("v", up), ("v", down)],
        4 * rows * width * units,
    )


def ffn_grads_of(half, h, act, df, du):
    units = act[0].shape[1] // 2
    cols = slice(half * units, (half + 1) * units)
    up = dot_tn(h[0][...], du[0][:, cols]) + dot_tn(h[1][...], du[1][:, cols])
    down = dot_tn(act[0][:, cols], df[0][...]) + dot_tn(act[1][:, cols], df[1][...])
    return up, down


def ffn_pair_kernel(h0, h1, a0, a1, df0, df1, du0, du1, out_ref):
    up, down = ffn_grads_of(1, (h0, h1), (a0, a1), (df0, df1), (du0, du1))
    out_ref[0] = up.astype(BF16)
    out_ref[1] = down.astype(BF16)


def ffn_own_kernel(where_ref, h0, h1, a0, a1, df0, df1, du0, du1, got_ref, *outs):
    up, down = ffn_grads_of(0, (h0, h1), (a0, a1), (df0, df1), (du0, du1))
    up += got_ref[0].astype(F32)
    down += got_ref[1].astype(F32)
    first = where_ref[0] == 0
    half = outs[0].shape[0]
    for part in range(2):
        rows = slice(part * half, (part + 1) * half)
        outs[2 * part][...] = jnp.where(first, down[rows], up[rows]).astype(BF16)
        outs[2 * part + 1][...] = jnp.where(first, up[rows], down[rows])


def ffn_pair(args):
    rows, width = args[0].shape
    units = args[2].shape[1] // 2
    return call(
        ffn_pair_kernel,
        [("v", shape((2, width, units)))],
        [("v", item) for item in args],
        8 * rows * width * units,
    )[0]


def ffn_own(where, args, got):
    rows, width = args[0].shape
    units = args[2].shape[1] // 2
    return call(
        ffn_own_kernel,
        [("v", shape((width // 2, units))), ("v", shape((width // 2, units), F32))] * 2,
        [("s", where)] + [("v", item) for item in (*args, got)],
        8 * rows * width * units,
    )


def attn_back_kernel(
    layer, turned, where_ref, dz_ref, q_ref, kv_ref, marks_ref, lse_ref, w_ref,
    dq_ref, dkv_ref, dkv_pair_ref, bias, do_ref,
):
    rows, width = q_ref.shape
    fill_bias(bias, turned, marks_ref)
    low = lanes_of(rows) < HEAD_DIM
    scale = HEAD_DIM**-0.5
    do_ref[...] = dot_nt(dz_ref[...], w_ref[0]).astype(BF16)
    for tile in range(width // PAIR):
        cols = slice(tile * PAIR, (tile + 1) * PAIR)
        vcols = slice(width + cols.start, width + cols.stop)
        q, do = q_ref[:, cols], do_ref[:, cols]
        dq, dk, dv = [], 0.0, 0.0
        for side in range(2):
            head = 2 * tile + side
            block = block_of(where_ref, layer, head, turned)
            part = low if side == 0 else ~low
            q_head = jnp.where(part, q, jnp.zeros_like(q))
            do_head = jnp.where(part, do, jnp.zeros_like(do))
            k = kv_ref[block, :, cols]
            s = dot_nt(q_head, k) * (scale * LOG2E) + bias[block]
            p = jnp.exp2(s - lse_ref[:, head : head + 1])
            dp = dot_nt(do_head, kv_ref[block, :, vcols])
            centre = jnp.sum(p * dp, axis=1, keepdims=True)
            ds = (p * (dp - centre)).astype(BF16)
            dq.append(dot(ds, k))
            dv += dot_tn(p.astype(BF16), do_head)
            dk += dot_tn(ds, q_head)
        dq_ref[:, cols] = (jnp.where(low, dq[0], dq[1]) * scale).astype(BF16)
        dkv_ref[:, cols] = dk[:rows] * scale
        dkv_ref[:, vcols] = dv[:rows]
        dkv_pair_ref[:, cols] = (dk[rows:] * scale).astype(BF16)
        dkv_pair_ref[:, vcols] = dv[rows:].astype(BF16)


def attn_back(layer, turned, where, dz, q, kv, marks, lse, w):
    rows, width = q.shape
    return call(
        partial(attn_back_kernel, layer, turned),
        [("v", shape((rows, width))), ("v", shape((rows, 2 * width), F32)), ("v", shape((rows, 2 * width)))],
        [("s", where)] + [("v", item) for item in (dz, q, kv, marks, lse, w)],
        20 * rows * rows * width,
        scratch=[pltpu.VMEM((2, rows, 2 * rows), F32), pltpu.VMEM((rows, width), BF16)],
    )


def row_grads_kernel(
    small_ref, dq0_ref, dq1_ref, kv0_ref, kv1_ref, pair0_ref, pair1_ref, w_ref, dx_ref, d0_ref, d1_ref
):
    width = dq0_ref.shape[1]
    turned = small_ref[TURNED : TURNED + 1, :] == 1.0
    near = kv0_ref[...] + pair0_ref[...].astype(F32)
    far = kv1_ref[...] + pair1_ref[...].astype(F32)
    d0_ref[:, :width] = dq0_ref[...]
    d1_ref[:, :width] = dq1_ref[...]
    d0_ref[:, width:] = jnp.where(turned, far, near).astype(BF16)
    d1_ref[:, width:] = jnp.where(turned, near, far).astype(BF16)
    total = None
    for k in range(3):
        part = dot(d1_ref[:, k * width : (k + 1) * width], w_ref[k])
        total = part if total is None else total + part
    dx_ref[...] = total.astype(BF16)


def row_grads(small, dq, kv, pair, w):
    rows, width = dq[0].shape
    return call(
        row_grads_kernel,
        [("v", shape((rows, w.shape[2])))] + [("v", shape((rows, 3 * width)))] * 2,
        [("v", item) for item in (small, *dq, *kv, *pair, w)],
        6 * rows * width * w.shape[2],
    )


def attn_grads_kernel(
    where_ref, d0_ref, d1_ref, x0_ref, x1_ref, o0_ref, o1_ref, dz0_ref, dz1_ref, w_ref,
    dx_ref, own_ref, pair_ref, db_ref,
):
    width = o0_ref.shape[1]
    first_core = where_ref[1] == 0
    share = width // 2
    db_ref[...] = jnp.zeros_like(db_ref)
    for k in range(4):
        cols = slice(k * width, (k + 1) * width)
        if k < 3:
            left, right = (d0_ref[:, cols], d1_ref[:, cols]), (x0_ref[...], x1_ref[...])
        else:
            left, right = (o0_ref[...], o1_ref[...]), (dz0_ref[...], dz1_ref[...])
        if k in (0, 2):
            sums = jnp.sum(left[0].astype(F32), axis=0, keepdims=True)
            sums += jnp.sum(left[1].astype(F32), axis=0, keepdims=True)
            db_ref[0:1, k // 2 * width : (k // 2 + 1) * width] = sums
        both = dot_tn(left[0], right[0]) + dot_tn(left[1], right[1])
        rows = slice(k * share, (k + 1) * share)
        own_ref[rows] = jnp.where(first_core, both[:share], both[share:])
        pair_ref[rows] = jnp.where(first_core, both[share:], both[:share]).astype(BF16)
    total = None
    for k in range(3):
        part = dot(d0_ref[:, k * width : (k + 1) * width], w_ref[k])
        total = part if total is None else total + part
    dx_ref[...] = total


def attn_grads(where, d, x, o, dz, w):
    rows, width = o[0].shape
    columns = x[0].shape[1]
    return call(
        attn_grads_kernel,
        [
            ("v", shape((rows, columns), F32)),
            ("v", shape((2 * width, columns), F32)),
            ("v", shape((2 * width, columns))),
            ("v", shape((8, 2 * width), F32)),
        ],
        [("s", where)] + [("v", item) for item in (*d, *x, *o, *dz, w)],
        22 * rows * width * columns,
    )


def split_kernel(where_ref, own_ref, got_ref, sent_ref, kept_ref):
    half = kept_ref.shape[0]
    first = where_ref[0] == 0
    top = own_ref[:half] + got_ref[:half].astype(F32)
    bottom = own_ref[half:] + got_ref[half:].astype(F32)
    kept_ref[...] = jnp.where(first, top, bottom)
    sent_ref[...] = jnp.where(first, bottom, top).astype(BF16)


def split(where, own, got):
    rows, columns = own.shape
    return call(
        split_kernel,
        [("v", shape((rows // 2, columns))), ("v", shape((rows // 2, columns), F32))],
        [("s", where), ("v", own), ("v", got)],
    )


def add_kernel(where_ref, kept_ref, got_ref, out_ref):
    out_ref[...] = (kept_ref[...] + got_ref[...].astype(F32)).astype(BF16)


def halve_sum_kernel(bit, parts, where_ref, *refs):
    kept, got, (sent_ref, own_ref) = refs[:parts], refs[parts : 2 * parts], refs[2 * parts :]
    mine = (where_ref[3] >> bit) & 1
    if parts == 2:
        for half in range(2):
            total = kept[half][...] + got[half][...].astype(F32)

            @pl.when(mine == half)
            def _():
                own_ref[...] = total

            @pl.when(mine != half)
            def _():
                sent_ref[...] = total.astype(BF16)

        return
    rows = own_ref.shape[0]
    at = pl.ds(pl.multiple_of(mine * rows, 16), rows)
    own_ref[...] = kept[0][at] + got[0][at].astype(F32)
    at = pl.ds(pl.multiple_of((1 - mine) * rows, 16), rows)
    sent_ref[...] = (kept[0][at] + got[0][at].astype(F32)).astype(BF16)


def join_kernel(bit, where_ref, own_ref, got_ref, out_ref):
    rows = own_ref.shape[0]
    mine = (where_ref[3] >> bit) & 1
    out_ref[pl.ds(pl.multiple_of(mine * rows, 16), rows)] = own_ref[...]
    out_ref[pl.ds(pl.multiple_of((1 - mine) * rows, 16), rows)] = got_ref[...]


def results_kernel(kind, where_ref, *refs):
    *pieces, first_ref, second_ref, buffer, sems = refs
    copies = Copies(sems)
    count = len(pieces) - 2
    rows = pieces[0].shape[0]
    first = where_ref[0] == 0
    for at in range(count):
        side, part = divmod(at, count // 2)
        other = pieces[count + side][part * rows : (part + 1) * rows]
        values = jnp.where(first, pieces[at][...], other).astype(F32)
        buffer[at * rows : (at + 1) * rows] = values
        if kind == "ffn":
            target = (first_ref, second_ref)[side].at[pl.ds(part * rows, rows)]
            copies.start(buffer.at[pl.ds(at * rows, rows)], target)
            continue
        local = rows // 2
        for k in (2 * at, 2 * at + 1):
            target = first_ref.at[k] if k < 3 else second_ref
            copies.start(buffer.at[pl.ds(k * local, local)], target)
    copies.done()


def results(kind, where, first, second):
    rows, columns = first[0].shape
    if kind == "attn":
        outs = [shape((3, rows // 2, columns), F32), shape((rows // 2, columns), F32)]
    else:
        outs = [shape((rows * len(first) // 2, columns), F32)] * 2
    return call(
        partial(results_kernel, kind),
        [("h", item) for item in outs],
        [("s", where)] + [("v", item) for item in (*first, *second)],
        scratch=[pltpu.VMEM((rows * len(first), columns), F32)],
        copies=4,
    )


def place_kernel(where_ref, first_ref, second_ref, first_got, second_got, out_ref, buffer, sems):
    copies = Copies(sems)
    first = where_ref[0] == 0
    buffer[0] = jnp.where(first, first_ref[...], second_got[...])
    buffer[1] = jnp.where(first, first_got[...], second_ref[...])
    copies.start(buffer, out_ref.at[0])
    copies.done()


def grad_in_kernel(where_ref, own_ref, far_ref, skip_ref, out_ref):
    out_ref[...] = (own_ref[...] + far_ref[...].astype(F32) + skip_ref[...]).astype(BF16)


def pack_sums_kernel(where_ref, *refs):
    own_ref, pair_ref = refs[-2:]
    for layer in range(2):
        norm1_ref, norm2_ref, up0_ref, up1_ref, qkv_ref = refs[5 * layer : 5 * layer + 5]
        at = 8 * layer
        for row, source in (
            (GAIN1, norm1_ref[0:1]),
            (GAIN2, norm2_ref[0:1]),
            (BIAS_OUT, norm1_ref[2:3]),
            (SHIFT1, norm1_ref[1:2]),
            (BIAS2, norm2_ref[2:3]),
            (SHIFT2, norm2_ref[1:2]),
            (7, qkv_ref[0:1]),
        ):
            own_ref[at + row : at + row + 1] = source
            pair_ref[at + row : at + row + 1] = source
        own_ref[at + 6 : at + 7] = up0_ref[0:1] + up1_ref[0:1]
        pair_ref[at + 6 : at + 7] = up0_ref[1:2] + up1_ref[1:2]


def small_add_kernel(where_ref, own_ref, got_ref, total_ref, shared_ref):
    total = own_ref[...] + got_ref[...]
    total_ref[...] = total
    row = lax.broadcasted_iota(jnp.int32, total.shape, 0)
    shared_ref[...] = jnp.where(row % 8 < BIAS_UP, total, 0.0)


def small_results_kernel(where_ref, own_ref, got_ref, *refs):
    outs, (gains, shifts, up, qkv_b), sems = refs[:4], refs[4:8], refs[8]
    total = own_ref[...] + got_ref[...]
    total = jnp.where(where_ref[0] == 0, total[:8], total[8:])
    gains[0] = total[0:2]
    shifts[0] = total[2:6]
    up[...] = total[6:7]
    local = qkv_b.shape[2]
    for k in range(2):
        both = total[7:8, 2 * k * local : 2 * (k + 1) * local]
        qkv_b[0, k : k + 1] = jnp.where(where_ref[1] == 0, both[:, :local], both[:, local:])
    copies = Copies(sems)
    for source, target in zip((gains, shifts, up, qkv_b), outs):
        copies.start(source, target)
    copies.done()


def swap(value, axis, bit):
    count = lax.axis_size(axis)
    return lax.ppermute(value, axis, [(source, source ^ bit) for source in range(count)])


def core_swap(value):
    return swap(value, "tensor", 1)


def chip_swap(value):
    return swap(value, "tensor", 2)


def tie(value, *after):
    return lax.optimization_barrier((value, *after))[0]


class Sum:
    def __init__(self, owner, *pieces):
        self.owner = owner
        self.kept = [kept for _, kept in pieces]
        self.got = [swap(sent, "pipe", 1) for sent, _ in pieces]
        count = lax.axis_size("dp")
        self.bits = count.bit_length() - 1
        self.halving = count == 1 << self.bits and self.kept[0].shape[0] % (16 * count) == 0

    def add(self, where):
        totals = [
            call(add_kernel, [("v", shape(kept.shape))], [("s", where), ("v", kept), ("v", got)])[0]
            for kept, got in zip(self.kept, self.got)
        ]
        self.total = totals[0] if len(totals) == 1 else jnp.concatenate(totals)
        return self.total

    def halve(self, bit, where):
        parts = len(self.kept)
        rows, columns = self.kept[0].shape
        dims = (rows * parts // 2, columns)
        sent, kept = call(
            partial(halve_sum_kernel, bit, parts),
            [("v", shape(dims)), ("v", shape(dims, F32))],
            [("s", where)] + [("v", item) for item in (*self.kept, *self.got)],
        )
        self.kept, self.got = [kept], [swap(sent, "dp", 1 << bit)]
        return sent

    def join(self, bit, where):
        rows, columns = self.total.shape
        got = swap(self.total, "dp", 1 << bit)
        (self.total,) = call(
            partial(join_kernel, bit),
            [("v", shape((2 * rows, columns)))],
            [("s", where), ("v", self.total), ("v", got)],
        )
        return self.total

    def steps(self):
        if not self.halving:

            def whole(where):
                self.add(where)
                self.total = lax.psum(self.total, "dp")
                return self.total

            return [whole]
        bits = range(self.bits)
        return (
            [partial(self.halve, bit) for bit in bits]
            + [self.add]
            + [partial(self.join, bit) for bit in reversed(bits)]
        )

    def finish(self, *after):
        self.other = lax.ppermute(
            tie(self.total, *after) if after else self.total, "pipe", [(1 - self.owner, self.owner)]
        )


def layer_forward(layer, own_in, far_in, w_qkv, small, marks, where, hooks):
    own_q, own_kv, own_x_kept, own_q_kept = qkv(own_in, w_qkv, small)
    own_pair = core_swap(own_kv)
    far_q, far_kv, far_x_kept, far_q_kept = qkv(far_in, w_qkv, small)
    far_pair = core_swap(far_kv)
    w_out = hooks["out"](far_q)
    far_out, kv, kv_kept, far_o, far_lse = attn(
        layer, where, far_q, (own_kv, own_pair, far_kv, far_pair), marks, w_out
    )
    far_out = chip_swap(far_out)
    own_out, own_o, own_lse = attn(layer, where, own_q, (kv,), marks, w_out)
    w_up, w_down = hooks["ffn"](own_out)
    own_out = tie(own_out, w_up)
    own_h, hidden, resid1, own_h_kept = norm1(own_in, own_out, far_out, small)
    far_h = chip_swap(own_h)
    own_branch, own_act, own_slope = ffn(own_h, w_up, w_down, small, False)
    far_h = tie(far_h, own_branch)
    far_branch, far_act, far_slope, far_h_kept = ffn(far_h, w_up, w_down, small, True)
    own_branch = tie(own_branch, *hooks["next"](far_branch))
    output, resid2, output_kept = norm2(hidden, own_branch, chip_swap(far_branch), small)
    kept = dict(
        x=(own_x_kept, far_x_kept),
        q=(own_q_kept, far_q_kept),
        kv=kv_kept,
        lse=(own_lse, far_lse),
        o=(own_o, far_o),
        resid=(resid1, resid2),
        h=(own_h_kept, far_h_kept),
        act=(own_act, far_act),
        slope=(own_slope, far_slope),
    )
    return output, output_kept, kept


def layer_backward(layer, upstream, kept, small, marks, where, loads, hooks):
    own_df, skip2, norm2_sums, *grad_in = norm2_back(upstream, kept["resid"][1], small)
    far_df = chip_swap(own_df)
    w_up, w_down, own_slope, far_slope = loads["ffn"](kept["slope"], own_df)
    own_dh, own_du, own_db = ffn_back(own_df, own_slope, w_up, w_down, False)
    far_df = tie(far_df, own_dh, *hooks["df"](own_dh))
    far_dh, far_du, far_db = ffn_back(far_df, far_slope, w_up, w_down, True)
    own_act, far_act, own_h, far_h = loads["rows"]((*kept["act"], *kept["h"]), far_dh)
    grads = (own_h, far_h, own_act, far_act, own_df, far_df, own_du, far_du)
    pair = ffn_pair(grads)
    own_dh = tie(own_dh, *hooks["dh"](pair))
    parts = ffn_own(where, grads, core_swap(pair))
    own_dh = tie(own_dh, parts[0])
    own_dz, skip1, norm1_sums = norm1_back(own_dh, chip_swap(far_dh), skip2, kept["resid"][0], small)
    far_dz = chip_swap(own_dz)
    w_out, kv, own_q, far_q, own_lse, far_lse = loads["out"](
        (kept["kv"], *kept["q"], *kept["lse"]), own_dz
    )
    own_dq, own_dkv, own_send = attn_back(layer, 0, where, own_dz, own_q, kv, marks, own_lse, w_out)
    own_pair = core_swap(own_send)
    w_qkv, own_x, far_x, own_o, far_o = loads["qkv"]((*kept["x"], *kept["o"]), own_send)
    far_dz = tie(far_dz, w_qkv, *hooks["dz"](own_send, parts))
    far_dq, far_dkv, far_send = attn_back(layer, 1, where, far_dz, far_q, kv, marks, far_lse, w_out)
    far_pair = core_swap(far_send)
    far_dx, own_d, far_d = row_grads(
        small, (own_dq, far_dq), (own_dkv, far_dkv), (own_pair, far_pair), w_qkv
    )
    far_dx = chip_swap(far_dx)
    own_dx, attn_own, attn_pair, qkv_sums = attn_grads(
        where, (own_d, far_d), (own_x, far_x), (own_o, far_o), (own_dz, far_dz), w_qkv
    )
    sums = (norm1_sums, norm2_sums, own_db, far_db, qkv_sums)
    return (own_dx, far_dx, skip1), grad_in, sums, (attn_own, core_swap(attn_pair)), parts


def body(
    tokens,
    segment_ids,
    pad_mask,
    block_perm,
    qkv_weight,
    qkv_bias,
    out_weight,
    up_weight,
    up_bias,
    down_weight,
    norm_gain,
    shift_bias,
    cotangent,
):
    section = lax.axis_index("pipe")
    place = lax.axis_index("tensor")
    replica = lax.axis_index("dp")
    paired = lax.axis_size("dp") % 2 == 0
    width = tokens.shape[2]
    local = qkv_bias.shape[2]
    here = jnp.stack([section, place % 2, replica % 2, replica, place]).astype(jnp.int32)
    qkv_rows = jnp.transpose(qkv_weight[0], (0, 2, 1))

    def other_half(half, whole):
        if paired:
            return swap(half, "dp", 1)
        even = replica % 2 == 0
        rest = jnp.where(even, whole[..., width // 2 :], whole[..., : width // 2])
        return swap(rest, "pipe", 1)

    qkv_half, out_half = halves_of(here, qkv_rows, out_weight)
    qkv_x = swap(qkv_half, "pipe", 1)
    rows = lax.optimization_barrier(lax.dynamic_index_in_dim(tokens, section, 0, keepdims=False))
    far_rows = chip_swap(rows)
    (own_small,) = call(
        pack_kernel,
        [("v", shape((16, width), F32))],
        [("h", norm_gain), ("h", shift_bias), ("h", up_bias), ("h", qkv_bias), ("s", block_perm)],
        scratch=[
            pltpu.VMEM(item.shape, item.dtype) for item in (norm_gain, shift_bias, up_bias, qkv_bias)
        ],
        copies=4,
    )
    other_small = swap(own_small, "pipe", 1)
    out_x = swap(tie(out_half, qkv_x), "pipe", 1)
    up_half, down_half = halves_of(tie(here, own_small), up_weight, down_weight)
    up_x = swap(tie(up_half, out_x, other_small), "pipe", 1)
    *smalls, flags = call(
        params_kernel,
        [("v", shape((16, width), F32))] * 2 + [("h", shape((8, PAIR), F32))],
        [("s", here)]
        + [
            ("v", item)
            for item in (own_small, other_small, core_swap(own_small), core_swap(other_small))
        ],
        scratch=[pltpu.VMEM((8, PAIR), F32)],
        copies=1,
    )
    heads = 2 * block_perm.shape[1]
    where = jnp.concatenate([here, flags[:2, :heads].reshape(-1).astype(jnp.int32)])
    (marks,) = call(
        marks_kernel,
        [("v", shape((8, segment_ids.shape[1] // 2), jnp.int32))],
        [("s", here), ("v", segment_ids), ("v", pad_mask)],
    )

    def item(by_core, own, other):
        return by_core, own, other, core_swap(own), tuple(core_swap(part) for part in other)

    items = dict(
        qkv=item(True, qkv_rows, (qkv_x, other_half(qkv_x, qkv_rows))),
        out=item(True, out_weight, (out_x, other_half(out_x, out_weight))),
    )
    ready = tie(where, far_rows, marks, *smalls)
    (first_qkv,) = load(0, ready, [items["qkv"]])

    fetched = {}

    def first_ffn(after):
        down_x = fetched["down"]
        items["up"] = item(False, up_weight, (up_x, fetched["up"]))
        items["down"] = item(False, down_weight, (down_x, other_half(down_x, down_weight)))
        return load_ffn(0, (), after)

    def first_out(after):
        fetched["down"] = swap(tie(down_half, up_x), "pipe", 1)
        fetched["up"] = other_half(up_x, up_weight)
        return load(0, tie(where, after, up_x), [items["out"]])[0]

    def load_ffn(layer, arrays, after):
        return load(layer, tie(where, after), [items["up"], items["down"]], arrays)

    def load_one(layer, name, arrays, after):
        return load(layer, tie(where, after), [items[name]], arrays)

    def load_rows(arrays, after):
        return load(0, tie(where, after), [], arrays)

    second = []

    def load_second(after):
        second.extend(load(1, tie(where, after), [items["qkv"], items["out"]]))
        return second

    out_first, first_kept, kept_first = layer_forward(
        0,
        rows,
        far_rows,
        first_qkv,
        smalls[0],
        marks,
        where,
        {"out": first_out, "ffn": first_ffn, "next": load_second},
    )
    def second_ffn(after):
        fetched["first"] = lax.ppermute(first_kept, "pipe", [(1, 0)])
        return load_ffn(1, (), tie(after, fetched["first"]))

    out_second, second_kept, kept_second = layer_forward(
        1,
        out_first,
        chip_swap(out_first),
        second[0],
        smalls[1],
        marks,
        where,
        {
            "out": lambda after: second[1],
            "ffn": second_ffn,
            "next": lambda after: (),
        },
    )

    def loads(layer):
        return {
            "out": partial(load_one, layer, "out"),
            "qkv": partial(load_one, layer, "qkv"),
            "ffn": partial(load_ffn, layer),
            "rows": load_rows,
        }

    def place_outputs(first, second, first_got, second_got, after):
        return call(
            place_kernel,
            [("h", shape((1, 2) + first.shape))],
            [("s", after)] + [("v", value) for value in (first, second, first_got, second_got)],
            scratch=[pltpu.VMEM((2,) + first.shape, BF16)],
            copies=1,
        )[0]

    sums, steps = {}, {}

    def begin(name, owner, *pieces):
        sums[name] = Sum(owner, *pieces)
        steps[name] = sums[name].steps()

    def run(name, after):
        return steps[name].pop(0)(tie(where, after)) if steps[name] else after

    upstream = lax.dynamic_index_in_dim(cotangent, section, 0, keepdims=False)
    outputs = []

    def later_df(after):
        second_got = lax.ppermute(second_kept, "pipe", [(0, 1)])
        outputs.append(
            place_outputs(first_kept, second_kept, fetched["first"], second_got, tie(where, after))
        )
        return (outputs[0],)

    def later_dz(after, parts):
        begin("ab1", 1, parts[0:2], parts[2:4])
        return (sums["ab1"].got[0],)

    grads, _, small_second, attn_second, _ = layer_backward(
        1,
        (upstream,),
        kept_second,
        smalls[1],
        marks,
        where,
        loads(1),
        {"df": later_df, "dh": lambda after: (), "dz": later_dz},
    )
    sent, kept = split(where, *attn_second)
    begin("c1", 1, (sent, kept))
    grads = (tie(grads[0], run("ab1", sent)),) + grads[1:]

    def first_df(after):
        one = run("ab1", after)
        return (run("c1", one),)

    def first_dh(after):
        one = run("ab1", after)
        return (run("c1", one),)

    def first_dz(after, parts):
        begin("a0", 0, parts[0:2])
        begin("b0", 0, parts[2:4])
        one = run("ab1", after)
        one = run("c1", one)
        return (run("a0", one),)

    grads, (grad_second,), small_first, attn_first, _ = layer_backward(
        0,
        grads,
        kept_first,
        smalls[0],
        marks,
        where,
        loads(0),
        {"df": first_df, "dh": first_dh, "dz": first_dz},
    )
    order = [attn_first[0]]

    def now():
        return tie(where, order[-1])

    def step(*names):
        for name in names:
            order.append(run(name, order[-1]))

    def small_add(total, got):
        total, shared = call(
            small_add_kernel,
            [("v", shape((16, width), F32))] * 2,
            [("s", now()), ("v", total), ("v", got)],
        )
        order.append(total)
        return total, shared

    sent, kept = split(now(), *attn_first)
    order.append(sent)
    begin("c0", 0, (sent, kept))
    total, pair_sums = call(
        pack_sums_kernel,
        [("v", shape((16, width), F32))] * 2,
        [("s", now())] + [("v", value) for value in (*small_first, *small_second)],
    )
    order.append(total)
    got = core_swap(pair_sums)
    step("a0", "c1", "b0")
    total, shared = small_add(total, got)
    got = chip_swap(shared)
    step("ab1")
    sums["ab1"].finish()
    (grad_first,) = call(
        grad_in_kernel, [("v", shape(rows.shape))], [("s", now())] + [("v", value) for value in grads]
    )
    order.append(grad_first)
    first_got = lax.ppermute(grad_first, "pipe", [(1, 0)])
    second_got = lax.ppermute(grad_second, "pipe", [(0, 1)])
    total, _ = small_add(total, got)
    hops = [("pipe", 1)]
    count = lax.axis_size("dp")
    if count & (count - 1):
        total = lax.psum(total, "dp")
    else:
        hops += [("dp", 1 << bit) for bit in range(count.bit_length() - 1)]
    got = swap(total, *hops[0])
    step("a0", "b0")
    for hop in hops[1:]:
        total, _ = small_add(total, got)
        got = swap(total, *hop)
        step("c0", "a0", "b0")
    while steps["c1"]:
        step("c1")
    sums["c1"].finish()
    for name in ("a0", "b0"):
        while steps[name]:
            step(name, "c0")
        sums[name].finish()
    while steps["c0"]:
        step("c0")
    sums["c0"].finish()
    outs = [shape(item.shape, F32) for item in (norm_gain, shift_bias, up_bias, qkv_bias)]
    gains, shifts, upb, qkvb = call(
        small_results_kernel,
        [("h", item) for item in outs],
        [("s", now()), ("v", total), ("v", got)],
        scratch=[pltpu.VMEM(item.shape, F32) for item in outs],
        copies=4,
    )
    layer_out = outputs[0]
    input_grad = place_outputs(grad_first, grad_second, first_got, second_got, tie(where, gains))

    def pieces(second, *names):
        first = [sums[name].total for name in names] + [sums[name].other for name in names]
        return first, [sums[second].other, sums[second].total]

    upw, downw = results("ffn", tie(where, input_grad), *pieces("ab1", "a0", "b0"))
    qkvw, outw = results("attn", tie(where, upw), *pieces("c1", "c0"))
    qkvw = jnp.transpose(qkvw, (0, 2, 1))
    return (
        layer_out,
        input_grad,
        qkvw[None],
        qkvb,
        outw[None],
        upw[None],
        upb,
        downw[None],
        gains,
        shifts,
    )


def solution(mesh):
    return jax.shard_map(
        body,
        mesh=mesh,
        in_specs=(
            P("dp", "tensor", None),
            P("dp", None),
            P("dp", None),
            P("pipe", "tensor", None),
            P("pipe", None, None, "tensor"),
            P("pipe", None, "tensor"),
            P("pipe", "tensor", None),
            P("pipe", None, "tensor"),
            P("pipe", "tensor"),
            P("pipe", "tensor", None),
            P("pipe", None, None),
            P("pipe", None, None),
            P("dp", "tensor", None),
        ),
        out_specs=(
            P("pipe", "dp", "tensor", None),
            P("pipe", "dp", "tensor", None),
            P("pipe", None, None, "tensor"),
            P("pipe", None, "tensor"),
            P("pipe", "tensor", None),
            P("pipe", None, "tensor"),
            P("pipe", "tensor"),
            P("pipe", "tensor", None),
            P("pipe", None, None),
            P("pipe", None, None),
        ),
        check_vma=False,
    )
```

time: 707 us -> 480 us (0.68)
  waiting for transfers between devices: 441 us -> 210 us
  Pallas kernels: 0 us -> 160 us
  matrix products: 103 us -> 0 us
  other arithmetic: 49.6 us -> 0.69 us
  starting transfers between devices: 56.8 us -> 93.5 us
  local copies, waits for them, and re-layouts: 32.8 us -> 3.92 us
  between operations: 16.9 us -> 2.13 us
    psum x1 -> x0, waiting for transfers between devices: 202 us -> none  [over_parts(): return lax.psum((grad + received.astype(F32)).astype(BF16), 'dp')]
    pallas_call x0 -> x92, Pallas kernels: none -> 160 us  [call(): pl.pallas_call(kernel, out_shape=[PLACES[space](item.shape, item.dtype) f...]
    dot_general x48 -> x0, matrix products: 103 us -> none  [the longest x12 35.6 us: dot(): return jnp.dot(left, right, preferred_element_type=F32)]
    ppermute x69 -> x82, starting transfers between devices: 40.3 us -> 72.8 us  [swap(): lax.ppermute(value, axis, [(source, source ^ bit) for source in range(cou...]
    convert_element_type x30 -> x1, other arithmetic: 21.8 us -> 0.69 us  [body(): flags[:2, :heads].reshape(-1).astype(jnp.int32)]
    ppermute x69 -> x82, waiting for transfers between devices: 194 us -> 177 us  [swap(): lax.ppermute(value, axis, [(source, source ^ bit) for source in range(cou...]
    ppermute x8 -> x9, waiting for transfers between devices: 45.8 us -> 33.1 us  [the longest x5 21.1 us: finish(): lax.ppermute(tie(self.total, *after) if after else self.total, 'pipe', [(...]
    reduce_sum x19 -> x0, other arithmetic: 12.1 us -> none  [the longest x2 4.24 us: attention_forward(): total = jnp.exp(-ceiling) + jnp.sum(weights, axis=-1, keepdims=True)]
  transfers between devices with their start and end apart: 78 -> 91, of which waited for: 41 -> 47; matrix products, arithmetic and copies ran while one was open for 17% -> 0% of each run, Pallas kernels for 0% -> 26%
where the time goes in v2:
time: 480 us; the launch traced here: 471 us
  waiting for transfers between devices  210 us (44%)
  Pallas kernels  160 us (33%)
  starting transfers between devices  93.5 us (19%)
    ppermute x82, waiting for transfers between devices, swap(): lax.ppermute(value, axis, [(source, source ^ bit) for source in range(cou...  177 us
    pallas_call x92, Pallas kernels, call(): pl.pallas_call(kernel, out_shape=[PLACES[space](item.shape, item.dtype) f...  160 us
    ppermute x82, starting transfers between devices, swap(): lax.ppermute(value, axis, [(source, source ^ bit) for source in range(cou...  72.8 us
    ppermute x5, waiting for transfers between devices, finish(): lax.ppermute(tie(self.total, *after) if after else self.total, 'pipe', [(...  21.1 us
    ppermute x5, starting transfers between devices, finish(): lax.ppermute(tie(self.total, *after) if after else self.total, 'pipe', [(...  12.1 us
    ppermute x1, waiting for transfers between devices, body(): second_got = lax.ppermute(grad_second, 'pipe', [(0, 1)])  12.1 us
  transfers between devices with their start and end apart: 91, of which 47 were waited for; matrix products, arithmetic and copies ran while one was open for 0% of the time, Pallas kernels for 26%

profile of v2, /device:TPU:0, one launch (start us, length us, event | category | flops | bytes accessed | tf_op | source)
XLA Modules:
  0.0 470.7 jit_solution(2516292160216349215)
XLA Ops:
  2.4 3.0 collective-permute-start.4
  5.4 10.2 %collective-permute-done.4.refs_1_ = bf16[3,192,384]{2,1,0:T(8,128)(2,1)S(1)} collective-permute-done((bf16[3,192,384]{2,1,0:T(8,128)(2,1)S(1)}, bf16[3,192,384]{2,1,0:T(8,128)(2,1)S(1)}, u32[]{:S(2)}, u32[]{:S(2)}) %collective-permute-start.4) | collective-permute-done | bytes 442400 | tf_op jit(solution)/shard_map/ppermute | solution.py:877
  30.0 4.1 collective-permute-done.3.x_ref
  37.2 6.8 %collective-permute-done.13.refs_2_.refs_8_ = bf16[1,192,384]{2,1,0:T(8,128)(2,1)} collective-permute-done((bf16[1,192,384]{2,1,0:T(8,128)(2,1)S(1)}, bf16[1,192,384]{2,1,0:T(8,128)(2,1)}, u32[]{:S(2)}, u32[]{:S(2)}) %collective-permute-start.13) | collective-permute-done | bytes 147488 | tf_op jit(solution)/shard_map/ppermute | solution.py:877
  49.6 9.3 %collective-permute-done.21.refs_7_ = bf16[1,768,384]{2,1,0:T(8,128)(2,1)} collective-permute-done((bf16[1,768,384]{2,1,0:T(8,128)(2,1)S(1)}, bf16[1,768,384]{2,1,0:T(8,128)(2,1)}, u32[]{:S(2)}, u32[]{:S(2)}) %collective-permute-start.21) | collective-permute-done | bytes 589856 | tf_op jit(solution)/shard_map/ppermute | solution.py:877
  68.6 8.1 %collective-permute-done.22.refs_8_ = bf16[1,768,384]{2,1,0:T(8,128)(2,1)} collective-permute-done((bf16[1,768,384]{2,1,0:T(8,128)(2,1)}, bf16[1,768,384]{2,1,0:T(8,128)(2,1)}, u32[]{:S(2)}, u32[]{:S(2)}) %collective-permute-start.22) | collective-permute-done | bytes 589856 | tf_op jit(solution)/shard_map/ppermute | solution.py:877
  78.4 4.9 %shard_map.213 = (bf16[256,768]{1,0:T(8,128)(2,1)S(1)}, bf16[2,512,768]{2,1,0:T(8,128)(2,1)S(1)}, bf16[2,512,768]{2,1,0:T(8,128)(2,1)}, bf16[256,384]{1,0:T(8,128)(2,1)}, f32[256,128]{1,0:T(8,128)}) custom-call(s32[17]{0:T(128)S(1)} %concatenate.4.where_ref, bf16[256,384]{1,0:T(8,128)(2,1)S(1)} %get-tuple-element.289.q_ref, ...), custom_call_target="tpu_custom_call" | custom-call | flops 352321536 | tf_op jit(solution)/shard_map/pallas_call | solution.py:33
  83.9 4.3 shard_map.214
  96.7 3.4 shard_map.217
  100.1 6.7 %collective-permute-done.27.h_ref = bf16[256,768]{1,0:T(8,128)(2,1)S(1)} collective-permute-done((bf16[256,768]{1,0:T(8,128)(2,1)S(1)}, bf16[256,768]{1,0:T(8,128)(2,1)S(1)}, u32[]{:S(2)}, u32[]{:S(2)}) %collective-permute-start.27) | collective-permute-done | bytes 393248 | tf_op jit(solution)/shard_map/ppermute | solution.py:877
  106.9 3.6 shard_map.218
  113.5 6.9 %collective-permute-done.28.far_ref = bf16[256,768]{1,0:T(8,128)(2,1)S(1)} collective-permute-done((bf16[256,768]{1,0:T(8,128)(2,1)S(1)}, bf16[256,768]{1,0:T(8,128)(2,1)S(1)}, u32[]{:S(2)}, u32[]{:S(2)}) %collective-permute-start.28) | collective-permute-done | bytes 393248 | tf_op jit(solution)/shard_map/ppermute | solution.py:877
  123.3 7.2 %collective-permute-done.29.x_ref = bf16[256,768]{1,0:T(8,128)(2,1)S(1)} collective-permute-done((bf16[256,768]{1,0:T(8,128)(2,1)S(1)}, bf16[256,768]{1,0:T(8,128)(2,1)S(1)}, u32[]{:S(2)}, u32[]{:S(2)}) %collective-permute-start.29) | collective-permute-done | bytes 393248 | tf_op jit(solution)/shard_map/ppermute | solution.py:877
  133.4 4.8 %shard_map.223 = (bf16[256,768]{1,0:T(8,128)(2,1)S(1)}, bf16[2,512,768]{2,1,0:T(8,128)(2,1)S(1)}, bf16[2,512,768]{2,1,0:T(8,128)(2,1)}, bf16[256,384]{1,0:T(8,128)(2,1)}, f32[256,128]{1,0:T(8,128)}) custom-call(s32[17]{0:T(128)S(1)} %concatenate.4.where_ref, bf16[256,384]{1,0:T(8,128)(2,1)S(1)} %get-tuple-element.318.q_ref, ...), custom_call_target="tpu_custom_call" | custom-call | flops 352321536 | tf_op jit(solution)/shard_map/pallas_call | solution.py:33
  138.9 2.9 shard_map.225
  141.9 4.3 shard_map.224
  146.1 3.3 collective-permute-done.32.far_ref
  151.4 3.6 shard_map.227
  155.0 6.1 %collective-permute-done.33.h_ref = bf16[256,768]{1,0:T(8,128)(2,1)S(1)} collective-permute-done((bf16[256,768]{1,0:T(8,128)(2,1)S(1)}, bf16[256,768]{1,0:T(8,128)(2,1)S(1)}, u32[]{:S(2)}, u32[]{:S(2)}) %collective-permute-start.33) | collective-permute-done | bytes 393248 | tf_op jit(solution)/shard_map/ppermute | solution.py:877
  161.1 3.1 shard_map.228
  166.2 7.5 %collective-permute-done.34.far_ref = bf16[256,768]{1,0:T(8,128)(2,1)S(1)} collective-permute-done((bf16[256,768]{1,0:T(8,128)(2,1)S(1)}, bf16[256,768]{1,0:T(8,128)(2,1)S(1)}, u32[]{:S(2)}, u32[]{:S(2)}) %collective-permute-start.34) | collective-permute-done | bytes 393248 | tf_op jit(solution)/shard_map/ppermute | solution.py:877
  180.5 3.4 shard_map.231
  194.5 3.9 collective-permute-done.38.got_ref
  200.8 4.5 collective-permute-done.39.far_ref
  210.2 4.3 shard_map.240
  217.8 4.8 %shard_map.242 = (bf16[256,384]{1,0:T(8,128)(2,1)S(1)}, f32[256,768]{1,0:T(8,128)S(1)}, bf16[256,768]{1,0:T(8,128)(2,1)S(1)}) custom-call(s32[17]{0:T(128)S(1)} %concatenate.4.where_ref, bf16[256,768]{1,0:T(8,128)(2,1)S(1)} %collective-permute-done.40.dz_ref.dz1_ref, bf16[256,384]{1,0:T(8,128)(2,1)S(1)} %get-tuple-element.382.q_ref, ...), custom_call_target="tpu_custom_call" | custom-call | flops 503316480 | tf_op jit(solution)/shard_map/pallas_call | solution.py:33
  231.8 12.0 %collective-permute-done.45.refs_3_ = bf16[384,768]{1,0:T(8,128)(2,1)S(1)} collective-permute-done((bf16[384,768]{1,0:T(8,128)(2,1)S(1)}, bf16[384,768]{1,0:T(8,128)(2,1)S(1)}, u32[]{:S(2)}, u32[]{:S(2)}) %collective-permute-start.45) | collective-permute-done | bytes 589856 | tf_op jit(solution)/shard_map/ppermute | solution.py:877
  249.4 3.4 shard_map.248
  254.6 5.0 %collective-permute-done.48.refs_1_ = bf16[384,768]{1,0:T(8,128)(2,1)S(1)} collective-permute-done((bf16[384,768]{1,0:T(8,128)(2,1)S(1)}, bf16[384,768]{1,0:T(8,128)(2,1)S(1)}, u32[]{:S(2)}, u32[]{:S(2)}) %collective-permute-start.48) | collective-permute-done | bytes 589856 | tf_op jit(solution)/shard_map/ppermute | solution.py:877
  274.3 7.4 %collective-permute-done.50.got_ref = bf16[192,768]{1,0:T(8,128)(2,1)S(1)} collective-permute-done((bf16[192,768]{1,0:T(8,128)(2,1)S(1)}, bf16[192,768]{1,0:T(8,128)(2,1)S(1)}, u32[]{:S(2)}, u32[]{:S(2)}) %collective-permute-start.50) | collective-permute-done | bytes 294944 | tf_op jit(solution)/shard_map/ppermute | solution.py:877
  292.4 4.3 shard_map.260
  296.8 10.1 %collective-permute-done.55.got_ref = bf16[192,768]{1,0:T(8,128)(2,1)S(1)} collective-permute-done((bf16[192,768]{1,0:T(8,128)(2,1)S(1)}, bf16[192,768]{1,0:T(8,128)(2,1)S(1)}, u32[]{:S(2)}, u32[]{:S(2)}) %collective-permute-start.55) | collective-permute-done | bytes 294944 | tf_op jit(solution)/shard_map/ppermute | solution.py:877
  312.3 4.5 shard_map.265
  323.5 3.4 collective-permute-start.62
  329.4 10.9 %collective-permute-done.62.got_ref = bf16[96,768]{1,0:T(8,128)(2,1)S(1)} collective-permute-done((bf16[96,768]{1,0:T(8,128)(2,1)S(1)}, bf16[96,768]{1,0:T(8,128)(2,1)S(1)}, u32[]{:S(2)}, u32[]{:S(2)}) %collective-permute-start.62) | collective-permute-done | bytes 147488 | tf_op jit(solution)/shard_map/ppermute | solution.py:877
  341.6 6.1 %collective-permute-done.61.refs_1_ = bf16[192,768]{1,0:T(8,128)(2,1)S(1)} collective-permute-done((bf16[192,768]{1,0:T(8,128)(2,1)S(1)}, bf16[192,768]{1,0:T(8,128)(2,1)S(1)}, u32[]{:S(2)}, u32[]{:S(2)}) %collective-permute-start.61) | collective-permute-done | bytes 294944 | tf_op jit(solution)/shard_map/ppermute | solution.py:877
  350.2 3.4 collective-permute-start.68
  360.9 3.4 collective-permute-start.72
  375.6 10.1 %collective-permute-done.73.got_ref = bf16[96,768]{1,0:T(8,128)(2,1)S(1)} collective-permute-done((bf16[96,768]{1,0:T(8,128)(2,1)S(1)}, bf16[96,768]{1,0:T(8,128)(2,1)S(1)}, u32[]{:S(2)}, u32[]{:S(2)}) %collective-permute-start.73) | collective-permute-done | bytes 147488 | tf_op jit(solution)/shard_map/ppermute | solution.py:877
  386.2 3.4 collective-permute-start.77
  401.0 3.6 collective-permute-start.88
  405.2 3.3 collective-permute-done.79.got_ref
  411.2 3.5 collective-permute-start.85
  420.5 12.1 %collective-permute-done.85.second_got = bf16[256,768]{1,0:T(8,128)(2,1)S(1)} collective-permute-done((bf16[256,768]{1,0:T(8,128)(2,1)S(1)}, bf16[256,768]{1,0:T(8,128)(2,1)S(1)}, u32[]{:S(2)}, u32[]{:S(2)}) %collective-permute-start.85) | collective-permute-done | bytes 393248 | tf_op jit(solution)/shard_map/ppermute | solution.py:1273
  435.8 4.7 collective-permute-start.90
  444.5 6.2 %collective-permute-done.86.refs_2_ = bf16[384,768]{1,0:T(8,128)(2,1)S(1)} collective-permute-done((bf16[384,768]{1,0:T(8,128)(2,1)S(1)}, bf16[384,768]{1,0:T(8,128)(2,1)S(1)}, u32[]{:S(2)}, u32[]{:S(2)}) %collective-permute-start.86) | collective-permute-done | bytes 589856 | tf_op jit(solution)/shard_map/ppermute | solution.py:948
  450.7 11.4 %collective-permute-done.87.refs_3_ = bf16[384,768]{1,0:T(8,128)(2,1)S(1)} collective-permute-done((bf16[384,768]{1,0:T(8,128)(2,1)S(1)}, bf16[384,768]{1,0:T(8,128)(2,1)S(1)}, u32[]{:S(2)}, u32[]{:S(2)}) %collective-permute-start.87) | collective-permute-done | bytes 589856 | tf_op jit(solution)/shard_map/ppermute | solution.py:948
  465.0 3.5 collective-permute-done.89.refs_1_
  (283 shorter events, 197.9 us)
Async XLA Ops:
  2.4 13.2 %collective-permute-start.4 = (bf16[3,192,384]{2,1,0:T(8,128)(2,1)S(1)}, bf16[3,192,384]{2,1,0:T(8,128)(2,1)S(1)}, u32[]{:S(2)}, u32[]{:S(2)}) collective-permute-start(bf16[3,192,384]{2,1,0:T(8,128)(2,1)S(1)} %get-tuple-element.287), channel_id=1, source_target_pairs={{0,16},{16,0},{1,17},{17,1},{2,18},{18,2},{3,19},{19,3},{4,20},{20... | collective-permute-start | bytes 1327112 | tf_op jit(solution)/shard_map/ppermute | solution.py:877
  24.3 12.9 %collective-permute-start.12 = (bf16[1,768,384]{2,1,0:T(8,128)(2,1)S(1)}, bf16[1,768,384]{2,1,0:T(8,128)(2,1)}, u32[]{:S(2)}, u32[]{:S(2)}) collective-permute-start(bf16[1,768,384]{2,1,0:T(8,128)(2,1)S(1)} %get-tuple-element.296), channel_id=1, source_target_pairs={{0,16},{16,0},{1,17},{17,1},{2,18},{18,2},{3,19},{19,3},{4,20},{20... | collective-permute-start | bytes 1769480 | tf_op jit(solution)/shard_map/ppermute | solution.py:877
  28.1 19.7 %collective-permute-start.6 = (bf16[3,192,768]{2,1,0:T(8,128)(2,1)S(1)}, bf16[3,192,768]{2,1,0:T(8,128)(2,1)S(1)}, u32[]{:S(2)}, u32[]{:S(2)}) collective-permute-start(bf16[3,192,768]{2,1,0:T(8,128)(2,1)S(1)} %bitcast.23), channel_id=1, source_target_pairs={{0,4},{4,0},{8,12},{12,8},{1,5},{5,1},{9,13},{13,9},{2,6},{6,2},{1... | collective-permute-start | bytes 2654216 | tf_op jit(solution)/shard_map/ppermute | solution.py:877
  28.3 17.2 %collective-permute-start.5 = (bf16[3,192,384]{2,1,0:T(8,128)(2,1)S(1)}, bf16[3,192,384]{2,1,0:T(8,128)(2,1)S(1)}, u32[]{:S(2)}, u32[]{:S(2)}) collective-permute-start(bf16[3,192,384]{2,1,0:T(8,128)(2,1)S(1)} %copy-done.16), channel_id=1, source_target_pairs={{0,1},{1,0},{2,3},{3,2},{4,5},{5,4},{6,7},{7,6},{8,9},{9,8},{10,11... | collective-permute-start | bytes 1327112 | tf_op jit(solution)/shard_map/ppermute | solution.py:877
  34.1 31.8 %collective-permute-start.18 = (bf16[1,768,768]{2,1,0:T(8,128)(2,1)S(1)}, bf16[1,768,768]{2,1,0:T(8,128)(2,1)}, u32[]{:S(2)}, u32[]{:S(2)}) collective-permute-start(bf16[1,768,768]{2,1,0:T(8,128)(2,1)S(1)} %copy-done.6), channel_id=1, source_target_pairs={{0,4},{4,0},{8,12},{12,8},{1,5},{5,1},{9,13},{13,9},{2,6},{6,2},{1... | collective-permute-start | bytes 3538952 | tf_op jit(solution)/shard_map/ppermute | solution.py:877
  44.0 14.9 %collective-permute-start.21 = (bf16[1,768,384]{2,1,0:T(8,128)(2,1)S(1)}, bf16[1,768,384]{2,1,0:T(8,128)(2,1)}, u32[]{:S(2)}, u32[]{:S(2)}) collective-permute-start(bf16[1,768,384]{2,1,0:T(8,128)(2,1)S(1)} %get-tuple-element.302), channel_id=1, source_target_pairs={{0,16},{16,0},{1,17},{17,1},{2,18},{18,2},{3,19},{19,3},{4,20},{20... | collective-permute-start | bytes 1769480 | tf_op jit(solution)/shard_map/ppermute | solution.py:877
  45.5 37.8 %collective-permute-start.23 = (bf16[1,768,768]{2,1,0:T(8,128)(2,1)}, bf16[1,768,768]{2,1,0:T(8,128)(2,1)}, u32[]{:S(2)}, u32[]{:S(2)}) collective-permute-start(bf16[1,768,768]{2,1,0:T(8,128)(2,1)} %refs_6_.9), channel_id=1, source_target_pairs={{0,4},{4,0},{8,12},{12,8},{1,5},{5,1},{9,13},{13,9},{2,6},{6,2},{1... | collective-permute-start | bytes 3538952 | tf_op jit(solution)/shard_map/ppermute | solution.py:877
  47.9 17.8 %collective-permute-start.16 = (bf16[1,192,384]{2,1,0:T(8,128)(2,1)}, bf16[1,192,384]{2,1,0:T(8,128)(2,1)S(1)}, u32[]{:S(2)}, u32[]{:S(2)}) collective-permute-start(bf16[1,192,384]{2,1,0:T(8,128)(2,1)} %collective-permute-done.13.refs_2_.refs_8_), channel_id=1, source_target_pairs={{0,4},{4,0},{8,12},{12,8},{1,5},{5,1},{9,13},{13,9},{2,6},{6,2},{1... | collective-permute-start | bytes 442376 | tf_op jit(solution)/shard_map/ppermute | solution.py:877
  48.0 20.2 %collective-permute-start.17 = (bf16[1,768,384]{2,1,0:T(8,128)(2,1)}, bf16[1,768,384]{2,1,0:T(8,128)(2,1)S(1)}, u32[]{:S(2)}, u32[]{:S(2)}) collective-permute-start(bf16[1,768,384]{2,1,0:T(8,128)(2,1)} %collective-permute-done.12.refs_1_), channel_id=1, source_target_pairs={{0,1},{1,0},{2,3},{3,2},{4,5},{5,4},{6,7},{7,6},{8,9},{9,8},{10,11... | collective-permute-start | bytes 1769480 | tf_op jit(solution)/shard_map/ppermute | solution.py:877
  58.9 17.8 %collective-permute-start.22 = (bf16[1,768,384]{2,1,0:T(8,128)(2,1)}, bf16[1,768,384]{2,1,0:T(8,128)(2,1)}, u32[]{:S(2)}, u32[]{:S(2)}) collective-permute-start(bf16[1,768,384]{2,1,0:T(8,128)(2,1)} %collective-permute-done.21.refs_7_), channel_id=1, source_target_pairs={{0,1},{1,0},{2,3},{3,2},{4,5},{5,4},{6,7},{7,6},{8,9},{9,8},{10,11... | collective-permute-start | bytes 1769480 | tf_op jit(solution)/shard_map/ppermute | solution.py:877
  67.5 20.7 %collective-permute-start.19 = (bf16[1,768,384]{2,1,0:T(8,128)(2,1)}, bf16[1,768,384]{2,1,0:T(8,128)(2,1)S(1)}, u32[]{:S(2)}, u32[]{:S(2)}) collective-permute-start(bf16[1,768,384]{2,1,0:T(8,128)(2,1)} %collective-permute-done.12.refs_1_), channel_id=1, source_target_pairs={{0,4},{4,0},{8,12},{12,8},{1,5},{5,1},{9,13},{13,9},{2,6},{6,2},{1... | collective-permute-start | bytes 1769480 | tf_op jit(solution)/shard_map/ppermute | solution.py:877
  68.1 20.1 %collective-permute-start.24 = (bf16[1,768,384]{2,1,0:T(8,128)(2,1)}, bf16[1,768,384]{2,1,0:T(8,128)(2,1)S(1)}, u32[]{:S(2)}, u32[]{:S(2)}) collective-permute-start(bf16[1,768,384]{2,1,0:T(8,128)(2,1)} %collective-permute-done.21.refs_7_), channel_id=1, source_target_pairs={{0,4},{4,0},{8,12},{12,8},{1,5},{5,1},{9,13},{13,9},{2,6},{6,2},{1... | collective-permute-start | bytes 1769480 | tf_op jit(solution)/shard_map/ppermute | solution.py:877
  68.2 20.0 %collective-permute-start.20 = (bf16[1,768,384]{2,1,0:T(8,128)(2,1)S(1)}, bf16[1,768,384]{2,1,0:T(8,128)(2,1)S(1)}, u32[]{:S(2)}, u32[]{:S(2)}) collective-permute-start(bf16[1,768,384]{2,1,0:T(8,128)(2,1)S(1)} %collective-permute-done.17.refs_2_), channel_id=1, source_target_pairs={{0,4},{4,0},{8,12},{12,8},{1,5},{5,1},{9,13},{13,9},{2,6},{6,2},{1... | collective-permute-start | bytes 1769480 | tf_op jit(solution)/shard_map/ppermute | solution.py:877
  164.9 20.7 %collective-permute-start.35 = (bf16[256,768]{1,0:T(8,128)(2,1)S(1)}, bf16[256,768]{1,0:T(8,128)(2,1)S(1)}, u32[]{:S(2)}, u32[]{:S(2)}) collective-permute-start(bf16[256,768]{1,0:T(8,128)(2,1)S(1)} %copy-done.2), channel_id=1, source_target_pairs={{16,0},{17,1},{18,2},{19,3},{20,4},{21,5},{22,6},{23,7},{24,8},{25... | collective-permute-start | bytes 1179656 | tf_op jit(solution)/shard_map/ppermute | solution.py:1138
  200.6 17.3 %collective-permute-start.41 = (bf16[384,768]{1,0:T(8,128)(2,1)S(1)}, bf16[384,768]{1,0:T(8,128)(2,1)S(1)}, u32[]{:S(2)}, u32[]{:S(2)}) collective-permute-start(bf16[384,768]{1,0:T(8,128)(2,1)S(1)} %get-tuple-element.358), channel_id=1, source_target_pairs={{0,16},{16,0},{1,17},{17,1},{2,18},{18,2},{3,19},{19,3},{4,20},{20... | collective-permute-start | bytes 1769480 | tf_op jit(solution)/shard_map/ppermute | solution.py:877
  228.1 15.6 %collective-permute-start.45 = (bf16[384,768]{1,0:T(8,128)(2,1)S(1)}, bf16[384,768]{1,0:T(8,128)(2,1)S(1)}, u32[]{:S(2)}, u32[]{:S(2)}) collective-permute-start(bf16[384,768]{1,0:T(8,128)(2,1)S(1)} %get-tuple-element.401), channel_id=1, source_target_pairs={{0,16},{16,0},{1,17},{17,1},{2,18},{18,2},{3,19},{19,3},{4,20},{20... | collective-permute-start | bytes 1769480 | tf_op jit(solution)/shard_map/ppermute | solution.py:877
  228.3 18.3 %collective-permute-start.46 = (bf16[256,768]{1,0:T(8,128)(2,1)S(1)}, bf16[256,768]{1,0:T(8,128)(2,1)S(1)}, u32[]{:S(2)}, u32[]{:S(2)}) collective-permute-start(bf16[256,768]{1,0:T(8,128)(2,1)S(1)} %get-tuple-element.404), channel_id=1, source_target_pairs={{0,8},{4,12},{8,0},{12,4},{1,9},{5,13},{9,1},{13,5},{2,10},{6,14},... | collective-permute-start | bytes 1179656 | tf_op jit(solution)/shard_map/ppermute | solution.py:877
  244.7 14.9 %collective-permute-start.48 = (bf16[384,768]{1,0:T(8,128)(2,1)S(1)}, bf16[384,768]{1,0:T(8,128)(2,1)S(1)}, u32[]{:S(2)}, u32[]{:S(2)}) collective-permute-start(bf16[384,768]{1,0:T(8,128)(2,1)S(1)} %get-tuple-element.402), channel_id=1, source_target_pairs={{0,1},{1,0},{2,3},{3,2},{4,5},{5,4},{6,7},{7,6},{8,9},{9,8},{10,11... | collective-permute-start | bytes 1769480 | tf_op jit(solution)/shard_map/ppermute | solution.py:877
  246.4 14.5 %collective-permute-start.49 = (bf16[384,768]{1,0:T(8,128)(2,1)S(1)}, bf16[384,768]{1,0:T(8,128)(2,1)S(1)}, u32[]{:S(2)}, u32[]{:S(2)}) collective-permute-start(bf16[384,768]{1,0:T(8,128)(2,1)S(1)} %get-tuple-element.397), channel_id=1, source_target_pairs={{0,16},{16,0},{1,17},{17,1},{2,18},{18,2},{3,19},{19,3},{4,20},{20... | collective-permute-start | bytes 1769480 | tf_op jit(solution)/shard_map/ppermute | solution.py:877
  248.4 13.2 %collective-permute-start.47 = (bf16[256,768]{1,0:T(8,128)(2,1)S(1)}, bf16[256,768]{1,0:T(8,128)(2,1)S(1)}, u32[]{:S(2)}, u32[]{:S(2)}) collective-permute-start(bf16[256,768]{1,0:T(8,128)(2,1)S(1)} %get-tuple-element.407.df_ref.df0), channel_id=1, source_target_pairs={{0,8},{4,12},{8,0},{12,4},{1,9},{5,13},{9,1},{13,5},{2,10},{6,14},... | collective-permute-start | bytes 1179656 | tf_op jit(solution)/shard_map/ppermute | solution.py:877
  267.0 16.8 %collective-permute-start.53 = (bf16[256,768]{1,0:T(8,128)(2,1)S(1)}, bf16[256,768]{1,0:T(8,128)(2,1)S(1)}, u32[]{:S(2)}, u32[]{:S(2)}) collective-permute-start(bf16[256,768]{1,0:T(8,128)(2,1)S(1)} %get-tuple-element.423), channel_id=1, source_target_pairs={{0,8},{4,12},{8,0},{12,4},{1,9},{5,13},{9,1},{13,5},{2,10},{6,14},... | collective-permute-start | bytes 1179656 | tf_op jit(solution)/shard_map/ppermute | solution.py:877
  267.8 15.4 %collective-permute-start.51 = (bf16[192,768]{1,0:T(8,128)(2,1)S(1)}, bf16[192,768]{1,0:T(8,128)(2,1)S(1)}, u32[]{:S(2)}, u32[]{:S(2)}) collective-permute-start(bf16[192,768]{1,0:T(8,128)(2,1)S(1)} %get-tuple-element.420), channel_id=1, source_target_pairs={{0,1},{1,0},{2,3},{3,2},{4,5},{5,4},{6,7},{7,6},{8,9},{9,8},{10,11... | collective-permute-start | bytes 884744 | tf_op jit(solution)/shard_map/ppermute | solution.py:877
  268.8 13.0 %collective-permute-start.50 = (bf16[192,768]{1,0:T(8,128)(2,1)S(1)}, bf16[192,768]{1,0:T(8,128)(2,1)S(1)}, u32[]{:S(2)}, u32[]{:S(2)}) collective-permute-start(bf16[192,768]{1,0:T(8,128)(2,1)S(1)} %get-tuple-element.417), channel_id=1, source_target_pairs={{0,2},{1,3},{2,0},{3,1},{4,6},{5,7},{6,4},{7,5},{8,10},{9,11},{10,... | collective-permute-start | bytes 884744 | tf_op jit(solution)/shard_map/ppermute | solution.py:877
  273.8 37.8 %collective-permute-start.57 = (bf16[384,768]{1,0:T(8,128)(2,1)S(1)}, bf16[384,768]{1,0:T(8,128)(2,1)S(1)}, u32[]{:S(2)}, u32[]{:S(2)}) collective-permute-start(bf16[384,768]{1,0:T(8,128)(2,1)S(1)} %get-tuple-element.441), channel_id=1, source_target_pairs={{0,16},{16,0},{1,17},{17,1},{2,18},{18,2},{3,19},{19,3},{4,20},{20... | collective-permute-start | bytes 1769480 | tf_op jit(solution)/shard_map/ppermute | solution.py:877
  285.6 26.8 %collective-permute-start.54 = (bf16[256,768]{1,0:T(8,128)(2,1)S(1)}, bf16[256,768]{1,0:T(8,128)(2,1)S(1)}, u32[]{:S(2)}, u32[]{:S(2)}) collective-permute-start(bf16[256,768]{1,0:T(8,128)(2,1)S(1)} %get-tuple-element.445.dz_ref.dz0_ref), channel_id=1, source_target_pairs={{0,8},{4,12},{8,0},{12,4},{1,9},{5,13},{9,1},{13,5},{2,10},{6,14},... | collective-permute-start | bytes 1179656 | tf_op jit(solution)/shard_map/ppermute | solution.py:877
  287.0 19.9 %collective-permute-start.55 = (bf16[192,768]{1,0:T(8,128)(2,1)S(1)}, bf16[192,768]{1,0:T(8,128)(2,1)S(1)}, u32[]{:S(2)}, u32[]{:S(2)}) collective-permute-start(bf16[192,768]{1,0:T(8,128)(2,1)S(1)} %shard_map.255.own_ref), channel_id=1, source_target_pairs={{0,2},{1,3},{2,0},{3,1},{4,6},{5,7},{6,4},{7,5},{8,10},{9,11},{10,... | collective-permute-start | bytes 884744 | tf_op jit(solution)/shard_map/ppermute | solution.py:877
  289.5 18.9 %collective-permute-start.56 = (bf16[96,768]{1,0:T(8,128)(2,1)S(1)}, bf16[96,768]{1,0:T(8,128)(2,1)S(1)}, u32[]{:S(2)}, u32[]{:S(2)}) collective-permute-start(bf16[96,768]{1,0:T(8,128)(2,1)S(1)} %get-tuple-element.439), channel_id=1, source_target_pairs={{0,2},{1,3},{2,0},{3,1},{4,6},{5,7},{6,4},{7,5},{8,10},{9,11},{10,... | collective-permute-start | bytes 442376 | tf_op jit(solution)/shard_map/ppermute | solution.py:877
  296.7 20.3 %collective-permute-start.58 = (bf16[256,768]{1,0:T(8,128)(2,1)S(1)}, bf16[256,768]{1,0:T(8,128)(2,1)S(1)}, u32[]{:S(2)}, u32[]{:S(2)}) collective-permute-start(bf16[256,768]{1,0:T(8,128)(2,1)S(1)} %get-tuple-element.457), channel_id=1, source_target_pairs={{0,4},{4,0},{8,12},{12,8},{1,5},{5,1},{9,13},{13,9},{2,6},{6,2},{1... | collective-permute-start | bytes 1179656 | tf_op jit(solution)/shard_map/ppermute | solution.py:877
  322.4 26.4 %collective-permute-start.63 = (bf16[384,768]{1,0:T(8,128)(2,1)S(1)}, bf16[384,768]{1,0:T(8,128)(2,1)S(1)}, u32[]{:S(2)}, u32[]{:S(2)}) collective-permute-start(bf16[384,768]{1,0:T(8,128)(2,1)S(1)} %get-tuple-element.504), channel_id=1, source_target_pairs={{0,16},{16,0},{1,17},{17,1},{2,18},{18,2},{3,19},{19,3},{4,20},{20... | collective-permute-start | bytes 1769480 | tf_op jit(solution)/shard_map/ppermute | solution.py:877
  322.9 31.3 %collective-permute-start.65 = (bf16[384,768]{1,0:T(8,128)(2,1)S(1)}, bf16[384,768]{1,0:T(8,128)(2,1)S(1)}, u32[]{:S(2)}, u32[]{:S(2)}) collective-permute-start(bf16[384,768]{1,0:T(8,128)(2,1)S(1)} %shard_map.262.own_ref), channel_id=1, source_target_pairs={{0,1},{1,0},{2,3},{3,2},{4,5},{5,4},{6,7},{7,6},{8,9},{9,8},{10,11... | collective-permute-start | bytes 1769480 | tf_op jit(solution)/shard_map/ppermute | solution.py:877
  323.5 16.9 %collective-permute-start.62 = (bf16[96,768]{1,0:T(8,128)(2,1)S(1)}, bf16[96,768]{1,0:T(8,128)(2,1)S(1)}, u32[]{:S(2)}, u32[]{:S(2)}) collective-permute-start(bf16[96,768]{1,0:T(8,128)(2,1)S(1)} %shard_map.263.own_ref), channel_id=1, source_target_pairs={{0,2},{1,3},{2,0},{3,1},{4,6},{5,7},{6,4},{7,5},{8,10},{9,11},{10,... | collective-permute-start | bytes 442376 | tf_op jit(solution)/shard_map/ppermute | solution.py:877
  326.9 20.8 %collective-permute-start.61 = (bf16[192,768]{1,0:T(8,128)(2,1)S(1)}, bf16[192,768]{1,0:T(8,128)(2,1)S(1)}, u32[]{:S(2)}, u32[]{:S(2)}) collective-permute-start(bf16[192,768]{1,0:T(8,128)(2,1)S(1)} %get-tuple-element.468), channel_id=1, source_target_pairs={{0,1},{1,0},{2,3},{3,2},{4,5},{5,4},{6,7},{7,6},{8,9},{9,8},{10,11... | collective-permute-start | bytes 884744 | tf_op jit(solution)/shard_map/ppermute | solution.py:877
  327.7 41.9 %collective-permute-start.71 = (bf16[384,768]{1,0:T(8,128)(2,1)S(1)}, bf16[384,768]{1,0:T(8,128)(2,1)S(1)}, u32[]{:S(2)}, u32[]{:S(2)}) collective-permute-start(bf16[384,768]{1,0:T(8,128)(2,1)S(1)} %get-tuple-element.485), channel_id=1, source_target_pairs={{0,16},{16,0},{1,17},{17,1},{2,18},{18,2},{3,19},{19,3},{4,20},{20... | collective-permute-start | bytes 1769480 | tf_op jit(solution)/shard_map/ppermute | solution.py:877
  340.3 15.2 %collective-permute-start.66 = (bf16[256,768]{1,0:T(8,128)(2,1)S(1)}, bf16[256,768]{1,0:T(8,128)(2,1)S(1)}, u32[]{:S(2)}, u32[]{:S(2)}) collective-permute-start(bf16[256,768]{1,0:T(8,128)(2,1)S(1)} %get-tuple-element.512), channel_id=1, source_target_pairs={{0,8},{4,12},{8,0},{12,4},{1,9},{5,13},{9,1},{13,5},{2,10},{6,14},... | collective-permute-start | bytes 1179656 | tf_op jit(solution)/shard_map/ppermute | solution.py:877
  349.6 16.4 %collective-permute-start.69 = (bf16[192,768]{1,0:T(8,128)(2,1)S(1)}, bf16[192,768]{1,0:T(8,128)(2,1)S(1)}, u32[]{:S(2)}, u32[]{:S(2)}) collective-permute-start(bf16[192,768]{1,0:T(8,128)(2,1)S(1)} %get-tuple-element.505), channel_id=1, source_target_pairs={{0,1},{1,0},{2,3},{3,2},{4,5},{5,4},{6,7},{7,6},{8,9},{9,8},{10,11... | collective-permute-start | bytes 884744 | tf_op jit(solution)/shard_map/ppermute | solution.py:877
  370.3 25.5 %collective-permute-start.75 = (bf16[192,768]{1,0:T(8,128)(2,1)S(1)}, bf16[192,768]{1,0:T(8,128)(2,1)S(1)}, u32[]{:S(2)}, u32[]{:S(2)}) collective-permute-start(bf16[192,768]{1,0:T(8,128)(2,1)S(1)} %get-tuple-element.526), channel_id=1, source_target_pairs={{0,1},{1,0},{2,3},{3,2},{4,5},{5,4},{6,7},{7,6},{8,9},{9,8},{10,11... | collective-permute-start | bytes 884744 | tf_op jit(solution)/shard_map/ppermute | solution.py:877
  371.8 24.5 %collective-permute-start.76 = (bf16[192,768]{1,0:T(8,128)(2,1)S(1)}, bf16[192,768]{1,0:T(8,128)(2,1)S(1)}, u32[]{:S(2)}, u32[]{:S(2)}) collective-permute-start(bf16[192,768]{1,0:T(8,128)(2,1)S(1)} %shard_map.281.own_ref), channel_id=1, source_target_pairs={{0,1},{1,0},{2,3},{3,2},{4,5},{5,4},{6,7},{7,6},{8,9},{9,8},{10,11... | collective-permute-start | bytes 884744 | tf_op jit(solution)/shard_map/ppermute | solution.py:877
  373.0 12.6 %collective-permute-start.73 = (bf16[96,768]{1,0:T(8,128)(2,1)S(1)}, bf16[96,768]{1,0:T(8,128)(2,1)S(1)}, u32[]{:S(2)}, u32[]{:S(2)}) collective-permute-start(bf16[96,768]{1,0:T(8,128)(2,1)S(1)} %get-tuple-element.521), channel_id=1, source_target_pairs={{0,2},{1,3},{2,0},{3,1},{4,6},{5,7},{6,4},{7,5},{8,10},{9,11},{10,... | collective-permute-start | bytes 442376 | tf_op jit(solution)/shard_map/ppermute | solution.py:877
  389.7 14.8 %collective-permute-start.78 = (bf16[192,768]{1,0:T(8,128)(2,1)S(1)}, bf16[192,768]{1,0:T(8,128)(2,1)S(1)}, u32[]{:S(2)}, u32[]{:S(2)}) collective-permute-start(bf16[192,768]{1,0:T(8,128)(2,1)S(1)} %shard_map.271.own_ref), channel_id=1, source_target_pairs={{0,1},{1,0},{2,3},{3,2},{4,5},{5,4},{6,7},{7,6},{8,9},{9,8},{10,11... | collective-permute-start | bytes 884744 | tf_op jit(solution)/shard_map/ppermute | solution.py:877
  401.0 43.5 %collective-permute-start.88 = (bf16[768,768]{1,0:T(8,128)(2,1)S(1)}, bf16[768,768]{1,0:T(8,128)(2,1)S(1)}, u32[]{:S(2)}, u32[]{:S(2)}) collective-permute-start(bf16[768,768]{1,0:T(8,128)(2,1)S(1)} %shard_map.274.refs_5_), channel_id=1, source_target_pairs={{0,16},{1,17},{2,18},{3,19},{4,20},{5,21},{6,22},{7,23},{8,24},{9,... | collective-permute-start | bytes 3538952 | tf_op jit(solution)/shard_map/ppermute | solution.py:948
  411.2 21.3 %collective-permute-start.85 = (bf16[256,768]{1,0:T(8,128)(2,1)S(1)}, bf16[256,768]{1,0:T(8,128)(2,1)S(1)}, u32[]{:S(2)}, u32[]{:S(2)}) collective-permute-start(bf16[256,768]{1,0:T(8,128)(2,1)S(1)} %get-tuple-element.546.second_ref), channel_id=1, source_target_pairs={{0,16},{1,17},{2,18},{3,19},{4,20},{5,21},{6,22},{7,23},{8,24},{9,... | collective-permute-start | bytes 1179656 | tf_op jit(solution)/shard_map/ppermute | solution.py:1273
  414.8 21.0 %collective-permute-start.84 = (bf16[256,768]{1,0:T(8,128)(2,1)S(1)}, bf16[256,768]{1,0:T(8,128)(2,1)S(1)}, u32[]{:S(2)}, u32[]{:S(2)}) collective-permute-start(bf16[256,768]{1,0:T(8,128)(2,1)S(1)} %shard_map.275.first_ref), channel_id=1, source_target_pairs={{16,0},{17,1},{18,2},{19,3},{20,4},{21,5},{22,6},{23,7},{24,8},{25... | collective-permute-start | bytes 1179656 | tf_op jit(solution)/shard_map/ppermute | solution.py:1272
  418.0 15.9 %collective-permute-start.82 = (bf16[192,768]{1,0:T(8,128)(2,1)S(1)}, bf16[192,768]{1,0:T(8,128)(2,1)S(1)}, u32[]{:S(2)}, u32[]{:S(2)}) collective-permute-start(bf16[192,768]{1,0:T(8,128)(2,1)S(1)} %shard_map.290.own_ref), channel_id=1, source_target_pairs={{0,1},{1,0},{2,3},{3,2},{4,5},{5,4},{6,7},{7,6},{8,9},{9,8},{10,11... | collective-permute-start | bytes 884744 | tf_op jit(solution)/shard_map/ppermute | solution.py:877
  418.0 22.4 %collective-permute-start.83 = (f32[16,768]{1,0:T(8,128)S(1)}, f32[16,768]{1,0:T(8,128)S(1)}, u32[]{:S(2)}, u32[]{:S(2)}) collective-permute-start(f32[16,768]{1,0:T(8,128)S(1)} %get-tuple-element.531.own_ref), channel_id=1, source_target_pairs={{0,2},{1,3},{2,0},{3,1},{4,6},{5,7},{6,4},{7,5},{8,10},{9,11},{10,... | collective-permute-start | bytes 147464 | tf_op jit(solution)/shard_map/ppermute | solution.py:877
  432.6 18.1 %collective-permute-start.86 = (bf16[384,768]{1,0:T(8,128)(2,1)S(1)}, bf16[384,768]{1,0:T(8,128)(2,1)S(1)}, u32[]{:S(2)}, u32[]{:S(2)}) collective-permute-start(bf16[384,768]{1,0:T(8,128)(2,1)S(1)} %shard_map.285.refs_0_), channel_id=1, source_target_pairs={{16,0},{17,1},{18,2},{19,3},{20,4},{21,5},{22,6},{23,7},{24,8},{25... | collective-permute-start | bytes 1769480 | tf_op jit(solution)/shard_map/ppermute | solution.py:948
  433.8 28.2 %collective-permute-start.87 = (bf16[384,768]{1,0:T(8,128)(2,1)S(1)}, bf16[384,768]{1,0:T(8,128)(2,1)S(1)}, u32[]{:S(2)}, u32[]{:S(2)}) collective-permute-start(bf16[384,768]{1,0:T(8,128)(2,1)S(1)} %shard_map.288.refs_1_), channel_id=1, source_target_pairs={{16,0},{17,1},{18,2},{19,3},{20,4},{21,5},{22,6},{23,7},{24,8},{25... | collective-permute-start | bytes 1769480 | tf_op jit(solution)/shard_map/ppermute | solution.py:948
  435.8 29.2 %collective-permute-start.90 = (bf16[384,768]{1,0:T(8,128)(2,1)S(1)}, bf16[384,768]{1,0:T(8,128)(2,1)S(1)}, u32[]{:S(2)}, u32[]{:S(2)}) collective-permute-start(bf16[384,768]{1,0:T(8,128)(2,1)S(1)} %shard_map.287.refs_3_), channel_id=1, source_target_pairs={{0,16},{1,17},{2,18},{3,19},{4,20},{5,21},{6,22},{7,23},{8,24},{9,... | collective-permute-start | bytes 1769480 | tf_op jit(solution)/shard_map/ppermute | solution.py:948
  440.4 28.0 %collective-permute-start.89 = (bf16[384,768]{1,0:T(8,128)(2,1)S(1)}, bf16[384,768]{1,0:T(8,128)(2,1)S(1)}, u32[]{:S(2)}, u32[]{:S(2)}) collective-permute-start(bf16[384,768]{1,0:T(8,128)(2,1)S(1)} %shard_map.291.refs_0_), channel_id=1, source_target_pairs={{16,0},{17,1},{18,2},{19,3},{20,4},{21,5},{22,6},{23,7},{24,8},{25... | collective-permute-start | bytes 1769480 | tf_op jit(solution)/shard_map/ppermute | solution.py:948
  (68 other events, 562.5 us)
